TPU v7x, 512 devices: a whole 4x8x8 slice. The times are simulated.
512 devices in a mesh: grp: 4 (over y_hi, core), col: 128 (over x, y_lo, z).
Axes of the slice: x: 4, y: 8 (y_hi: 2, y_lo: 4; y = y_hi * 4 + y_lo), z: 8, core: 2. Of those that a mesh axis runs over, the one named last changes fastest.
Arguments:
- spectral: bfloat16 [1280, 128, 1280], P('col', None, 'grp'), may hold values from -0.4375 to 0.4375
- legendre: bfloat16 [1280, 1280, 512], P('col', 'grp'), may hold values from -0.15625 to 0.15625
- wavenumbers: int32 [1280], replicated, may hold values from 0 to 1279, each once
- regime: int32 [512, 88, 1], P(('grp', 'col')), may hold values from 0 to 127; in each aligned block of 88 rows (0 to 87, 88 to 175, ..., all dimensions but the last counted through in order) at most 2 rows name the same one
- daylight: int32 [512, 88], P(('grp', 'col')), may hold values 0 or 1
- gauss_weight: float32 [512], P(('grp', 'col')), may hold values from 106.131996 to 849.05597
- w_in: bfloat16 [128, 64, 512], P('col'), may hold values from -0.75 to 0.75
- b_in: bfloat16 [128, 512], P('col'), may hold values from -3 to 3
- w_out: bfloat16 [128, 16, 512], P('col'), may hold values from -0.25 to 0.25
Outputs:
- heating: bfloat16 [512, 8, 11264], P(('grp', 'col'))
- heating_spectral: bfloat16 [1280, 16, 1280], P('col', None, 'grp')
Inputs may be any that keep to these rules, and one draw needn't show every extreme that they name: `wavenumbers`: each wavenumber from 0 to 1279 is held by exactly one slot. Among the 88 blocks of one latitude no regime is named more than 2 times, and in every draw some latitude names some regime exactly 2 times; every regime is named somewhere.
All inputs are finite; a program needn't handle non-finite values. No bound on the sum of `daylight` on one device may be relied on, other than what follows from the above.
Results may differ from a plain program's by a relative error of at most 0.022.
Values may be sent and summed in bfloat16 or wider, within the bound.
No kernel may reach another device: no remote copies, remote signals or barrier semaphores. Data moves between devices by JAX's collectives and lax.ppermute only.
A program may use at most 64 MiB of HBM per device.

v0:
```python
import math

import jax
import jax.numpy as jnp
from jax import lax
from jax.sharding import PartitionSpec as P

NLON = 11264


PRECISE = lax.Precision.HIGH


def twiddle_tables(quarters, inner, outer, length):
    wave = (
        jnp.arange(quarters, dtype=jnp.int32)[:, None] * inner
        + jnp.arange(inner, dtype=jnp.int32)[None, :]
    )
    phase = wave[:, :, None] * jnp.arange(outer, dtype=jnp.int32)[None, None, :] % length
    angle = phase.astype(jnp.float32) * (2.0 * math.pi / length)
    return (jnp.cos(angle), jnp.sin(angle))


def synthesize(ordered, lon_count):
    rows_pad, width = ordered.shape
    feat = width // 2
    quarters = rows_pad // 128
    outer = lon_count // 128
    cos_one, sin_one = twiddle_tables(quarters, 128, outer, lon_count)
    cos_two, sin_two = twiddle_tables(1, 128, 128, 128)
    cos_two, sin_two = (cos_two[0], sin_two[0])
    real_part = ordered[:, :feat].reshape(quarters, 128, feat)
    imag_part = ordered[:, feat:].reshape(quarters, 128, feat)
    first_re = jnp.einsum("qrf,qrj->rjf", real_part, cos_one, precision=PRECISE) - jnp.einsum(
        "qrf,qrj->rjf", imag_part, sin_one, precision=PRECISE
    )
    first_im = jnp.einsum("qrf,qrj->rjf", real_part, sin_one, precision=PRECISE) + jnp.einsum(
        "qrf,qrj->rjf", imag_part, cos_one, precision=PRECISE
    )
    values = jnp.einsum("rjf,rk->fkj", first_re, cos_two, precision=PRECISE) - jnp.einsum(
        "rjf,rk->fkj", first_im, sin_two, precision=PRECISE
    )
    return values.reshape(feat, lon_count)


def analyze(heat, wave_count):
    levels, lon_count = heat.shape
    outer = lon_count // 128
    quarters = -(-wave_count // 128)
    cos_one, sin_one = twiddle_tables(quarters, 128, outer, lon_count)
    cos_two, sin_two = twiddle_tables(1, 128, 128, 128)
    cos_two, sin_two = (cos_two[0], sin_two[0])
    values = heat.astype(jnp.float32).reshape(levels, 128, outer)
    inner_re = jnp.einsum("lkj,rk->lrj", values, cos_two, precision=PRECISE)
    inner_im = -jnp.einsum("lkj,rk->lrj", values, sin_two, precision=PRECISE)
    outer_re = jnp.einsum("lrj,qrj->qrl", inner_re, cos_one, precision=PRECISE) + jnp.einsum(
        "lrj,qrj->qrl", inner_im, sin_one, precision=PRECISE
    )
    outer_im = jnp.einsum("lrj,qrj->qrl", inner_im, cos_one, precision=PRECISE) - jnp.einsum(
        "lrj,qrj->qrl", inner_re, sin_one, precision=PRECISE
    )
    stacked = jnp.concatenate(
        [outer_re.reshape(quarters * 128, levels), outer_im.reshape(quarters * 128, levels)], axis=1
    )
    return stacked / lon_count


def radiate_each(blocks, sunlit, first, bias, second):
    levels = second.shape[1] // 2
    pre = (
        jnp.einsum("bfh,bfc->bhc", first, blocks, preferred_element_type=jnp.float32)
        + bias.astype(jnp.float32)[:, :, None]
    )
    act = jax.nn.silu(pre).astype(jnp.bfloat16)
    out = jnp.einsum("boh,bhc->boc", second, act, preferred_element_type=jnp.float32)
    return (out[:, :levels] + sunlit.astype(jnp.float32)[:, None, None] * out[:, levels:]).astype(
        jnp.bfloat16
    )


def grouped(work, arrays):
    count = arrays[0].shape[0]
    groups = math.gcd(8, count)
    shaped = tuple((item.reshape((groups, count // groups) + item.shape[1:]) for item in arrays))
    result = lax.map(lambda parts: work(*parts), shaped)
    return result.reshape((count,) + result.shape[2:])


def body(spectral, legendre, wavenumbers, regime, daylight, gauss_weight, w_in, b_in, w_out):
    col_count = lax.axis_size("col")
    slots, width, degrees = spectral.shape
    feat = width // 2
    levels = w_out.shape[1] // 2
    wave_count = slots * col_count
    lat_count = legendre.shape[2]
    mine = lax.dynamic_slice_in_dim(wavenumbers, lax.axis_index("col") * slots, slots)
    degree = lax.axis_index("grp") * degrees + jnp.arange(degrees, dtype=jnp.int32)
    keep = degree[None, :] < (wave_count - mine)[:, None]
    masked = jnp.where(keep[:, None, :], spectral, jnp.zeros_like(spectral))
    band_rows_dev = lat_count // lax.axis_size("grp")
    table = legendre
    term = jnp.einsum("skl,sck->lsc", table, masked, preferred_element_type=jnp.float32)
    band = lax.psum_scatter(
        term.reshape(band_rows_dev * lax.axis_size("grp"), slots * width).astype(jnp.bfloat16),
        "grp",
        scatter_dimension=0,
        tiled=True,
    ).astype(jnp.float32)
    band = band.astype(jnp.bfloat16).reshape(col_count, slots, width)
    coeffs = lax.all_to_all(band, "col", split_axis=0, concat_axis=1, tiled=True)
    rows_pad = -(-wave_count // 128) * 128
    ordered = (
        jnp.zeros((rows_pad, width), jnp.float32).at[wavenumbers].set(coeffs[0].astype(jnp.float32))
    )
    doubling = jnp.where(jnp.arange(rows_pad) == 0, 1.0, 2.0).astype(jnp.float32)
    grid = synthesize(ordered * doubling[:, None], NLON).astype(jnp.bfloat16)
    block_count = NLON // 128
    columns = jnp.transpose(grid.reshape(feat, block_count, 128), (1, 0, 2))
    target = regime[0, :, 0]
    sunlit = daylight[0]
    first_all, bias_all, second_all = (
        lax.all_gather(w_in, "col", axis=0, tiled=True),
        lax.all_gather(b_in, "col", axis=0, tiled=True),
        lax.all_gather(w_out, "col", axis=0, tiled=True),
    )

    def compute(part_blocks, part_lights, picks):
        return radiate_each(
            part_blocks, part_lights, first_all[picks], bias_all[picks], second_all[picks]
        )

    heat_blocks = grouped(compute, (columns, sunlit, target))
    heat = jnp.transpose(heat_blocks, (1, 0, 2)).reshape(levels, NLON)
    spectrum = analyze(heat, wave_count) * gauss_weight[0]
    weighted = spectrum[wavenumbers].astype(jnp.bfloat16).reshape(1, col_count, slots * 2 * levels)
    band_rows = lax.all_to_all(weighted, "col", split_axis=1, concat_axis=0, tiled=True)
    piece = lax.all_gather(band_rows, "grp", axis=0, tiled=True)
    rows = piece.shape[0]
    table = legendre
    summed = jnp.einsum(
        "skl,lsc->sck",
        table,
        piece.reshape(rows, slots, 2 * levels),
        preferred_element_type=jnp.float32,
    )
    heating_spectral = jnp.where(keep[:, None, :], summed, jnp.zeros_like(summed)).astype(
        jnp.bfloat16
    )
    return (heat[None], heating_spectral)


def solution(mesh):
    placed = (
        P("col", None, "grp"),
        P("col", "grp", None),
        P(),
        P(("grp", "col"), None, None),
        P(("grp", "col"), None),
        P(("grp", "col")),
        P("col", None, None),
        P("col", None),
        P("col", None, None),
    )
    return jax.shard_map(
        body,
        mesh=mesh,
        in_specs=placed,
        out_specs=(P(("grp", "col"), None, None), P("col", None, "grp")),
        check_vma=False,
    )
```

profile of v0, /device:TPU:1, one launch (start us, length us, event | category | flops | bytes accessed | tf_op | source)
XLA Modules:
  0.0 1609.8 jit_solution(15591605305744163139)
XLA Ops:
  19.3 320.0 %all-gather.1 = bf16[128,1,512]{2,1,0:T(2,128)(2,1)S(1)} all-gather(bf16[1,1,512]{2,1,0:T(2,128)(2,1)S(1)} %bitcast.113), channel_id=1, replica_groups=mesh['grp'=4,'col'=128] {'col'}, dimensions={0}, use_global_device_ids=true | all-gather | bytes 132096 | tf_op jit(solution)/shard_map/all_gather | solution.py:123
  344.1 7.3 all-to-all-start
  351.4 14.0 all-to-all-done
  367.5 7.6 scatter_custom_fusion
  376.7 9.0 fusion.31
  385.7 9.0 fusion.29
  394.7 9.1 convolution_add_fusion
  403.8 5.2 fusion.16
  409.0 9.3 convolution_subtract_fusion
  418.3 6.3 fusion.22
  428.4 5.7 convert_element_type.132
  436.9 192.0 %all-gather.5.cloned.1.call-done = bf16[128,16,512]{2,1,0:T(8,128)(2,1)} async-done(((bf16[1,16,512]{2,1,0:T(8,128)(2,1)}), bf16[128,16,512]{2,1,0:T(8,128)(2,1)}) %all-gather.5.cloned.1.call-update) | async-done | bytes 2097168 | tf_op jit(solution)/shard_map/all_gather | solution.py:124
  628.9 703.7 %all-gather.7.cloned.1.call-done = bf16[128,64,512]{2,1,0:T(8,128)(2,1)} async-done(((bf16[1,64,512]{2,1,0:T(8,128)(2,1)}), bf16[128,64,512]{2,1,0:T(8,128)(2,1)}) %all-gather.7.cloned.1.call-update) | async-done | bytes 8388624 | tf_op jit(solution)/shard_map/all_gather | solution.py:122
  1332.7 92.6 %while.10 = (s32[]{:T(128)}, bf16[8,11,8,128]{3,2,1,0:T(8,128)(2,1)}, s32[8,11]{1,0:T(8,128)S(1)}, bf16[128,16,512]{2,1,0:T(8,128)(2,1)}, bf16[128,64,512]{2,1,0...) while((s32[]{:T(128)}, ...), condition=%wide.region_3.4_spmd, body=%wide.region_2.3_spmd.sunk | while | flops 119709224 | bytes 3170801 | solution.py:85
  1344.2 4.9 gather_fusion.1
  1367.4 4.9 gather_fusion.1
  1402.1 4.9 gather_fusion.1
  1435.5 6.9 fusion.42
  1445.2 6.8 fusion.40
  1452.0 6.1 fusion.26
  1460.0 7.0 fusion.25
  1477.4 7.2 all-to-all-start.1
  1485.3 10.5 all-to-all-done.1
  1496.8 103.7 %all-gather = bf16[1,512,160]{1,2,0:T(8,128)(2,1)S(1)} all-gather(bf16[1,128,160]{1,2,0:T(8,128)(2,1)S(1)} %copy.186), channel_id=2, replica_groups=mesh['grp'=4,'col'=128] {'grp'}, dimensions={1}, use_global_device_ids=true | all-gather | bytes 204800 | tf_op jit(solution)/shard_map/all_gather | solution.py:137
  (137 shorter events, 132.0 us)
Async XLA Ops:
  8.0 1.9 copy-start
  8.0 332.0 %reduce-scatter.4.cloned.1.call-start = ((), (), s32[]{:S(2)}) async-start(), calls=%async_computation.5 | async-start | bytes 1638400
  13.7 4.2 copy-start.7
  13.7 4.9 copy-start.8
  13.7 5.7 copy-start.6
  16.1 335.3 %copy-start.5 = (s32[1280]{0:T(1024)S(1)}, s32[1280]{0:T(1024)}, u32[]{:S(2)}) copy-start(s32[1280]{0:T(1024)} %param.13) | copy-start | bytes 15364
  16.2 612.8 %all-gather.5.cloned.1.call-start = ((), (), s32[]{:S(2)}) async-start(), calls=%async_computation.3 | async-start | bytes 2113536 | tf_op jit(solution)/shard_map/all_gather | solution.py:124
  16.7 1315.9 %all-gather.7.cloned.1.call-start = ((), (), s32[]{:S(2)}) async-start(), calls=%async_computation.4 | async-start | bytes 8454144 | tf_op jit(solution)/shard_map/all_gather | solution.py:122
  344.1 21.4 %all-to-all-start = ((bf16[128,10,128]{2,1,0:T(8,128)(2,1)}), bf16[128,10,128]{2,1,0:T(8,128)(2,1)}, u32[]{:S(2)}, u32[]{:S(2)}) async-start(bf16[128,10,128]{2,1,0:T(8,128)(2,1)} %copy.164), calls=%async_computation | async-start | bytes 1048576 | tf_op jit(solution)/shard_map/all_to_all | solution.py:110
  351.4 57.6 %copy-start.1 = (s32[10,128]{0,1:T(8,128)}, s32[10,128]{0,1:T(8,128)S(1)}, u32[]{:S(2)}) copy-start(s32[10,128]{0,1:T(8,128)S(1)} %iota_add_fusion) | copy-start | bytes 15364
  1425.3 10.2 copy-start.2
  1435.5 6.9 copy-start.3
  1445.2 6.8 copy-start.4
  1445.2 6.8 copy-start.9
  1477.4 18.4 %all-to-all-start.1 = ((bf16[1,128,160]{2,0,1:T(2,128)(2,1)}), bf16[1,128,160]{2,0,1:T(2,128)(2,1)}, u32[]{:S(2)}, u32[]{:S(2)}) async-start(bf16[1,128,160]{2,0,1:T(2,128)(2,1)} %convert_element_type.138), calls=%async_computation.1 | async-start | bytes 262144 | tf_op jit(solution)/shard_map/all_to_all | solution.py:136
Sparse Core Ops, SparseCore 0:
  16.3 56.1 reduce-scatter.3
Sparse Core Ops, SparseCore 1:
  18.7 610.2 all-gather.4
  630.9 701.7 all-gather.6
where the time goes:
time: 1620 us; the launch traced here: 1610 us
  waiting for transfers between devices  921 us (57%)
  blocking collectives  424 us (26%)
  local copies, waits for them, and re-layouts  117 us (7%)
  matrix products  105 us (6%)
  between operations  16.6 us (1%)
    all_gather x1, waiting for transfers between devices, body(): lax.all_gather(w_in, 'col', axis=0, tiled=True)  704 us
    all_gather x1, blocking collectives, body(): lax.all_gather(b_in, 'col', axis=0, tiled=True)  320 us
    all_gather x1, waiting for transfers between devices, body(): lax.all_gather(w_out, 'col', axis=0, tiled=True)  192 us
    all_gather x1, blocking collectives, body(): piece = lax.all_gather(band_rows, 'grp', axis=0, tiled=True)  104 us
    gather x8, local copies, waits for them, and re-layouts, compute(): first_all[picks]  39 us
  transfers between devices with their start and end apart: 5, of which 4 were waited for; matrix products, arithmetic and copies ran while one was open for 5% of the time, Pallas kernels for 0%

commit v1 on v0

v1 whole, which is shorter than its diff:
```python
import functools
import math

import jax
import jax.numpy as jnp
import numpy as np
from jax import lax
from jax.sharding import Mesh, PartitionSpec as P
from jax.experimental import pallas as pl
from jax.experimental.pallas import tpu as pltpu

NLON = 11264
BLK = 128
NBLK = NLON // BLK
NHI = 15
BROWS = 96
HALF_ROWS = 176
F32 = jnp.float32
BF16 = jnp.bfloat16


def dot(a, b, ca, cb):
    return lax.dot_general(a, b, (((ca,), (cb,)), ((), ())), preferred_element_type=F32)


def trig(phase, length):
    angle = (np.asarray(phase, np.int64) % length) * (2.0 * np.pi / length)
    return np.cos(angle), np.sin(angle)


def tables():
    c = np.arange(BLK)
    p = np.arange(16)
    cos_pc, sin_pc = trig(np.outer(c, p), BLK)
    live = (p < NHI)[None, :]
    cos_pc, sin_pc = cos_pc * live, sin_pc * live
    first = np.zeros((2, BLK, 16, 2))
    first[0, :, :, 0], first[0, :, :, 1] = cos_pc, -sin_pc
    first[1, :, :, 0], first[1, :, :, 1] = sin_pc, cos_pc
    last = np.zeros((16, 2, 2, BLK))
    last[:, 0, 0], last[:, 0, 1] = cos_pc.T, sin_pc.T
    last[:, 1, 0], last[:, 1, 1] = -sin_pc.T, cos_pc.T
    turn_cos, turn_sin = trig(np.outer(c, c), NLON)
    s = np.arange(BLK)
    cos_sb, sin_sb = trig(np.outer(np.arange(NBLK), s), NBLK)
    cos_sb, sin_sb = cos_sb * (s < NBLK), sin_sb * (s < NBLK)
    second = np.concatenate([2.0 * cos_sb, -2.0 * sin_sb], axis=1)
    inner = np.zeros((2 * BLK, BROWS))
    inner[:BLK, :NBLK], inner[BLK:, :NBLK] = cos_sb.T, -sin_sb.T
    cast = lambda x: jnp.asarray(np.asarray(x, np.float32)).astype(BF16)
    return dict(
        first=cast(first.reshape(2 * BLK, 32)),
        second=cast(second),
        inner=cast(inner),
        last=cast(last.reshape(32, 2 * BLK)),
        turn_cos=jnp.asarray(turn_cos, F32),
        turn_sin=jnp.asarray(turn_sin, F32),
    )


def legendre_kernel(limit_ref, core_ref, table_ref, spec_ref, theirs_ref, ours_ref):
    step = pl.program_id(0)
    width, degrees = spec_ref.shape[1:]
    degree = lax.broadcasted_iota(jnp.int32, (width, degrees), 1)
    spec = spec_ref[0]
    masked = jnp.where(degree < limit_ref[step], spec, jnp.zeros_like(spec))
    core = core_ref[0]
    for which, ref in ((1 - core, theirs_ref), (core, ours_ref)):
        for y_hi in range(2):
            start = pl.multiple_of((2 * y_hi + which) * BLK, BLK)
            part = dot(masked, table_ref[0, :, pl.ds(start, BLK)], 1, 0)
            ref[pl.ds(y_hi * BLK, BLK), :] = part.T.astype(ref.dtype)


def inverse_legendre(spectral, legendre, limit, core):
    slots, width, degrees = spectral.shape
    lats = legendre.shape[2]
    sm = pl.BlockSpec(memory_space=pltpu.SMEM)
    out = pl.BlockSpec((lats // 2, width), lambda s: (0, s))
    return pl.pallas_call(
        legendre_kernel,
        grid=(slots,),
        out_shape=(
            jax.ShapeDtypeStruct((lats // 2, slots * width), BF16),
            jax.ShapeDtypeStruct((lats // 2, slots * width), F32),
        ),
        in_specs=[
            sm,
            sm,
            pl.BlockSpec((1, degrees, lats), lambda s: (s, 0, 0)),
            pl.BlockSpec((1, width, degrees), lambda s: (s, 0, 0)),
        ],
        out_specs=(out, out),
        cost_estimate=pl.CostEstimate(
            flops=2 * slots * width * degrees * lats, bytes_accessed=6_000_000, transcendentals=0
        ),
        name="inverse_legendre",
    )(limit, core, legendre, spectral)


def synth_kernel(coef_ref, pos_ref, first_ref, second_ref, tc_ref, ts_ref, cols_ref, grid_ref, out_ref):
    dests = coef_ref.shape[0] // 2
    local = coef_ref.shape[1] // BLK
    slots = dests * local
    cut = lambda half, i: coef_ref[pl.ds(half * dests, dests), pl.ds(i * BLK, BLK)].astype(F32)
    coef = jnp.concatenate(
        [(cut(0, i) + cut(1, i)).astype(BF16) for i in range(local)], axis=0
    )
    pos = pos_ref[...]
    grid_ref[pl.ds(NHI * BLK, BLK), :] = jnp.zeros((BLK, BLK), F32)

    def place(p, carry):
        want = lax.broadcasted_iota(jnp.int32, (BLK, slots), 0) + p * BLK
        value = jnp.where(want == 0, 0.5, 1.0)
        pick = jnp.where(want == pos, value, 0.0).astype(BF16)
        grid_ref[pl.ds(pl.multiple_of(p * BLK, BLK), BLK), :] = dot(pick, coef, 1, 0).T
        return carry

    lax.fori_loop(0, NHI, place, 0, unroll=3)
    first = first_ref[...]
    second = second_ref[...]
    tc = tc_ref[...]
    ts = ts_ref[...]

    def pair(i, carry):
        f = i * 2
        x = jnp.concatenate(
            [grid_ref[pl.ds(f, 32, stride=64), :], grid_ref[pl.ds(f + 1, 32, stride=64), :]], axis=1
        ).astype(BF16)
        z = dot(first, x, 1, 0)
        rows = []
        for k in range(2):
            re, im = z[:BLK, k * BLK : (k + 1) * BLK], z[BLK:, k * BLK : (k + 1) * BLK]
            rows.append(
                jnp.concatenate([re * tc - im * ts, re * ts + im * tc], axis=1).astype(BF16)
            )
        out = dot(second, jnp.concatenate(rows, axis=0), 1, 1)
        out_ref[pl.ds(f, NBLK, stride=64), :] = out[:, :BLK]
        out_ref[pl.ds(f + 1, NBLK, stride=64), :] = out[:, BLK:]
        return carry

    lax.fori_loop(0, 32, pair, 0, unroll=2)
    cols_ref[...] = out_ref[...].astype(BF16)


def synthesize(coef, pos, tab):
    vm = pl.BlockSpec(memory_space=pltpu.VMEM)
    return pl.pallas_call(
        synth_kernel,
        out_shape=jax.ShapeDtypeStruct((NBLK * 64, BLK), BF16),
        in_specs=[vm] * 6,
        out_specs=vm,
        scratch_shapes=[pltpu.VMEM((16 * BLK, BLK), F32), pltpu.VMEM((NBLK * 64, BLK), F32)],
        compiler_params=pltpu.CompilerParams(vmem_limit_bytes=40 * 1024 * 1024),
        cost_estimate=pl.CostEstimate(flops=3_000_000_000, bytes_accessed=2_500_000, transcendentals=0),
        name="synthesize",
    )(coef, pos, tab["first"], tab["second"], tab["turn_cos"], tab["turn_sin"])


def network_kernel(
    n0, n1, sel_ref, sun_ref, gauss_ref, cols_ref, pos_ref, inner_ref, last_ref, tc_ref, ts_ref, *rest
):
    parts = (rest[:n0], rest[n0 : n0 + n1])
    heat_ref, pay_ref, w_ref, hs_ref, r_ref, sems = rest[n0 + n1 :]

    def fetch(b, carry):
        for half in range(2):
            for d, part in enumerate(parts[half]):

                @pl.when(sel_ref[2 * half, b] == d)
                def _(part=part, half=half):
                    pltpu.make_async_copy(
                        part.at[sel_ref[2 * half + 1, b]], w_ref.at[b, half], sems.at[b, half]
                    ).start()

        return carry

    lax.fori_loop(0, NBLK, fetch, 0)
    hs_ref[...] = jnp.zeros(hs_ref.shape, F32)

    def block(b, carry):
        for half in range(2):
            pltpu.make_async_copy(parts[half][0].at[0], w_ref.at[b, half], sems.at[b, half]).wait()
        cols = cols_ref[pl.ds(pl.multiple_of(b * 64, 64), 64), :]
        out = None
        for half in range(2):
            w = lambda lo, n: w_ref[b, half, pl.ds(lo, n), :]
            w_in = jnp.concatenate([w(0, 64), w(64, 64)], axis=1)
            w_out = jnp.concatenate([w(128, 16), w(144, 16)], axis=1)
            bias = w(160, 16)[:2].astype(F32)
            bias = jnp.concatenate([bias[0:1], bias[1:2]], axis=1)
            pre = dot(cols, w_in, 0, 0) + bias
            h = 0.5 * pre
            act = (h * jnp.tanh(h) + h).astype(BF16)
            part = dot(w_out, act, 1, 1)
            out = part if out is None else out + part
        heat = (out[:8] + sun_ref[b].astype(F32) * out[8:]).astype(BF16)
        heat_ref[:, pl.ds(pl.multiple_of(b * BLK, BLK), BLK)] = heat
        hs_ref[pl.ds(b, 8, stride=BROWS), :] = heat.astype(F32)
        return carry

    lax.fori_loop(0, NBLK, block, 0, unroll=4)
    inner = inner_ref[...]
    last = last_ref[...]
    tc = tc_ref[...]
    ts = ts_ref[...]
    scale = gauss_ref[0] * (1.0 / NLON)
    for lev in range(0, 8, 2):
        h = jnp.concatenate([hs_ref[pl.ds((lev + k) * BROWS, BROWS), :] for k in range(2)], axis=1)
        u = dot(inner, h.astype(BF16), 1, 0)
        rows = []
        for k in range(2):
            re, im = u[:BLK, k * BLK : (k + 1) * BLK], u[BLK:, k * BLK : (k + 1) * BLK]
            rows.append(
                jnp.concatenate([re * tc + im * ts, im * tc - re * ts], axis=1).astype(BF16)
            )
        spec = dot(last, jnp.concatenate(rows, axis=0), 1, 1) * scale
        r_ref[pl.ds(lev, 32, stride=8), :] = spec[:, :BLK]
        r_ref[pl.ds(lev + 1, 32, stride=8), :] = spec[:, BLK:]
    spectrum = jnp.concatenate(
        [r_ref[pl.ds(p * 16, 16), :].astype(BF16) for p in range(NHI)], axis=1
    )
    want = lax.broadcasted_iota(jnp.int32, (NHI * BLK, BLK), 0)
    rows = []
    for i in range(pos_ref.shape[0]):
        pick = jnp.where(want == pos_ref[pl.ds(i, 1), :], 1.0, 0.0).astype(BF16)
        rows.append(dot(spectrum, pick, 1, 0))
    rows.append(jnp.zeros((pay_ref.shape[1] - 16 * len(rows), BLK), F32))
    pay_ref[...] = jnp.concatenate(rows, axis=0).T.astype(BF16)


def network(cols, sel, sun, gauss, pos_local, parts, tab):
    vm = pl.BlockSpec(memory_space=pltpu.VMEM)
    sm = pl.BlockSpec(memory_space=pltpu.SMEM)
    hbm = pl.BlockSpec(memory_space=pl.ANY)
    n0, n1 = len(parts[0]), len(parts[1])
    local, dests = pos_local.shape
    return pl.pallas_call(
        functools.partial(network_kernel, n0, n1),
        out_shape=(
            jax.ShapeDtypeStruct((8, NLON), BF16),
            jax.ShapeDtypeStruct((dests, 2 * BLK), BF16),
        ),
        in_specs=[sm] * 3 + [vm] * 6 + [hbm] * (n0 + n1),
        out_specs=(vm, vm),
        scratch_shapes=[
            pltpu.VMEM((NBLK, 2, HALF_ROWS, BLK), BF16),
            pltpu.VMEM((8 * BROWS, BLK), F32),
            pltpu.VMEM((32 * 8, BLK), F32),
            pltpu.SemaphoreType.DMA((NBLK, 2)),
        ],
        compiler_params=pltpu.CompilerParams(vmem_limit_bytes=48 * 1024 * 1024),
        cost_estimate=pl.CostEstimate(
            flops=4_000_000_000, bytes_accessed=11_000_000, transcendentals=5_800_000
        ),
        name="network",
    )(sel, sun, gauss, cols, pos_local, tab["inner"], tab["last"], tab["turn_cos"], tab["turn_sin"], *parts[0], *parts[1])


AXES = ("y_hi", "core", "x", "y_lo", "z")
SIZES = (2, 2, 4, 4, 8)


def shifted(moves):
    ids = np.arange(math.prod(SIZES)).reshape(SIZES)
    pairs = []
    for (y_hi, core, x, y_lo, z), source in np.ndenumerate(ids):
        axis, by = moves[core]
        y = y_hi * SIZES[3] + y_lo
        if axis == "x":
            x = (x + by) % SIZES[2]
        else:
            y = (y + by) % (SIZES[0] * SIZES[3])
        pairs.append((int(source), int(ids[y // SIZES[3], core, x, y % SIZES[3], z])))
    return pairs


def lines(axes):
    ids = np.arange(math.prod(SIZES)).reshape(SIZES)
    groups = []
    for core in range(2):
        along = 1 if axes[core] == "x" else 2
        groups += np.moveaxis(ids[:, core], along, -1).reshape(-1, 4).tolist()
    return groups


def hop(value, *moves):
    return lax.ppermute(value, AXES, shifted(moves))


def swap(value):
    return lax.ppermute(value, "core", [(0, 1), (1, 0)])


def pack_weights(w_in, b_in, w_out, core):
    lo = core * 256
    parts = []
    cut = lambda a, k: lax.dynamic_slice_in_dim(a, lo + k * BLK, BLK, axis=1)
    parts = [cut(w_in, 0), cut(w_in, 1), cut(w_out, 0), cut(w_out, 1), cut(b_in, 0), cut(b_in, 1)]
    parts.append(jnp.zeros((HALF_ROWS - 162, BLK), BF16))
    return jnp.concatenate(parts, axis=0)


def gather_planes(mine):
    line = lax.all_gather(mine[None], AXES, axis_index_groups=lines(("y", "x")), tiled=True)
    return lax.all_gather(line[None], "z", tiled=True).reshape((32,) + mine.shape)


def gather_rest(plane):
    ahead = hop(plane, ("x", 1), ("y", 1))
    behind = hop(plane, ("x", -1), ("y", -1))
    far_a = hop(ahead[:16], ("x", 1), ("y", 1))
    far_b = hop(behind[16:], ("x", -1), ("y", -1))
    own = [plane, ahead, behind, far_a, far_b]
    other = [swap(part) for part in own]
    return own, other


def places(target):
    z = target % 8
    y = target // 8 % 4
    x = target // 32

    def order(minor, major, me):
        index = z * 4 + minor
        away = (major - me) % 4
        part = jnp.where(away == 0, 0, jnp.where(away == 3, 1, jnp.where(away == 1, 2, 3)))
        part = jnp.where((away == 2) & (index >= 16), 4, part)
        return part, jnp.where(part == 4, index - 16, index)

    by_x = order(y, x, lax.axis_index("x"))
    by_y = order(x, y, lax.axis_index("y_lo"))
    return by_x, by_y


def body(spectral, legendre, wavenumbers, regime, daylight, gauss_weight, w_in, b_in, w_out):
    slots, width, degrees = spectral.shape
    tab = tables()
    core = lax.axis_index("core")
    band = lax.axis_index("y_hi") * 2 + core
    column = (lax.axis_index("x") * 4 + lax.axis_index("y_lo")) * 8 + lax.axis_index("z")
    wave_count = wavenumbers.shape[0]
    dests = wave_count // slots

    mine = lax.dynamic_slice_in_dim(wavenumbers, column * slots, slots)
    degree = band * degrees + jnp.arange(degrees, dtype=jnp.int32)
    keep = degree[None, :] < (wave_count - mine)[:, None]
    place = wavenumbers // NBLK * BLK + wavenumbers % NBLK

    plane = gather_planes(pack_weights(w_in[0], b_in, w_out[0], core))

    limit = wave_count - mine - band * degrees
    theirs, ours = inverse_legendre(spectral, legendre, limit, core[None].astype(jnp.int32))
    pair = (ours + swap(theirs).astype(F32)).astype(BF16)
    got = lax.all_to_all(
        pair.reshape(2 * dests, 2, slots * width // 2),
        ("y_hi", "x", "y_lo", "z"),
        0,
        0,
        tiled=True,
    ).reshape(2 * dests, slots * width)
    local_place = place.reshape(dests, slots).T
    cols = synthesize(got, local_place.reshape(1, wave_count), tab)

    plane, _ = lax.optimization_barrier((plane, got))
    own, other = gather_rest(plane)
    by_x, by_y = places(regime[0, :, 0])
    first = [jnp.where(core == 0, a, b) for a, b in zip(by_x, by_y)]
    second = [jnp.where(core == 0, b, a) for a, b in zip(by_x, by_y)]
    sel = jnp.stack(first + second).astype(jnp.int32)
    heat, pay = network(
        cols, sel, daylight[0], gauss_weight, local_place, (own, other), tab
    )

    pay = jnp.broadcast_to(pay[None], (4,) + pay.shape).reshape(4 * dests, 2, BLK)
    piece = lax.all_to_all(pay, AXES, 0, 0, tiled=True).reshape(4 * dests, 2 * BLK)
    summed = jnp.einsum(
        "skl,lsc->sck",
        legendre,
        piece[:, : slots * 16].reshape(piece.shape[0], slots, 16),
        preferred_element_type=F32,
    )
    heating_spectral = jnp.where(keep[:, None, :], summed, jnp.zeros_like(summed)).astype(BF16)
    return (heat[None], heating_spectral)


def solution(mesh):
    fine = Mesh(mesh.devices.reshape(SIZES), AXES)
    grp, col = ("y_hi", "core"), ("x", "y_lo", "z")
    both = grp + col
    placed = (
        P(col, None, grp),
        P(col, grp, None),
        P(),
        P(both, None, None),
        P(both, None),
        P(both),
        P(col, None, None),
        P(col, None),
        P(col, None, None),
    )
    return jax.shard_map(
        body,
        mesh=fine,
        in_specs=placed,
        out_specs=(P(both, None, None), P(col, None, grp)),
        check_vma=False,
    )
```

time: 1620 us -> 239 us (0.15)
  waiting for transfers between devices: 921 us -> 34.1 us
  blocking collectives: 424 us -> 49.5 us
  local copies, waits for them, and re-layouts: 117 us -> 14.8 us
  matrix products: 105 us -> 3.54 us
  Pallas kernels: 0 us -> 62.7 us
  starting transfers between devices: 14.6 us -> 53.2 us
    all_gather x2 -> x1, waiting for transfers between devices: 896 us -> 0.02 us  [gather_planes(): lax.all_gather(line[None], 'z', tiled=True).reshape((32,) + mine.shape)]
    all_gather x2 -> x1, blocking collectives: 424 us -> 11.4 us  [gather_planes(): lax.all_gather(mine[None], AXES, axis_index_groups=lines(('y', 'x')), til...]
    dot_general x20 -> x1, matrix products: 101 us -> 3.54 us  [body(): jnp.einsum('skl,lsc->sck', legendre, piece[:, :slots * 16].reshape(piece....]
    gather x25 -> x0, local copies, waits for them, and re-layouts: 70.3 us -> none  [the longest x8 39 us: compute(): first_all[picks]]
    pallas_call x0 -> x3, Pallas kernels: none -> 62.7 us  [the longest x1 43.5 us: network(): pl.pallas_call(functools.partial(network_kernel, n0, n1), out_shape=(jax....]
    ppermute x0 -> x10, starting transfers between devices: none -> 39.5 us  [the longest x6 26.4 us: swap(): return lax.ppermute(value, 'core', [(0, 1), (1, 0)])]
    all_to_all x0 -> x1, blocking collectives: none -> 38.1 us  [body(): lax.all_to_all(pair.reshape(2 * dests, 2, slots * width // 2), ('y_hi', '...]
    ppermute x0 -> x10, waiting for transfers between devices: none -> 17 us  [the longest x4 15.1 us: hop(): return lax.ppermute(value, AXES, shifted(moves))]
  transfers between devices with their start and end apart: 5 -> 12, of which waited for: 4 -> 3; matrix products, arithmetic and copies ran while one was open for 5% -> 5% of each run, Pallas kernels for 0% -> 8%
where the time goes in v1:
time: 239 us; the launch traced here: 238 us
  Pallas kernels  62.7 us (26%)
  starting transfers between devices  53.2 us (22%)
  blocking collectives  49.5 us (21%)
  waiting for transfers between devices  34.1 us (14%)
  between operations  15.1 us (6%)
  local copies, waits for them, and re-layouts  14.8 us (6%)
  other arithmetic  4.77 us (2%)
  matrix products  3.54 us (1%)
    pallas_call x1, Pallas kernels, network(): pl.pallas_call(functools.partial(network_kernel, n0, n1), out_shape=(jax....  43.5 us
    all_to_all x1, blocking collectives, body(): lax.all_to_all(pair.reshape(2 * dests, 2, slots * width // 2), ('y_hi', '...  38.1 us
    ppermute x6, starting transfers between devices, swap(): return lax.ppermute(value, 'core', [(0, 1), (1, 0)])  26.4 us
    all_to_all x1, waiting for transfers between devices, body(): lax.all_to_all(pay, AXES, 0, 0, tiled=True).reshape(4 * dests, 2 * BLK)  17 us
    ppermute x4, waiting for transfers between devices, hop(): return lax.ppermute(value, AXES, shifted(moves))  15.1 us
    all_to_all x1, starting transfers between devices, body(): lax.all_to_all(pay, AXES, 0, 0, tiled=True).reshape(4 * dests, 2 * BLK)  13.7 us
    ppermute x4, starting transfers between devices, hop(): return lax.ppermute(value, AXES, shifted(moves))  13.1 us
    all_gather x1, blocking collectives, gather_planes(): lax.all_gather(mine[None], AXES, axis_index_groups=lines(('y', 'x')), til...  11.4 us
  transfers between devices with their start and end apart: 12, of which 3 were waited for; matrix products, arithmetic and copies ran while one was open for 5% of the time, Pallas kernels for 8%

profile of v1, /device:TPU:1, one launch (start us, length us, event | category | flops | bytes accessed | tf_op | source)
XLA Modules:
  0.0 237.6 jit_solution(9438483530896035500)
XLA Ops:
  9.5 11.4 %all-gather = bf16[704,128]{1,0:T(8,128)(2,1)} all-gather(bf16[176,128]{1,0:T(8,128)(2,1)S(1)} %concatenate.3), channel_id=2, replica_groups={{0,8,16,24},{1,9,17,25},{2,10,18,26},{3,11,19,27},{4,12,20,28},{5,13,21..., dimensions={0}, use_global_device_ids=true | all-gather | bytes 225280 | tf_op jit(solution)/shard_map/all_gather | solution.py:305
  21.0 2.2 copy.22.spec_ref
  23.8 8.4 %inverse_legendre.1 = (bf16[256,1280]{1,0:T(8,128)(2,1)}, f32[256,1280]{1,0:T(8,128)}) custom-call(s32[10]{0:T(128)} %get-tuple-element.12.limit_ref, s32[1]{0:T(128)} %bitcast.2.core_ref, bf16[10,320,512]{2,1,0:T(8,128)(2,1)} %table_ref.1, bf16[10,128,320]{2,1,0:T(8,128)(2,1)} %copy.22.spec_ref), custom_call_target="tpu_custom_call" | custom-call | flops 419430400 | bytes 6000000 | tf_op jit(solution)/shard_map/inverse_legendre/pallas_call | solution.py:80
  32.2 11.6 %collective-permute-start = (bf16[256,1280]{1,0:T(8,128)(2,1)}, bf16[256,1280]{1,0:T(8,128)(2,1)S(1)}, u32[]{:S(2)}, u32[]{:S(2)}) collective-permute-start(bf16[256,1280]{1,0:T(8,128)(2,1)} %get-tuple-element.8), channel_id=1, source_target_pairs={{0,128},{128,0},{1,129},{129,1},{2,130},{130,2},{3,131},{131,3},{4... | collective-permute-start | bytes 1966088 | tf_op jit(solution)/shard_map/ppermute | solution.py:292
  43.8 1.9 collective-permute-done
  45.7 1.5 add_convert_fusion
  47.3 38.1 %all_to_all.10 = bf16[256,2,640]{2,1,0:T(2,128)(2,1)S(1)} all-to-all(bf16[256,2,640]{2,1,0:T(2,128)(2,1)S(1)} %reshape.437), channel_id=1, replica_groups=mesh['y_hi'=2,'core'=2,'x'=4,'y_lo'=4,'z'=8] {'y_hi','x','y_lo','z'}, dimensions={0} | all-to-all | bytes 1310720 | tf_op jit(solution)/shard_map/all_to_all | solution.py:355
  85.5 4.7 %collective-permute-start.1 = (bf16[32,176,128]{2,1,0:T(8,128)(2,1)}, bf16[32,176,128]{2,1,0:T(8,128)(2,1)}, u32[]{:S(2)}, u32[]{:S(2)}) collective-permute-start(bf16[32,176,128]{2,1,0:T(8,128)(2,1)} %all-gather.4.cloned.1.call-done.rest_0_), channel_id=1, source_target_pairs={{0,32},{1,33},{2,34},{3,35},{4,36},{5,37},{6,38},{7,39},{8,40},{9,... | collective-permute-start | bytes 4325384 | tf_op jit(solution)/shard_map/ppermute | solution.py:288
  90.2 1.9 collective-permute-start.2
  92.2 15.1 %collective-permute-done.1.rest_1_ = bf16[32,176,128]{2,1,0:T(8,128)(2,1)} collective-permute-done((bf16[32,176,128]{2,1,0:T(8,128)(2,1)}, bf16[32,176,128]{2,1,0:T(8,128)(2,1)}, u32[]{:S(2)}, u32[]{:S(2)}) %collective-permute-start.1) | collective-permute-done | bytes 1441824 | tf_op jit(solution)/shard_map/ppermute | solution.py:288
  107.2 2.1 slice.12
  109.3 3.4 %collective-permute-start.3 = (bf16[16,176,128]{2,1,0:T(8,128)(2,1)}, bf16[16,176,128]{2,1,0:T(8,128)(2,1)S(1)}, u32[]{:S(2)}, u32[]{:S(2)}) collective-permute-start(bf16[16,176,128]{2,1,0:T(8,128)(2,1)} %slice.12), channel_id=1, source_target_pairs={{0,32},{1,33},{2,34},{3,35},{4,36},{5,37},{6,38},{7,39},{8,40},{9,... | collective-permute-start | bytes 2162696 | tf_op jit(solution)/shard_map/ppermute | solution.py:288
  112.7 2.1 slice.13
  114.7 3.1 %collective-permute-start.4 = (bf16[16,176,128]{2,1,0:T(8,128)(2,1)}, bf16[16,176,128]{2,1,0:T(8,128)(2,1)S(1)}, u32[]{:S(2)}, u32[]{:S(2)}) collective-permute-start(bf16[16,176,128]{2,1,0:T(8,128)(2,1)} %slice.13), channel_id=1, source_target_pairs={{0,96},{1,97},{2,98},{3,99},{4,100},{5,101},{6,102},{7,103},{8,104... | collective-permute-start | bytes 2162696 | tf_op jit(solution)/shard_map/ppermute | solution.py:288
  117.9 5.8 %collective-permute-start.5 = (bf16[32,176,128]{2,1,0:T(8,128)(2,1)S(1)}, bf16[32,176,128]{2,1,0:T(8,128)(2,1)}, u32[]{:S(2)}, u32[]{:S(2)}) collective-permute-start(bf16[32,176,128]{2,1,0:T(8,128)(2,1)S(1)} %copy-done), channel_id=1, source_target_pairs={{0,128},{128,0},{1,129},{129,1},{2,130},{130,2},{3,131},{131,3},{4... | collective-permute-start | bytes 4325384 | tf_op jit(solution)/shard_map/ppermute | solution.py:292
  123.6 1.9 collective-permute-start.6
  125.6 2.4 %collective-permute-start.7 = (bf16[32,176,128]{2,1,0:T(8,128)(2,1)}, bf16[32,176,128]{2,1,0:T(8,128)(2,1)}, u32[]{:S(2)}, u32[]{:S(2)}) collective-permute-start(bf16[32,176,128]{2,1,0:T(8,128)(2,1)} %collective-permute-done.2.rest_2_), channel_id=1, source_target_pairs={{0,128},{128,0},{1,129},{129,1},{2,130},{130,2},{3,131},{131,3},{4... | collective-permute-start | bytes 4325384 | tf_op jit(solution)/shard_map/ppermute | solution.py:292
  128.0 1.9 collective-permute-start.8
  130.0 2.7 %collective-permute-start.9 = (bf16[16,176,128]{2,1,0:T(8,128)(2,1)S(1)}, bf16[16,176,128]{2,1,0:T(8,128)(2,1)}, u32[]{:S(2)}, u32[]{:S(2)}) collective-permute-start(bf16[16,176,128]{2,1,0:T(8,128)(2,1)S(1)} %collective-permute-done.4.rest_4_), channel_id=1, source_target_pairs={{0,128},{128,0},{1,129},{129,1},{2,130},{130,2},{3,131},{131,3},{4... | collective-permute-start | bytes 2162696 | tf_op jit(solution)/shard_map/ppermute | solution.py:292
  141.0 10.8 %synthesize.1.cols_ref = bf16[5632,128]{1,0:T(8,128)(2,1)S(1)} custom-call(bf16[256,1280]{1,0:T(8,128)(2,1)S(1)} %bitcast.53, s32[1,1280]{1,0:T(1,128)S(1)} %bitcast.56, bf16[256,32]{1,0:T(8,128)(2,1)S(1)} %copy-done.7, bf16[88,256]{1,0:T(8,128)(2,1)S(1)} %copy-done.8, f32[128,128]{1,0:T(8,128)S(1)} %copy-done.2, f32[128,128]{1,0:T(8,128)S(1)} %copy-done.4), custom_call_target="tpu_custom_call" | custom-call | flops 3000000000 | bytes 2500000 | tf_op jit(solution)/shard_map/synthesize/pallas_call | solution.py:148
  151.9 43.5 %network.1 = (bf16[8,11264]{1,0:T(8,128)(2,1)}, bf16[128,256]{1,0:T(8,128)(2,1)S(1)}) custom-call(s32[4,88]{1,0:T(4,128)S(1)} %pad_add_fusion.sel_ref, s32[88]{0:T(128)S(1)} %bitcast.57, f32[1]{0:T(128)S(6)} %copy.30.gauss_ref, bf16[5632,128]{1,0:T(8,128)(2,1)S(1)} %synthesize.1.cols_ref, s32[10,128]{1,0:T(8,128)S(1)} %bitcast.55, ...), custom_call_target="tpu_custom_call" | custom-call | flops 4000000000 | bytes 11000000 | tf_op jit(solution)/shard_map/network/pallas_call | solution.py:238
  196.2 13.7 %all-to-all-start.1 = ((bf16[512,2,128]{2,1,0:T(2,128)(2,1)}), bf16[512,2,128]{2,1,0:T(2,128)(2,1)S(1)}, u32[]{:S(2)}, u32[]{:S(2)}) async-start(bf16[512,2,128]{2,1,0:T(2,128)(2,1)} %reshape.442), calls=%async_computation.1 | async-start | bytes 524288 | tf_op jit(solution)/shard_map/all_to_all | solution.py:376
  210.0 17.0 %all-to-all-done.1 = bf16[512,2,128]{2,1,0:T(2,128)(2,1)S(1)} async-done(((bf16[512,2,128]{2,1,0:T(2,128)(2,1)}), bf16[512,2,128]{2,1,0:T(2,128)(2,1)S(1)}, u32[]{:S(2)}, u32[]{:S(2)}) %all-to-all-start.1) | async-done | bytes 262176 | tf_op jit(solution)/shard_map/all_to_all | solution.py:376
  227.2 3.5 %fusion = bf16[10,16,320]{2,1,0:T(8,128)(2,1)} fusion(bf16[512,10,16]{0,2,1:T(8,128)(2,1)S(1)} %bitcast.61, bf16[10,320,512]{2,1,0:T(8,128)(2,1)} %table_ref.1, pred[10,320]{1,0:T(8,128)(4,1)S(1)} %broadcast_compare_fusion), kind=kOutput, calls=%fused_computation.2 | convolution fusion | flops 52531200 | bytes 3546240 | tf_op jit(solution)/shard_map/skl,lsc->sck/dot_general | solution.py:377
  (56 shorter events, 11.9 us)
Async XLA Ops:
  7.2 16.1 %copy-start.10 = (s32[1280]{0:T(1024)S(1)}, s32[1280]{0:T(1024)}, u32[]{:S(2)}) copy-start(s32[1280]{0:T(1024)} %param.17) | copy-start | bytes 15364
  7.2 78.3 %all-gather.4.cloned.1.call-start = ((), (), s32[]{:S(2)}) async-start(), calls=%async_computation.2 | async-start | bytes 1622016 | tf_op jit(solution)/shard_map/all_gather | solution.py:306
  32.2 13.5 %collective-permute-start = (bf16[256,1280]{1,0:T(8,128)(2,1)}, bf16[256,1280]{1,0:T(8,128)(2,1)S(1)}, u32[]{:S(2)}, u32[]{:S(2)}) collective-permute-start(bf16[256,1280]{1,0:T(8,128)(2,1)} %get-tuple-element.8), channel_id=1, source_target_pairs={{0,128},{128,0},{1,129},{129,1},{2,130},{130,2},{3,131},{131,3},{4... | collective-permute-start | bytes 1966088 | tf_op jit(solution)/shard_map/ppermute | solution.py:292
  85.5 32.3 %copy-start = (bf16[32,176,128]{2,1,0:T(8,128)(2,1)S(1)}, bf16[32,176,128]{2,1,0:T(8,128)(2,1)}, u32[]{:S(2)}) copy-start(bf16[32,176,128]{2,1,0:T(8,128)(2,1)} %all-gather.4.cloned.1.call-done.rest_0_) | copy-start | bytes 4325380
  85.5 21.7 %collective-permute-start.1 = (bf16[32,176,128]{2,1,0:T(8,128)(2,1)}, bf16[32,176,128]{2,1,0:T(8,128)(2,1)}, u32[]{:S(2)}, u32[]{:S(2)}) collective-permute-start(bf16[32,176,128]{2,1,0:T(8,128)(2,1)} %all-gather.4.cloned.1.call-done.rest_0_), channel_id=1, source_target_pairs={{0,32},{1,33},{2,34},{3,35},{4,36},{5,37},{6,38},{7,39},{8,40},{9,... | collective-permute-start | bytes 4325384 | tf_op jit(solution)/shard_map/ppermute | solution.py:288
  90.2 22.4 %collective-permute-start.2 = (bf16[32,176,128]{2,1,0:T(8,128)(2,1)}, bf16[32,176,128]{2,1,0:T(8,128)(2,1)}, u32[]{:S(2)}, u32[]{:S(2)}) collective-permute-start(bf16[32,176,128]{2,1,0:T(8,128)(2,1)} %all-gather.4.cloned.1.call-done.rest_0_), channel_id=1, source_target_pairs={{0,96},{1,97},{2,98},{3,99},{4,100},{5,101},{6,102},{7,103},{8,104... | collective-permute-start | bytes 4325384 | tf_op jit(solution)/shard_map/ppermute | solution.py:288
  109.3 18.7 %collective-permute-start.3 = (bf16[16,176,128]{2,1,0:T(8,128)(2,1)}, bf16[16,176,128]{2,1,0:T(8,128)(2,1)S(1)}, u32[]{:S(2)}, u32[]{:S(2)}) collective-permute-start(bf16[16,176,128]{2,1,0:T(8,128)(2,1)} %slice.12), channel_id=1, source_target_pairs={{0,32},{1,33},{2,34},{3,35},{4,36},{5,37},{6,38},{7,39},{8,40},{9,... | collective-permute-start | bytes 2162696 | tf_op jit(solution)/shard_map/ppermute | solution.py:288
  114.7 15.2 %collective-permute-start.4 = (bf16[16,176,128]{2,1,0:T(8,128)(2,1)}, bf16[16,176,128]{2,1,0:T(8,128)(2,1)S(1)}, u32[]{:S(2)}, u32[]{:S(2)}) collective-permute-start(bf16[16,176,128]{2,1,0:T(8,128)(2,1)} %slice.13), channel_id=1, source_target_pairs={{0,96},{1,97},{2,98},{3,99},{4,100},{5,101},{6,102},{7,103},{8,104... | collective-permute-start | bytes 2162696 | tf_op jit(solution)/shard_map/ppermute | solution.py:288
  117.9 33.9 %collective-permute-start.5 = (bf16[32,176,128]{2,1,0:T(8,128)(2,1)S(1)}, bf16[32,176,128]{2,1,0:T(8,128)(2,1)}, u32[]{:S(2)}, u32[]{:S(2)}) collective-permute-start(bf16[32,176,128]{2,1,0:T(8,128)(2,1)S(1)} %copy-done), channel_id=1, source_target_pairs={{0,128},{128,0},{1,129},{129,1},{2,130},{130,2},{3,131},{131,3},{4... | collective-permute-start | bytes 4325384 | tf_op jit(solution)/shard_map/ppermute | solution.py:292
  123.6 28.2 %collective-permute-start.6 = (bf16[32,176,128]{2,1,0:T(8,128)(2,1)}, bf16[32,176,128]{2,1,0:T(8,128)(2,1)}, u32[]{:S(2)}, u32[]{:S(2)}) collective-permute-start(bf16[32,176,128]{2,1,0:T(8,128)(2,1)} %collective-permute-done.1.rest_1_), channel_id=1, source_target_pairs={{0,128},{128,0},{1,129},{129,1},{2,130},{130,2},{3,131},{131,3},{4... | collective-permute-start | bytes 4325384 | tf_op jit(solution)/shard_map/ppermute | solution.py:292
  125.6 26.3 %collective-permute-start.7 = (bf16[32,176,128]{2,1,0:T(8,128)(2,1)}, bf16[32,176,128]{2,1,0:T(8,128)(2,1)}, u32[]{:S(2)}, u32[]{:S(2)}) collective-permute-start(bf16[32,176,128]{2,1,0:T(8,128)(2,1)} %collective-permute-done.2.rest_2_), channel_id=1, source_target_pairs={{0,128},{128,0},{1,129},{129,1},{2,130},{130,2},{3,131},{131,3},{4... | collective-permute-start | bytes 4325384 | tf_op jit(solution)/shard_map/ppermute | solution.py:292
  128.0 23.8 %collective-permute-start.8 = (bf16[16,176,128]{2,1,0:T(8,128)(2,1)S(1)}, bf16[16,176,128]{2,1,0:T(8,128)(2,1)}, u32[]{:S(2)}, u32[]{:S(2)}) collective-permute-start(bf16[16,176,128]{2,1,0:T(8,128)(2,1)S(1)} %collective-permute-done.3.rest_3_), channel_id=1, source_target_pairs={{0,128},{128,0},{1,129},{129,1},{2,130},{130,2},{3,131},{131,3},{4... | collective-permute-start | bytes 2162696 | tf_op jit(solution)/shard_map/ppermute | solution.py:292
  130.0 21.9 %collective-permute-start.9 = (bf16[16,176,128]{2,1,0:T(8,128)(2,1)S(1)}, bf16[16,176,128]{2,1,0:T(8,128)(2,1)}, u32[]{:S(2)}, u32[]{:S(2)}) collective-permute-start(bf16[16,176,128]{2,1,0:T(8,128)(2,1)S(1)} %collective-permute-done.4.rest_4_), channel_id=1, source_target_pairs={{0,128},{128,0},{1,129},{129,1},{2,130},{130,2},{3,131},{131,3},{4... | collective-permute-start | bytes 2162696 | tf_op jit(solution)/shard_map/ppermute | solution.py:292
  137.7 0.8 copy-start.2
  138.5 0.8 copy-start.4
  139.4 0.8 copy-start.7
  140.2 0.8 copy-start.8
  141.0 10.9 %copy-start.1 = (s32[1,88]{1,0:T(1,128)S(1)}, s32[1,88]{1,0:T(1,128)}, u32[]{:S(2)}) copy-start(s32[1,88]{1,0:T(1,128)} %param.19) | copy-start | bytes 1060
  141.0 10.9 %copy-start.3 = (f32[128,128]{1,0:T(8,128)S(1)}, f32[128,128]{1,0:T(8,128)}, u32[]{:S(2)}) copy-start(f32[128,128]{1,0:T(8,128)} %constant.152.clone.tc_ref) | copy-start | bytes 196612
  141.0 10.9 %copy-start.5 = (f32[128,128]{1,0:T(8,128)S(1)}, f32[128,128]{1,0:T(8,128)}, u32[]{:S(2)}) copy-start(f32[128,128]{1,0:T(8,128)} %constant.153.clone.ts_ref) | copy-start | bytes 196612
  141.0 10.9 %copy-start.6 = (bf16[256,96]{1,0:T(8,128)(2,1)S(1)}, bf16[256,96]{1,0:T(8,128)(2,1)}, u32[]{:S(2)}) copy-start(bf16[256,96]{1,0:T(8,128)(2,1)} %constant.164.inner_ref) | copy-start | bytes 147460
  141.0 10.9 %copy-start.9 = (bf16[32,256]{1,0:T(8,128)(2,1)S(1)}, bf16[32,256]{1,0:T(8,128)(2,1)}, u32[]{:S(2)}) copy-start(bf16[32,256]{1,0:T(8,128)(2,1)} %constant.165.last_ref) | copy-start | bytes 49156
  151.9 58.0 %copy-start.11 = (s32[10]{0:T(128)S(1)}, s32[10]{0:T(128)}, u32[]{:S(2)}) copy-start(s32[10]{0:T(128)} %get-tuple-element.13) | copy-start | bytes 124
  196.2 30.8 %all-to-all-start.1 = ((bf16[512,2,128]{2,1,0:T(2,128)(2,1)}), bf16[512,2,128]{2,1,0:T(2,128)(2,1)S(1)}, u32[]{:S(2)}, u32[]{:S(2)}) async-start(bf16[512,2,128]{2,1,0:T(2,128)(2,1)} %reshape.442), calls=%async_computation.1 | async-start | bytes 524288 | tf_op jit(solution)/shard_map/all_to_all | solution.py:376
Sparse Core Ops, SparseCore 0:
  21.1 58.3 all-gather.3

commit v2 on v1

v2 whole, which is shorter than its diff:
```python
import functools
import math

import jax
import jax.numpy as jnp
import numpy as np
from jax import lax
from jax.sharding import Mesh, PartitionSpec as P
from jax.experimental import pallas as pl
from jax.experimental.pallas import tpu as pltpu

NLON = 11264
BLK = 128
NBLK = NLON // BLK
NHI = 15
BROWS = 96
HALF_ROWS = 176
F32 = jnp.float32
BF16 = jnp.bfloat16


def dot(a, b, ca, cb):
    return lax.dot_general(a, b, (((ca,), (cb,)), ((), ())), preferred_element_type=F32)


def trig(phase, length):
    angle = (np.asarray(phase, np.int64) % length) * (2.0 * np.pi / length)
    return np.cos(angle), np.sin(angle)


TURN, INNER, LAST, FIRST, SECOND, ROWS = 0, 256, 512, 576, 832, 1008


def tables():
    c = np.arange(BLK)
    p = np.arange(16)
    cos_pc, sin_pc = trig(np.outer(c, p), BLK)
    live = (p < NHI)[None, :]
    cos_pc, sin_pc = cos_pc * live, sin_pc * live
    first = np.zeros((2, BLK, 16, 2))
    first[0, :, :, 0], first[0, :, :, 1] = cos_pc, -sin_pc
    first[1, :, :, 0], first[1, :, :, 1] = sin_pc, cos_pc
    last = np.zeros((16, 2, 2, BLK))
    last[:, 0, 0], last[:, 0, 1] = cos_pc.T, sin_pc.T
    last[:, 1, 0], last[:, 1, 1] = -sin_pc.T, cos_pc.T
    turn_cos, turn_sin = trig(np.outer(c, c), NLON)
    cos_sb, sin_sb = trig(np.outer(np.arange(NBLK), c), NBLK)
    cos_sb, sin_sb = cos_sb * (c < NBLK), sin_sb * (c < NBLK)
    out = np.zeros((ROWS, BLK), np.float32)
    out[TURN : TURN + BLK], out[TURN + BLK : INNER] = turn_cos, turn_sin
    out[INNER : INNER + BLK, :NBLK], out[INNER + BLK : LAST, :NBLK] = cos_sb.T, -sin_sb.T
    out[LAST:FIRST] = last.reshape(32, 2, BLK).transpose(1, 0, 2).reshape(64, BLK)
    out[FIRST:SECOND, :32] = first.reshape(2 * BLK, 32)
    out[SECOND : SECOND + NBLK], out[SECOND + NBLK :] = 2.0 * cos_sb, -2.0 * sin_sb
    return jnp.asarray(out)


def pack_kernel(core_ref, w_in_ref, b_in_ref, w_out_ref, out_ref):
    core = core_ref[0]
    rows = [[], [], []]
    for k in range(2):
        lanes = pl.ds(pl.multiple_of((2 * core + k) * BLK, BLK), BLK)
        rows[0].append(w_in_ref[0, :, lanes].astype(F32) * 0.5)
        rows[1].append(w_out_ref[0, :, lanes].astype(F32))
        rows[2].append(b_in_ref[:, lanes].astype(F32) * 0.5)
    rows.append([jnp.zeros((HALF_ROWS - 162, BLK), F32)])
    packed = jnp.concatenate(sum(rows, []), axis=0).astype(BF16)
    for k in range(out_ref.shape[0]):
        out_ref[k] = packed


def pack_weights(w_in, b_in, w_out, core, copies):
    vm = pl.BlockSpec(memory_space=pltpu.VMEM)
    return pl.pallas_call(
        pack_kernel,
        out_shape=jax.ShapeDtypeStruct((copies, HALF_ROWS, BLK), BF16),
        in_specs=[pl.BlockSpec(memory_space=pltpu.SMEM)] + [vm] * 3,
        out_specs=vm,
        name="pack_weights",
    )(core, w_in, b_in, w_out)


def legendre_kernel(limit_ref, core_ref, table_ref, spec_ref, theirs_ref, ours_ref):
    slots, degrees, width = spec_ref.shape
    degree = lax.broadcasted_iota(jnp.int32, (degrees, width), 0)
    core = core_ref[0]

    def slot(i, carry):
        spec = spec_ref[i]
        masked = jnp.where(degree < limit_ref[i], spec, jnp.zeros_like(spec))
        lanes = pl.ds(pl.multiple_of(i * BLK, BLK), BLK)
        for which, ref in ((1 - core, theirs_ref), (core, ours_ref)):
            for k, y_hi in enumerate((0, 1)):
                start = pl.multiple_of((2 * y_hi + which) * BLK, BLK)
                part = dot(table_ref[i, :, pl.ds(start, BLK)], masked, 0, 0)
                ref[pl.ds(k * BLK, BLK), lanes] = part.astype(ref.dtype)
        return carry

    lax.fori_loop(0, slots, slot, 0, unroll=10)


def inverse_legendre(spectral, legendre, limit, core):
    slots, degrees, width = spectral.shape
    lats = legendre.shape[2]
    sm = pl.BlockSpec(memory_space=pltpu.SMEM)
    vm = pl.BlockSpec(memory_space=pltpu.VMEM)
    shape = (lats // 2, slots * width)
    return pl.pallas_call(
        legendre_kernel,
        out_shape=(jax.ShapeDtypeStruct(shape, BF16), jax.ShapeDtypeStruct(shape, F32)),
        in_specs=[sm, sm, vm, vm],
        out_specs=(vm, vm),
        cost_estimate=pl.CostEstimate(
            flops=2 * slots * width * degrees * lats, bytes_accessed=6_000_000, transcendentals=0
        ),
        compiler_params=pltpu.CompilerParams(vmem_limit_bytes=24 * 1024 * 1024),
        name="inverse_legendre",
    )(limit, core, legendre, spectral)


def synth_kernel(coef_ref, pos_ref, held_ref, low_ref, high_ref, grid_ref, out_ref, tab_ref, sem):
    fetch = pltpu.make_async_copy(held_ref, tab_ref, sem)
    fetch.start()
    dests, lanes = coef_ref.shape[0] // 2, coef_ref.shape[1]
    slots = dests * lanes // BLK
    coef = []
    for i in range(0, lanes, BLK):
        parts = [coef_ref[pl.ds(k * dests, dests), pl.ds(i, BLK)].astype(F32) for k in range(2)]
        coef.append((parts[0] + parts[1]).astype(BF16))
    coef = jnp.concatenate(coef, axis=0)
    pos = pos_ref[...]
    grid_ref[pl.ds(NHI * BLK, BLK), :] = jnp.zeros((BLK, BLK), F32)

    def place(p, carry):
        want = lax.broadcasted_iota(jnp.int32, (BLK, slots), 0) + p * BLK
        value = jnp.where(want == 0, 0.5, 1.0)
        pick = jnp.where(want == pos, value, 0.0).astype(BF16)
        grid_ref[pl.ds(pl.multiple_of(p * BLK, BLK), BLK), :] = dot(pick, coef, 1, 0).T
        return carry

    lax.fori_loop(0, NHI, place, 0, unroll=5)
    fetch.wait()
    first = tab_ref[pl.ds(FIRST, 2 * BLK), :][:, :32].astype(BF16)
    second = jnp.concatenate(
        [tab_ref[pl.ds(SECOND, NBLK), :], tab_ref[pl.ds(SECOND + NBLK, NBLK), :]], axis=1
    ).astype(BF16)
    tc = tab_ref[pl.ds(TURN, BLK), :]
    ts = tab_ref[pl.ds(TURN + BLK, BLK), :]

    def pair(i, carry):
        f = i * 2
        x = jnp.concatenate(
            [grid_ref[pl.ds(f, 32, stride=64), :], grid_ref[pl.ds(f + 1, 32, stride=64), :]], axis=1
        ).astype(BF16)
        z = dot(first, x, 1, 0)
        rows = []
        for k in range(2):
            re, im = z[:BLK, k * BLK : (k + 1) * BLK], z[BLK:, k * BLK : (k + 1) * BLK]
            rows.append(
                jnp.concatenate([re * tc - im * ts, re * ts + im * tc], axis=1).astype(BF16)
            )
        out = dot(second, jnp.concatenate(rows, axis=0), 1, 1)
        out_ref[pl.ds(f, NBLK, stride=64), :] = out[:, :BLK]
        out_ref[pl.ds(f + 1, NBLK, stride=64), :] = out[:, BLK:]
        return carry

    lax.fori_loop(0, 32, pair, 0, unroll=8)
    rows = low_ref.shape[0]
    low_ref[...] = out_ref[pl.ds(0, rows), :].astype(BF16)
    high_ref[...] = out_ref[pl.ds(rows, rows), :].astype(BF16)


def synthesize(coef, pos, tab):
    vm = pl.BlockSpec(memory_space=pltpu.VMEM)
    return pl.pallas_call(
        synth_kernel,
        out_shape=(jax.ShapeDtypeStruct((NBLK * 32, BLK), BF16),) * 2,
        in_specs=[vm, vm, pl.BlockSpec(memory_space=pl.ANY)],
        out_specs=(vm, vm),
        scratch_shapes=[
            pltpu.VMEM((16 * BLK, BLK), F32),
            pltpu.VMEM((NBLK * 64, BLK), F32),
            pltpu.VMEM((ROWS, BLK), F32),
            pltpu.SemaphoreType.DMA,
        ],
        compiler_params=pltpu.CompilerParams(vmem_limit_bytes=40 * 1024 * 1024),
        cost_estimate=pl.CostEstimate(flops=3_000_000_000, bytes_accessed=2_500_000, transcendentals=0),
        name="synthesize",
    )(coef, pos, tab)


def regime_blocks(at_ref, list_ref, low_ref, high_ref, w_ref, out_ref):
    core, me = at_ref[0], at_ref[1]

    for b in range(NBLK):
        cols_ref, row = (low_ref, b) if b < NBLK // 2 else (high_ref, b - NBLK // 2)
        regime = list_ref[0, b]
        x, y, z = regime // 32, regime // 8 % 4, regime % 8
        minor = jnp.where(core == 0, y, x)
        away = (jnp.where(core == 0, x, y) - me + 4) % 4
        part = jnp.where(away == 0, 0, jnp.where(away == 3, 1, jnp.where(away == 1, 2, 3)))
        e = part * 32 + minor * 8 + z
        cols = cols_ref[pl.ds(row * 64, 64), :]
        w = lambda lo, n: w_ref[e, pl.ds(lo, n), :]
        w_in = jnp.concatenate([w(0, 64), w(64, 64)], axis=1)
        w_out = jnp.concatenate([w(128, 16), w(144, 16)], axis=1)
        bias = w(160, 16)[:2].astype(F32)
        bias = jnp.concatenate([bias[0:1], bias[1:2]], axis=1)
        h = dot(cols, w_in, 0, 0) + bias
        act = (h * jnp.tanh(h) + h).astype(BF16)
        out = dot(w_out, act, 1, 1)
        out_ref[:, pl.ds(b * BLK, BLK)] = out[:8] + list_ref[1, b].astype(F32) * out[8:]


def first_network_kernel(counts, at_ref, list_ref, low_ref, high_ref, *rest):
    parts = rest[: len(counts)]
    out_ref, w_ref, sems = rest[len(counts) :]
    copies = []
    start = 0
    for k, (part, count) in enumerate(zip(parts, counts)):
        copies.append(pltpu.make_async_copy(part, w_ref.at[pl.ds(start, count)], sems.at[k]))
        copies[-1].start()
        start += count
    for copy in copies:
        copy.wait()
    regime_blocks(at_ref, list_ref, low_ref, high_ref, w_ref, out_ref)


def first_network(at, listed, cols, parts):
    vm = pl.BlockSpec(memory_space=pltpu.VMEM)
    sm = pl.BlockSpec(memory_space=pltpu.SMEM)
    hbm = pl.BlockSpec(memory_space=pl.ANY)
    counts = tuple(part.shape[0] for part in parts)
    return pl.pallas_call(
        functools.partial(first_network_kernel, counts),
        out_shape=(
            jax.ShapeDtypeStruct((8, NLON), F32),
            jax.ShapeDtypeStruct((sum(counts), HALF_ROWS, BLK), BF16),
        ),
        in_specs=[sm, sm, vm, vm] + [hbm] * len(parts),
        out_specs=(vm, vm),
        scratch_shapes=[pltpu.SemaphoreType.DMA((len(parts),))],
        compiler_params=pltpu.CompilerParams(vmem_limit_bytes=32 * 1024 * 1024),
        cost_estimate=pl.CostEstimate(
            flops=2_000_000_000, bytes_accessed=13_000_000, transcendentals=2_900_000
        ),
        name="first_network",
    )(at, listed, *cols, *parts)


def second_network(at, listed, cols, weights):
    vm = pl.BlockSpec(memory_space=pltpu.VMEM)
    sm = pl.BlockSpec(memory_space=pltpu.SMEM)
    return pl.pallas_call(
        regime_blocks,
        out_shape=jax.ShapeDtypeStruct((8, NLON), F32),
        in_specs=[sm, sm, vm, vm, vm],
        out_specs=vm,
        compiler_params=pltpu.CompilerParams(vmem_limit_bytes=32 * 1024 * 1024),
        cost_estimate=pl.CostEstimate(
            flops=2_000_000_000, bytes_accessed=8_000_000, transcendentals=2_900_000
        ),
        name="second_network",
    )(at, listed, *cols, weights)


def analysis_kernel(
    gauss_ref, own_ref, got_ref, pos_ref, held_ref, heat_ref, pay_ref, hs_ref, r_ref, tab_ref, sem
):
    fetch = pltpu.make_async_copy(held_ref, tab_ref, sem)
    fetch.start()
    for b in range(NBLK):
        lanes = pl.ds(b * BLK, BLK)
        heat = (own_ref[:, lanes] + got_ref[:, lanes]).astype(BF16)
        heat_ref[:, lanes] = heat
        hs_ref[pl.ds(b, 8, stride=BROWS), :] = heat.astype(F32)
    for lev in range(8):
        hs_ref[pl.ds(lev * BROWS + NBLK, BROWS - NBLK), :] = jnp.zeros((BROWS - NBLK, BLK), F32)
    fetch.wait()
    inner = tab_ref[pl.ds(INNER, 2 * BLK), :][:, :BROWS].astype(BF16)
    last = jnp.concatenate([tab_ref[pl.ds(LAST, 32), :], tab_ref[pl.ds(LAST + 32, 32), :]], axis=1)
    last = last.astype(BF16)
    tc = tab_ref[pl.ds(TURN, BLK), :]
    ts = tab_ref[pl.ds(TURN + BLK, BLK), :]
    scale = gauss_ref[0] * (1.0 / NLON)
    for lev in range(0, 8, 2):
        h = jnp.concatenate([hs_ref[pl.ds((lev + k) * BROWS, BROWS), :] for k in range(2)], axis=1)
        u = dot(inner, h.astype(BF16), 1, 0)
        rows = []
        for k in range(2):
            re, im = u[:BLK, k * BLK : (k + 1) * BLK], u[BLK:, k * BLK : (k + 1) * BLK]
            rows.append(
                jnp.concatenate([re * tc + im * ts, im * tc - re * ts], axis=1).astype(BF16)
            )
        spec = dot(last, jnp.concatenate(rows, axis=0), 1, 1) * scale
        r_ref[pl.ds(lev, 32, stride=8), :] = spec[:, :BLK]
        r_ref[pl.ds(lev + 1, 32, stride=8), :] = spec[:, BLK:]
    spectrum = jnp.concatenate(
        [r_ref[pl.ds(p * 16, 16), :].astype(BF16) for p in range(NHI)], axis=1
    )
    want = lax.broadcasted_iota(jnp.int32, (NHI * BLK, BLK), 0)
    rows = []
    for i in range(pos_ref.shape[0]):
        pick = jnp.where(want == pos_ref[pl.ds(i, 1), :], 1.0, 0.0).astype(BF16)
        rows.append(dot(spectrum, pick, 1, 0))
    rows.append(jnp.zeros((pay_ref.shape[1] - 16 * len(rows), BLK), F32))
    pay_ref[...] = jnp.concatenate(rows, axis=0).T.astype(BF16)


def analyze(gauss, own, got, pos_local, tab):
    vm = pl.BlockSpec(memory_space=pltpu.VMEM)
    sm = pl.BlockSpec(memory_space=pltpu.SMEM)
    return pl.pallas_call(
        analysis_kernel,
        out_shape=(
            jax.ShapeDtypeStruct((8, NLON), BF16),
            jax.ShapeDtypeStruct((pos_local.shape[1], 2 * BLK), BF16),
        ),
        in_specs=[sm] + [vm] * 3 + [pl.BlockSpec(memory_space=pl.ANY)],
        out_specs=(vm, vm),
        scratch_shapes=[
            pltpu.VMEM((8 * BROWS, BLK), F32),
            pltpu.VMEM((32 * 8, BLK), F32),
            pltpu.VMEM((ROWS, BLK), F32),
            pltpu.SemaphoreType.DMA,
        ],
        compiler_params=pltpu.CompilerParams(vmem_limit_bytes=24 * 1024 * 1024),
        cost_estimate=pl.CostEstimate(flops=1_000_000_000, bytes_accessed=1_500_000, transcendentals=0),
        name="analyze",
    )(gauss, own, got, pos_local, tab)


def forward_kernel(limit_ref, core_ref, table_ref, ours_ref, theirs_ref, out_ref):
    slots, degrees, lats = table_ref.shape
    rows = []
    for y_hi in range(2):
        ours = ours_ref[pl.ds(y_hi * BLK, BLK), :]
        theirs = theirs_ref[pl.ds(y_hi * BLK, BLK), :]
        rows += [jnp.where(core_ref[0] == k, ours, theirs) for k in range(2)]
    values = jnp.concatenate(rows, axis=0)
    flipped = jnp.concatenate([values[:, :BLK].astype(F32).T, values[:, BLK:].astype(F32).T], axis=0).astype(BF16)
    degree = lax.broadcasted_iota(jnp.int32, (16, degrees), 1)
    for i in range(slots):
        total = dot(flipped[i * 16 : i * 16 + 16], table_ref[i], 1, 1)
        out_ref[i] = jnp.where(degree < limit_ref[i], total, 0.0).astype(BF16)


def forward_legendre(legendre, ours, theirs, limit, core):
    slots, degrees, lats = legendre.shape
    sm = pl.BlockSpec(memory_space=pltpu.SMEM)
    vm = pl.BlockSpec(memory_space=pltpu.VMEM)
    return pl.pallas_call(
        forward_kernel,
        out_shape=jax.ShapeDtypeStruct((slots, 16, degrees), BF16),
        in_specs=[sm, sm, vm, vm, vm],
        out_specs=vm,
        cost_estimate=pl.CostEstimate(
            flops=32 * slots * degrees * lats, bytes_accessed=4_000_000, transcendentals=0
        ),
        compiler_params=pltpu.CompilerParams(vmem_limit_bytes=16 * 1024 * 1024),
        name="forward_legendre",
    )(limit, core, legendre, ours, theirs)


AXES = ("y_hi", "core", "x", "y_lo", "z")
SIZES = (2, 2, 4, 4, 8)


def moved(value, step):
    ids = np.arange(math.prod(SIZES)).reshape(SIZES)
    pairs = []
    for (y_hi, core, x, y_lo, z), source in np.ndenumerate(ids):
        y = y_hi * SIZES[3] + y_lo
        if core == 0:
            x = (x + step) % SIZES[2]
        else:
            y = (y + step) % (SIZES[0] * SIZES[3])
        pairs.append((int(source), int(ids[y // SIZES[3], core, x, y % SIZES[3], z])))
    return lax.ppermute(value, AXES, pairs)


def sheets():
    ids = np.arange(math.prod(SIZES)).reshape(SIZES)
    groups = ids[:, 0].reshape(-1, 32).tolist()
    return groups + np.swapaxes(ids[:, 1], 1, 2).reshape(-1, 32).tolist()


def swap(value):
    return lax.ppermute(value, "core", [(0, 1), (1, 0)])


def after(value, other):
    return lax.optimization_barrier((value, other))[0]


def exchange(value, axes):
    return lax.all_to_all(value, axes, 0, 0, tiled=True)


def gather_plane(copies):
    return lax.all_to_all(copies, AXES, 0, 0, axis_index_groups=sheets(), tiled=True)


def from_latitudes(pay):
    rows, lanes = pay.shape
    pay = jnp.broadcast_to(pay[None], (2, rows, lanes)).reshape(2 * rows, 2, lanes // 2)
    ours = exchange(pay, ("y_hi", "x", "y_lo", "z")).reshape(2 * rows, lanes)
    return ours, swap(ours)


def body(spectral, legendre, wavenumbers, regime, daylight, gauss_weight, w_in, b_in, w_out):
    slots, width, degrees = spectral.shape
    tab = tables()
    core = lax.axis_index("core").astype(jnp.int32)
    half = lax.axis_index("y_hi").astype(jnp.int32)
    band = half * 2 + core
    column = (lax.axis_index("x") * 4 + lax.axis_index("y_lo")) * 8 + lax.axis_index("z")
    wave_count = wavenumbers.shape[0]

    mine = lax.dynamic_slice_in_dim(wavenumbers, column * slots, slots)
    limit = wave_count - mine - band * degrees
    copies = pack_weights(w_in, b_in, w_out, core[None], 32)
    copies, legendre = lax.optimization_barrier((copies, legendre))
    plane = gather_plane(copies)
    theirs, ours = inverse_legendre(
        jnp.swapaxes(spectral, 1, 2), legendre, limit, core[None]
    )
    pair = (ours + swap(theirs).astype(F32)).astype(BF16)
    pair = pair.reshape(pair.shape[0], 2, -1)
    listed = jnp.stack([regime[0, :, 0], daylight[0]])
    place = wavenumbers // NBLK * BLK + wavenumbers % NBLK
    place = place.reshape(-1, slots).T
    line = place.reshape(1, wave_count)
    plane, pair, listed, place, line = lax.optimization_barrier((plane, pair, listed, place, line))
    coef = exchange(pair, ("y_hi", "x", "y_lo", "z")).reshape(pair.shape[0], -1)
    one, three, sibling = moved(plane, 1), moved(plane, -1), swap(listed)
    coef, one, three, sibling = lax.optimization_barrier((coef, one, three, sibling))
    two = moved(one, 1)

    cols = synthesize(coef, line, tab)
    theirs = tuple(swap(part) for part in cols)

    me = jnp.where(core == 0, lax.axis_index("x"), lax.axis_index("y_lo"))
    at = jnp.stack([core, me.astype(jnp.int32)])
    own, weights = first_network(at, listed, cols, (plane, one, three, two))
    sib = second_network(at, sibling, theirs, weights)
    heat, pay = analyze(gauss_weight, own, swap(sib), place, tab)
    ours, theirs = from_latitudes(pay)
    return (heat[None], forward_legendre(legendre, ours, theirs, limit, core[None]))


def solution(mesh):
    fine = Mesh(mesh.devices.reshape(SIZES), AXES)
    grp, col = ("y_hi", "core"), ("x", "y_lo", "z")
    both = grp + col
    placed = (
        P(col, None, grp),
        P(col, grp, None),
        P(),
        P(both, None, None),
        P(both, None),
        P(both),
        P(col, None, None),
        P(col, None),
        P(col, None, None),
    )
    return jax.shard_map(
        body,
        mesh=fine,
        in_specs=placed,
        out_specs=(P(both, None, None), P(col, None, grp)),
        check_vma=False,
    )
```

time: 239 us -> 171 us (0.72)
  Pallas kernels: 62.7 us -> 30.2 us
  blocking collectives: 49.5 us -> 26.6 us
  between operations: 15.1 us -> 1.56 us
  waiting for transfers between devices: 34.1 us -> 43.4 us
  local copies, waits for them, and re-layouts: 14.8 us -> 7.24 us
  starting transfers between devices: 53.2 us -> 58.9 us
  matrix products: 3.54 us -> 0 us
    pallas_call x3 -> x7, Pallas kernels: 62.7 us -> 30.2 us  [the longest x1 8.51 us: synthesize(): pl.pallas_call(synth_kernel, out_shape=(jax.ShapeDtypeStruct((NBLK * 32,...]
    all_to_all x1 -> x2, waiting for transfers between devices: 17 us -> 37.5 us  [the longest x1 20.9 us: gather_plane(): lax.all_to_all(copies, AXES, 0, 0, axis_index_groups=sheets(), tiled=True)]
    all_to_all x1 -> x2, starting transfers between devices: 13.7 us -> 30.5 us  [the longest x1 16.5 us: exchange(): return lax.all_to_all(value, axes, 0, 0, tiled=True)]
    ppermute x4 -> x3, waiting for transfers between devices: 15.1 us -> 2.09 us  [moved(): return lax.ppermute(value, AXES, pairs)]
    all_to_all x1, blocking collectives: 38.1 us -> 26.6 us  [exchange(): return lax.all_to_all(value, axes, 0, 0, tiled=True)]
    all_gather x1 -> x0, blocking collectives: 11.4 us -> none  [gather_planes(): lax.all_gather(mine[None], AXES, axis_index_groups=lines(('y', 'x')), til...]
    ppermute x6, starting transfers between devices: 26.4 us -> 15.3 us  [swap(): return lax.ppermute(value, 'core', [(0, 1), (1, 0)])]
    slice x3 -> x0, local copies, waits for them, and re-layouts: 4.14 us -> none  [the longest x1 2.07 us: gather_rest(): far_b = hop(behind[16:], ('x', -1), ('y', -1))]
  transfers between devices with their start and end apart: 12 -> 11, of which waited for: 3 -> 6; matrix products, arithmetic and copies ran while one was open for 5% -> 4% of each run, Pallas kernels for 8% -> 11%
where the time goes in v2:
time: 171 us; the launch traced here: 170 us
  starting transfers between devices  58.9 us (34%)
  waiting for transfers between devices  43.4 us (25%)
  Pallas kernels  30.2 us (18%)
  blocking collectives  26.6 us (16%)
  local copies, waits for them, and re-layouts  7.24 us (4%)
  other arithmetic  2.64 us (2%)
    all_to_all x1, blocking collectives, exchange(): return lax.all_to_all(value, axes, 0, 0, tiled=True)  26.6 us
    all_to_all x1, waiting for transfers between devices, gather_plane(): lax.all_to_all(copies, AXES, 0, 0, axis_index_groups=sheets(), tiled=True)  20.9 us
    all_to_all x1, waiting for transfers between devices, exchange(): return lax.all_to_all(value, axes, 0, 0, tiled=True)  16.6 us
    all_to_all x1, starting transfers between devices, exchange(): return lax.all_to_all(value, axes, 0, 0, tiled=True)  16.5 us
    ppermute x6, starting transfers between devices, swap(): return lax.ppermute(value, 'core', [(0, 1), (1, 0)])  15.3 us
    all_to_all x1, starting transfers between devices, gather_plane(): lax.all_to_all(copies, AXES, 0, 0, axis_index_groups=sheets(), tiled=True)  14 us
    ppermute x3, starting transfers between devices, moved(): return lax.ppermute(value, AXES, pairs)  13.1 us
    pallas_call x1, Pallas kernels, synthesize(): pl.pallas_call(synth_kernel, out_shape=(jax.ShapeDtypeStruct((NBLK * 32,...  8.51 us
  transfers between devices with their start and end apart: 11, of which 6 were waited for; matrix products, arithmetic and copies ran while one was open for 4% of the time, Pallas kernels for 11%

profile of v2, /device:TPU:1, one launch (start us, length us, event | category | flops | bytes accessed | tf_op | source)
XLA Modules:
  0.0 170.5 jit_solution(14662958801189683674)
XLA Ops:
  0.6 2.2 %pack_weights.1 = bf16[32,176,128]{2,1,0:T(8,128)(2,1)} custom-call(s32[1]{0:T(128)} %bitcast.core_ref, bf16[1,64,512]{2,1,0:T(8,128)(2,1)} %w_in_ref.1, bf16[1,512]{1,0:T(2,128)(2,1)} %b_in_ref.1, bf16[1,16,512]{2,1,0:T(8,128)(2,1)} %w_out_ref.1), custom_call_target="tpu_custom_call" | custom-call | tf_op jit(solution)/shard_map/pack_weights/pallas_call | solution.py:74
  2.9 14.0 %all-to-all-start = ((bf16[32,176,128]{2,1,0:T(8,128)(2,1)}), bf16[32,176,128]{2,1,0:T(8,128)(2,1)}, u32[]{:S(2)}, u32[]{:S(2)}) async-start(bf16[32,176,128]{2,1,0:T(8,128)(2,1)} %pack_weights.1), calls=%async_computation | async-start | bytes 2883584 | tf_op jit(solution)/shard_map/all_to_all | solution.py:401
  18.1 2.6 %inverse_legendre.1 = (bf16[256,1280]{1,0:T(8,128)(2,1)}, f32[256,1280]{1,0:T(8,128)S(1)}) custom-call(s32[10]{0:T(128)S(1)} %subtract_subtract_fusion.limit_ref, s32[1]{0:T(128)} %bitcast.core_ref, bf16[10,320,512]{2,1,0:T(8,128)(2,1)S(1)} %copy-done, bf16[10,320,128]{2,1,0:T(8,128)(2,1)S(1)} %bitcast.17), custom_call_target="tpu_custom_call" | custom-call | flops 419430400 | bytes 6000000 | tf_op jit(solution)/shard_map/inverse_legendre/pallas_call | solution.py:108
  21.8 3.4 %collective-permute-start = (bf16[256,1280]{1,0:T(8,128)(2,1)}, bf16[256,1280]{1,0:T(8,128)(2,1)}, u32[]{:S(2)}, u32[]{:S(2)}) collective-permute-start(bf16[256,1280]{1,0:T(8,128)(2,1)} %get-tuple-element.24), channel_id=1, source_target_pairs={{0,128},{128,0},{1,129},{129,1},{2,130},{130,2},{3,131},{131,3},{4... | collective-permute-start | bytes 1966088 | tf_op jit(solution)/shard_map/ppermute | solution.py:389
  27.3 2.5 %add_convert_fusion = bf16[256,1280]{1,0:T(8,128)(2,1)} fusion(f32[256,1280]{1,0:T(8,128)} %copy-done.1, bf16[256,1280]{1,0:T(8,128)(2,1)} %collective-permute-done), kind=kLoop, calls=%fused_computation | loop fusion | flops 983040 | bytes 2621440 | tf_op jit(solution)/shard_map/convert_element_type | solution.py:428
  29.8 2.5 %reshape.23 = bf16[256,2,640]{2,1,0:T(2,128)(2,1)} reshape(bf16[256,1280]{1,0:T(8,128)(2,1)} %add_convert_fusion) | data formatting | bytes 1310720 | tf_op jit(solution)/shard_map/reshape | solution.py:429
  32.3 20.9 %all-to-all-done.rest_0_ = bf16[32,176,128]{2,1,0:T(8,128)(2,1)} async-done(((bf16[32,176,128]{2,1,0:T(8,128)(2,1)}), bf16[32,176,128]{2,1,0:T(8,128)(2,1)}, u32[]{:S(2)}, u32[]{:S(2)}) %all-to-all-start) | async-done | bytes 1441824 | tf_op jit(solution)/shard_map/all_to_all | solution.py:401
  53.2 3.3 %collective-permute-start.1 = (bf16[32,176,128]{2,1,0:T(8,128)(2,1)}, bf16[32,176,128]{2,1,0:T(8,128)(2,1)}, u32[]{:S(2)}, u32[]{:S(2)}) collective-permute-start(bf16[32,176,128]{2,1,0:T(8,128)(2,1)} %all-to-all-done.rest_0_), channel_id=1, source_target_pairs={{0,32},{1,33},{2,34},{3,35},{4,36},{5,37},{6,38},{7,39},{8,40},{9,... | collective-permute-start | bytes 4325384 | tf_op jit(solution)/shard_map/ppermute | solution.py:379
  56.5 3.2 %collective-permute-start.2 = (bf16[32,176,128]{2,1,0:T(8,128)(2,1)}, bf16[32,176,128]{2,1,0:T(8,128)(2,1)}, u32[]{:S(2)}, u32[]{:S(2)}) collective-permute-start(bf16[32,176,128]{2,1,0:T(8,128)(2,1)} %all-to-all-done.rest_0_), channel_id=1, source_target_pairs={{0,96},{1,97},{2,98},{3,99},{4,100},{5,101},{6,102},{7,103},{8,104... | collective-permute-start | bytes 4325384 | tf_op jit(solution)/shard_map/ppermute | solution.py:379
  59.7 16.5 %all-to-all-start.1 = ((bf16[256,2,640]{2,1,0:T(2,128)(2,1)}), bf16[256,2,640]{2,1,0:T(2,128)(2,1)}, u32[]{:S(2)}, u32[]{:S(2)}) async-start(bf16[256,2,640]{2,1,0:T(2,128)(2,1)} %reshape.23), calls=%async_computation.1 | async-start | bytes 1310720 | tf_op jit(solution)/shard_map/all_to_all | solution.py:397
  76.2 1.9 %collective-permute-start.3 = (s32[2,88]{1,0:T(2,128)S(1)}, s32[2,88]{1,0:T(2,128)S(1)}, u32[]{:S(2)}, u32[]{:S(2)}) collective-permute-start(s32[2,88]{1,0:T(2,128)S(1)} %pad_add_fusion.list_ref), channel_id=1, source_target_pairs={{0,128},{128,0},{1,129},{129,1},{2,130},{130,2},{3,131},{131,3},{4... | collective-permute-start | bytes 2120 | tf_op jit(solution)/shard_map/ppermute | solution.py:389
  78.2 16.6 %all-to-all-done.1 = bf16[256,2,640]{2,1,0:T(2,128)(2,1)} async-done(((bf16[256,2,640]{2,1,0:T(2,128)(2,1)}), bf16[256,2,640]{2,1,0:T(2,128)(2,1)}, u32[]{:S(2)}, u32[]{:S(2)}) %all-to-all-start.1) | async-done | bytes 655392 | tf_op jit(solution)/shard_map/all_to_all | solution.py:397
  96.0 6.6 %collective-permute-start.4 = (bf16[32,176,128]{2,1,0:T(8,128)(2,1)}, bf16[32,176,128]{2,1,0:T(8,128)(2,1)}, u32[]{:S(2)}, u32[]{:S(2)}) collective-permute-start(bf16[32,176,128]{2,1,0:T(8,128)(2,1)} %collective-permute-done.1.rest_1_), channel_id=1, source_target_pairs={{0,32},{1,33},{2,34},{3,35},{4,36},{5,37},{6,38},{7,39},{8,40},{9,... | collective-permute-start | bytes 4325384 | tf_op jit(solution)/shard_map/ppermute | solution.py:379
  103.6 8.5 %synthesize.1 = (bf16[2816,128]{1,0:T(8,128)(2,1)}, bf16[2816,128]{1,0:T(8,128)(2,1)}) custom-call(bf16[256,1280]{1,0:T(8,128)(2,1)S(1)} %bitcast.18, s32[1,1280]{1,0:T(1,128)S(1)} %bitcast.23, f32[1008,128]{1,0:T(8,128)S(1)} %copy-done.3), custom_call_target="tpu_custom_call" | custom-call | flops 3000000000 | bytes 2500000 | tf_op jit(solution)/shard_map/synthesize/pallas_call | solution.py:175
  112.2 1.9 %collective-permute-start.5 = (bf16[2816,128]{1,0:T(8,128)(2,1)}, bf16[2816,128]{1,0:T(8,128)(2,1)}, u32[]{:S(2)}, u32[]{:S(2)}) collective-permute-start(bf16[2816,128]{1,0:T(8,128)(2,1)} %get-tuple-element.30.low_ref), channel_id=1, source_target_pairs={{0,128},{128,0},{1,129},{129,1},{2,130},{130,2},{3,131},{131,3},{4... | collective-permute-start | bytes 2162696 | tf_op jit(solution)/shard_map/ppermute | solution.py:389
  114.1 2.6 %collective-permute-start.6 = (bf16[2816,128]{1,0:T(8,128)(2,1)}, bf16[2816,128]{1,0:T(8,128)(2,1)}, u32[]{:S(2)}, u32[]{:S(2)}) collective-permute-start(bf16[2816,128]{1,0:T(8,128)(2,1)} %get-tuple-element.31.high_ref), channel_id=1, source_target_pairs={{0,128},{128,0},{1,129},{129,1},{2,130},{130,2},{3,131},{131,3},{4... | collective-permute-start | bytes 2162696 | tf_op jit(solution)/shard_map/ppermute | solution.py:389
  116.8 2.1 %collective-permute-done.4.rest_3_ = bf16[32,176,128]{2,1,0:T(8,128)(2,1)} collective-permute-done((bf16[32,176,128]{2,1,0:T(8,128)(2,1)}, bf16[32,176,128]{2,1,0:T(8,128)(2,1)}, u32[]{:S(2)}, u32[]{:S(2)}) %collective-permute-start.4) | collective-permute-done | bytes 1441824 | tf_op jit(solution)/shard_map/ppermute | solution.py:379
  118.8 7.3 %first_network.1 = (f32[8,11264]{1,0:T(8,128)S(1)}, bf16[128,176,128]{2,1,0:T(8,128)(2,1)S(1)}) custom-call(s32[2]{0:T(128)S(1)} %pad_add_fusion.1.at_ref, s32[2,88]{1,0:T(2,128)S(1)} %pad_add_fusion.list_ref, bf16[2816,128]{1,0:T(8,128)(2,1)} %get-tuple-element.30.low_ref, bf16[2816,128]{1,0:T(8,128)(2,1)} %get-tuple-element.31.high_ref, ...), custom_call_target="tpu_custom_call" | custom-call | flops 2000000000 | bytes 13000000 | tf_op jit(solution)/shard_map/first_network/pallas_call | solution.py:234
  126.2 4.7 %second_network.1 = f32[8,11264]{1,0:T(8,128)S(1)} custom-call(s32[2]{0:T(128)S(1)} %pad_add_fusion.1.at_ref, s32[2,88]{1,0:T(2,128)S(1)} %collective-permute-done.3.list_ref, bf16[2816,128]{1,0:T(8,128)(2,1)} %collective-permute-done.5.low_ref, bf16[2816,128]{1,0:T(8,128)(2,1)} %collective-permute-done.6.high_ref, ...), custom_call_target="tpu_custom_call" | custom-call | flops 2000000000 | bytes 8000000 | tf_op jit(solution)/shard_map/second_network/pallas_call | solution.py:254
  130.9 1.9 %collective-permute-start.7 = (f32[8,11264]{1,0:T(8,128)S(1)}, f32[8,11264]{1,0:T(8,128)S(1)}, u32[]{:S(2)}, u32[]{:S(2)}) collective-permute-start(f32[8,11264]{1,0:T(8,128)S(1)} %second_network.1), channel_id=1, source_target_pairs={{0,128},{128,0},{1,129},{129,1},{2,130},{130,2},{3,131},{131,3},{4... | collective-permute-start | bytes 1081352 | tf_op jit(solution)/shard_map/ppermute | solution.py:389
  134.5 2.5 %analyze.1 = (bf16[8,11264]{1,0:T(8,128)(2,1)}, bf16[128,256]{1,0:T(8,128)(2,1)S(1)}) custom-call(f32[1]{0:T(128)S(6)} %copy.20.gauss_ref, f32[8,11264]{1,0:T(8,128)S(1)} %get-tuple-element.34.own_ref, f32[8,11264]{1,0:T(8,128)S(1)} %collective-permute-done.7.got_ref, s32[10,128]{1,0:T(8,128)S(1)} %bitcast.22, f32[1008,128]{1,0:T(8,128)S(1)} %copy-done.4), custom_call_target="tpu_custom_call" | custom-call | flops 1000000000 | bytes 1500000 | tf_op jit(solution)/shard_map/analyze/pallas_call | solution.py:313
  137.1 26.6 %all_to_all.15 = bf16[256,2,128]{2,1,0:T(2,128)(2,1)S(1)} all-to-all(bf16[256,2,128]{2,1,0:T(2,128)(2,1)S(1)} %reshape.27), channel_id=1, replica_groups=mesh['y_hi'=2,'core'=2,'x'=4,'y_lo'=4,'z'=8] {'y_hi','x','y_lo','z'}, dimensions={0} | all-to-all | bytes 262144 | tf_op jit(solution)/shard_map/all_to_all | solution.py:397
  163.7 3.5 %collective-permute-start.8 = (bf16[256,256]{1,0:T(8,128)(2,1)S(1)}, bf16[256,256]{1,0:T(8,128)(2,1)S(1)}, u32[]{:S(2)}, u32[]{:S(2)}) collective-permute-start(bf16[256,256]{1,0:T(8,128)(2,1)S(1)} %bitcast.19), channel_id=1, source_target_pairs={{0,128},{128,0},{1,129},{129,1},{2,130},{130,2},{3,131},{131,3},{4... | collective-permute-start | bytes 393224 | tf_op jit(solution)/shard_map/ppermute | solution.py:389
  168.2 2.2 %forward_legendre.1 = bf16[10,16,320]{2,1,0:T(8,128)(2,1)} custom-call(s32[10]{0:T(128)S(1)} %subtract_subtract_fusion.limit_ref, s32[1]{0:T(128)} %bitcast.core_ref, bf16[10,320,512]{2,1,0:T(8,128)(2,1)S(1)} %copy-done, bf16[256,256]{1,0:T(8,128)(2,1)S(1)} %bitcast.20, bf16[256,256]{1,0:T(8,128)(2,1)S(1)} %collective-permute-done.8.theirs_ref), custom_call_target="tpu_custom_call" | custom-call | flops 52428800 | bytes 4000000 | tf_op jit(solution)/shard_map/forward_legendre/pallas_call | solution.py:352
  (35 shorter events, 8.6 us)
Async XLA Ops:
  0.6 16.3 %copy-start = (bf16[10,320,512]{2,1,0:T(8,128)(2,1)S(1)}, bf16[10,320,512]{2,1,0:T(8,128)(2,1)}, u32[]{:S(2)}) copy-start(bf16[10,320,512]{2,1,0:T(8,128)(2,1)} %table_ref.1) | copy-start | bytes 9830404
  2.9 14.0 %copy-start.5 = (s32[1280]{0:T(1024)S(1)}, s32[1280]{0:T(1024)}, u32[]{:S(2)}) copy-start(s32[1280]{0:T(1024)} %param.12) | copy-start | bytes 15364
  2.9 50.3 %all-to-all-start = ((bf16[32,176,128]{2,1,0:T(8,128)(2,1)}), bf16[32,176,128]{2,1,0:T(8,128)(2,1)}, u32[]{:S(2)}, u32[]{:S(2)}) async-start(bf16[32,176,128]{2,1,0:T(8,128)(2,1)} %pack_weights.1), calls=%async_computation | async-start | bytes 2883584 | tf_op jit(solution)/shard_map/all_to_all | solution.py:401
  17.0 1.1 copy-start.2
  18.1 7.4 %copy-start.6 = (s32[1,88]{1,0:T(1,128)S(1)}, s32[1,88]{1,0:T(1,128)}, u32[]{:S(2)}) copy-start(s32[1,88]{1,0:T(1,128)} %param.14) | copy-start | bytes 1060
  18.1 7.4 %copy-start.7 = (s32[1,88,1]{1,2,0:T(1,128)S(1)}, s32[1,88,1]{1,2,0:T(1,128)}, u32[]{:S(2)}) copy-start(s32[1,88,1]{1,2,0:T(1,128)} %param.13) | copy-start | bytes 1060
  20.7 1.1 copy-start.1
  21.8 5.5 %collective-permute-start = (bf16[256,1280]{1,0:T(8,128)(2,1)}, bf16[256,1280]{1,0:T(8,128)(2,1)}, u32[]{:S(2)}, u32[]{:S(2)}) collective-permute-start(bf16[256,1280]{1,0:T(8,128)(2,1)} %get-tuple-element.24), channel_id=1, source_target_pairs={{0,128},{128,0},{1,129},{129,1},{2,130},{130,2},{3,131},{131,3},{4... | collective-permute-start | bytes 1966088 | tf_op jit(solution)/shard_map/ppermute | solution.py:389
  53.2 42.7 %collective-permute-start.1 = (bf16[32,176,128]{2,1,0:T(8,128)(2,1)}, bf16[32,176,128]{2,1,0:T(8,128)(2,1)}, u32[]{:S(2)}, u32[]{:S(2)}) collective-permute-start(bf16[32,176,128]{2,1,0:T(8,128)(2,1)} %all-to-all-done.rest_0_), channel_id=1, source_target_pairs={{0,32},{1,33},{2,34},{3,35},{4,36},{5,37},{6,38},{7,39},{8,40},{9,... | collective-permute-start | bytes 4325384 | tf_op jit(solution)/shard_map/ppermute | solution.py:379
  56.5 39.4 %collective-permute-start.2 = (bf16[32,176,128]{2,1,0:T(8,128)(2,1)}, bf16[32,176,128]{2,1,0:T(8,128)(2,1)}, u32[]{:S(2)}, u32[]{:S(2)}) collective-permute-start(bf16[32,176,128]{2,1,0:T(8,128)(2,1)} %all-to-all-done.rest_0_), channel_id=1, source_target_pairs={{0,96},{1,97},{2,98},{3,99},{4,100},{5,101},{6,102},{7,103},{8,104... | collective-permute-start | bytes 4325384 | tf_op jit(solution)/shard_map/ppermute | solution.py:379
  59.7 35.1 %all-to-all-start.1 = ((bf16[256,2,640]{2,1,0:T(2,128)(2,1)}), bf16[256,2,640]{2,1,0:T(2,128)(2,1)}, u32[]{:S(2)}, u32[]{:S(2)}) async-start(bf16[256,2,640]{2,1,0:T(2,128)(2,1)} %reshape.23), calls=%async_computation.1 | async-start | bytes 1310720 | tf_op jit(solution)/shard_map/all_to_all | solution.py:397
  76.2 19.7 %collective-permute-start.3 = (s32[2,88]{1,0:T(2,128)S(1)}, s32[2,88]{1,0:T(2,128)S(1)}, u32[]{:S(2)}, u32[]{:S(2)}) collective-permute-start(s32[2,88]{1,0:T(2,128)S(1)} %pad_add_fusion.list_ref), channel_id=1, source_target_pairs={{0,128},{128,0},{1,129},{129,1},{2,130},{130,2},{3,131},{131,3},{4... | collective-permute-start | bytes 2120 | tf_op jit(solution)/shard_map/ppermute | solution.py:389
  96.0 22.9 %collective-permute-start.4 = (bf16[32,176,128]{2,1,0:T(8,128)(2,1)}, bf16[32,176,128]{2,1,0:T(8,128)(2,1)}, u32[]{:S(2)}, u32[]{:S(2)}) collective-permute-start(bf16[32,176,128]{2,1,0:T(8,128)(2,1)} %collective-permute-done.1.rest_1_), channel_id=1, source_target_pairs={{0,32},{1,33},{2,34},{3,35},{4,36},{5,37},{6,38},{7,39},{8,40},{9,... | collective-permute-start | bytes 4325384 | tf_op jit(solution)/shard_map/ppermute | solution.py:379
  102.6 1.0 copy-start.3
  112.2 14.0 %collective-permute-start.5 = (bf16[2816,128]{1,0:T(8,128)(2,1)}, bf16[2816,128]{1,0:T(8,128)(2,1)}, u32[]{:S(2)}, u32[]{:S(2)}) collective-permute-start(bf16[2816,128]{1,0:T(8,128)(2,1)} %get-tuple-element.30.low_ref), channel_id=1, source_target_pairs={{0,128},{128,0},{1,129},{129,1},{2,130},{130,2},{3,131},{131,3},{4... | collective-permute-start | bytes 2162696 | tf_op jit(solution)/shard_map/ppermute | solution.py:389
  114.1 12.1 %collective-permute-start.6 = (bf16[2816,128]{1,0:T(8,128)(2,1)}, bf16[2816,128]{1,0:T(8,128)(2,1)}, u32[]{:S(2)}, u32[]{:S(2)}) collective-permute-start(bf16[2816,128]{1,0:T(8,128)(2,1)} %get-tuple-element.31.high_ref), channel_id=1, source_target_pairs={{0,128},{128,0},{1,129},{129,1},{2,130},{130,2},{3,131},{131,3},{4... | collective-permute-start | bytes 2162696 | tf_op jit(solution)/shard_map/ppermute | solution.py:389
  126.2 8.3 %copy-start.4 = (f32[1008,128]{1,0:T(8,128)S(1)}, f32[1008,128]{1,0:T(8,128)}, u32[]{:S(2)}) copy-start(f32[1008,128]{1,0:T(8,128)} %constant.59.clone.held_ref) | copy-start | bytes 1548292
  130.9 3.6 %collective-permute-start.7 = (f32[8,11264]{1,0:T(8,128)S(1)}, f32[8,11264]{1,0:T(8,128)S(1)}, u32[]{:S(2)}, u32[]{:S(2)}) collective-permute-start(f32[8,11264]{1,0:T(8,128)S(1)} %second_network.1), channel_id=1, source_target_pairs={{0,128},{128,0},{1,129},{129,1},{2,130},{130,2},{3,131},{131,3},{4... | collective-permute-start | bytes 1081352 | tf_op jit(solution)/shard_map/ppermute | solution.py:389
  163.7 4.5 %collective-permute-start.8 = (bf16[256,256]{1,0:T(8,128)(2,1)S(1)}, bf16[256,256]{1,0:T(8,128)(2,1)S(1)}, u32[]{:S(2)}, u32[]{:S(2)}) collective-permute-start(bf16[256,256]{1,0:T(8,128)(2,1)S(1)} %bitcast.19), channel_id=1, source_target_pairs={{0,128},{128,0},{1,129},{129,1},{2,130},{130,2},{3,131},{131,3},{4... | collective-permute-start | bytes 393224 | tf_op jit(solution)/shard_map/ppermute | solution.py:389

commit v3 on v2

--- a/solution.py
+++ b/solution.py
@@ -80,17 +80,17 @@
     )(core, w_in, b_in, w_out)
 
 
-def legendre_kernel(limit_ref, core_ref, table_ref, spec_ref, theirs_ref, ours_ref):
+def legendre_kernel(limit_ref, at_ref, table_ref, spec_ref, theirs_ref, ours_ref):
     slots, degrees, width = spec_ref.shape
     degree = lax.broadcasted_iota(jnp.int32, (degrees, width), 0)
-    core = core_ref[0]
+    core, half = at_ref[0], at_ref[1]
 
     def slot(i, carry):
         spec = spec_ref[i]
         masked = jnp.where(degree < limit_ref[i], spec, jnp.zeros_like(spec))
         lanes = pl.ds(pl.multiple_of(i * BLK, BLK), BLK)
         for which, ref in ((1 - core, theirs_ref), (core, ours_ref)):
-            for k, y_hi in enumerate((0, 1)):
+            for k, y_hi in enumerate((1 - half, half)):
                 start = pl.multiple_of((2 * y_hi + which) * BLK, BLK)
                 part = dot(table_ref[i, :, pl.ds(start, BLK)], masked, 0, 0)
                 ref[pl.ds(k * BLK, BLK), lanes] = part.astype(ref.dtype)
@@ -99,7 +99,7 @@
     lax.fori_loop(0, slots, slot, 0, unroll=10)
 
 
-def inverse_legendre(spectral, legendre, limit, core):
+def inverse_legendre(spectral, legendre, limit, at):
     slots, degrees, width = spectral.shape
     lats = legendre.shape[2]
     sm = pl.BlockSpec(memory_space=pltpu.SMEM)
@@ -113,21 +113,17 @@
         cost_estimate=pl.CostEstimate(
             flops=2 * slots * width * degrees * lats, bytes_accessed=6_000_000, transcendentals=0
         ),
-        compiler_params=pltpu.CompilerParams(vmem_limit_bytes=24 * 1024 * 1024),
+        compiler_params=pltpu.CompilerParams(vmem_limit_bytes=12 * 1024 * 1024),
         name="inverse_legendre",
-    )(limit, core, legendre, spectral)
+    )(limit, at, legendre, spectral)
 
 
 def synth_kernel(coef_ref, pos_ref, held_ref, low_ref, high_ref, grid_ref, out_ref, tab_ref, sem):
     fetch = pltpu.make_async_copy(held_ref, tab_ref, sem)
     fetch.start()
-    dests, lanes = coef_ref.shape[0] // 2, coef_ref.shape[1]
+    dests, lanes = coef_ref.shape
     slots = dests * lanes // BLK
-    coef = []
-    for i in range(0, lanes, BLK):
-        parts = [coef_ref[pl.ds(k * dests, dests), pl.ds(i, BLK)].astype(F32) for k in range(2)]
-        coef.append((parts[0] + parts[1]).astype(BF16))
-    coef = jnp.concatenate(coef, axis=0)
+    coef = jnp.concatenate([coef_ref[:, pl.ds(i, BLK)] for i in range(0, lanes, BLK)], axis=0)
     pos = pos_ref[...]
     grid_ref[pl.ds(NHI * BLK, BLK), :] = jnp.zeros((BLK, BLK), F32)
 
@@ -183,7 +179,7 @@
             pltpu.VMEM((ROWS, BLK), F32),
             pltpu.SemaphoreType.DMA,
         ],
-        compiler_params=pltpu.CompilerParams(vmem_limit_bytes=40 * 1024 * 1024),
+        compiler_params=pltpu.CompilerParams(vmem_limit_bytes=14 * 1024 * 1024),
         cost_estimate=pl.CostEstimate(flops=3_000_000_000, bytes_accessed=2_500_000, transcendentals=0),
         name="synthesize",
     )(coef, pos, tab)
@@ -240,7 +236,7 @@
         in_specs=[sm, sm, vm, vm] + [hbm] * len(parts),
         out_specs=(vm, vm),
         scratch_shapes=[pltpu.SemaphoreType.DMA((len(parts),))],
-        compiler_params=pltpu.CompilerParams(vmem_limit_bytes=32 * 1024 * 1024),
+        compiler_params=pltpu.CompilerParams(vmem_limit_bytes=14 * 1024 * 1024),
         cost_estimate=pl.CostEstimate(
             flops=2_000_000_000, bytes_accessed=13_000_000, transcendentals=2_900_000
         ),
@@ -256,7 +252,7 @@
         out_shape=jax.ShapeDtypeStruct((8, NLON), F32),
         in_specs=[sm, sm, vm, vm, vm],
         out_specs=vm,
-        compiler_params=pltpu.CompilerParams(vmem_limit_bytes=32 * 1024 * 1024),
+        compiler_params=pltpu.CompilerParams(vmem_limit_bytes=10 * 1024 * 1024),
         cost_estimate=pl.CostEstimate(
             flops=2_000_000_000, bytes_accessed=8_000_000, transcendentals=2_900_000
         ),
@@ -304,7 +300,9 @@
         pick = jnp.where(want == pos_ref[pl.ds(i, 1), :], 1.0, 0.0).astype(BF16)
         rows.append(dot(spectrum, pick, 1, 0))
     rows.append(jnp.zeros((pay_ref.shape[1] - 16 * len(rows), BLK), F32))
-    pay_ref[...] = jnp.concatenate(rows, axis=0).T.astype(BF16)
+    pay = jnp.concatenate(rows, axis=0).T.astype(BF16)
+    for y_hi in range(2):
+        pay_ref[pl.ds(y_hi * BLK, BLK), :] = pay
 
 
 def analyze(gauss, own, got, pos_local, tab):
@@ -314,7 +312,7 @@
         analysis_kernel,
         out_shape=(
             jax.ShapeDtypeStruct((8, NLON), BF16),
-            jax.ShapeDtypeStruct((pos_local.shape[1], 2 * BLK), BF16),
+            jax.ShapeDtypeStruct((2 * pos_local.shape[1], 2 * BLK), BF16),
         ),
         in_specs=[sm] + [vm] * 3 + [pl.BlockSpec(memory_space=pl.ANY)],
         out_specs=(vm, vm),
@@ -324,7 +322,7 @@
             pltpu.VMEM((ROWS, BLK), F32),
             pltpu.SemaphoreType.DMA,
         ],
-        compiler_params=pltpu.CompilerParams(vmem_limit_bytes=24 * 1024 * 1024),
+        compiler_params=pltpu.CompilerParams(vmem_limit_bytes=8 * 1024 * 1024),
         cost_estimate=pl.CostEstimate(flops=1_000_000_000, bytes_accessed=1_500_000, transcendentals=0),
         name="analyze",
     )(gauss, own, got, pos_local, tab)
@@ -357,7 +355,7 @@
         cost_estimate=pl.CostEstimate(
             flops=32 * slots * degrees * lats, bytes_accessed=4_000_000, transcendentals=0
         ),
-        compiler_params=pltpu.CompilerParams(vmem_limit_bytes=16 * 1024 * 1024),
+        compiler_params=pltpu.CompilerParams(vmem_limit_bytes=8 * 1024 * 1024),
         name="forward_legendre",
     )(limit, core, legendre, ours, theirs)
 
@@ -403,8 +401,8 @@
 
 def from_latitudes(pay):
     rows, lanes = pay.shape
-    pay = jnp.broadcast_to(pay[None], (2, rows, lanes)).reshape(2 * rows, 2, lanes // 2)
-    ours = exchange(pay, ("y_hi", "x", "y_lo", "z")).reshape(2 * rows, lanes)
+    pay = pay.reshape(rows, 2, lanes // 2)
+    ours = exchange(pay, ("y_hi", "x", "y_lo", "z")).reshape(rows, lanes)
     return ours, swap(ours)
 
 
@@ -423,18 +421,22 @@
     copies, legendre = lax.optimization_barrier((copies, legendre))
     plane = gather_plane(copies)
     theirs, ours = inverse_legendre(
-        jnp.swapaxes(spectral, 1, 2), legendre, limit, core[None]
+        jnp.swapaxes(spectral, 1, 2), legendre, limit, jnp.stack([core, half])
     )
-    pair = (ours + swap(theirs).astype(F32)).astype(BF16)
-    pair = pair.reshape(pair.shape[0], 2, -1)
+    got = swap(theirs)
+    rows, lanes = ours.shape[0] // 2, ours.shape[1]
+    far = (ours[:rows] + got[:rows].astype(F32)).astype(BF16)
+    far = lax.ppermute(far, "y_hi", [(0, 1), (1, 0)])
+    near = ours[rows:] + got[rows:].astype(F32) + far.astype(F32)
+    near = near.astype(BF16).reshape(rows, 2, lanes // 2)
     listed = jnp.stack([regime[0, :, 0], daylight[0]])
     place = wavenumbers // NBLK * BLK + wavenumbers % NBLK
     place = place.reshape(-1, slots).T
     line = place.reshape(1, wave_count)
-    plane, pair, listed, place, line = lax.optimization_barrier((plane, pair, listed, place, line))
-    coef = exchange(pair, ("y_hi", "x", "y_lo", "z")).reshape(pair.shape[0], -1)
+    plane, near, listed, place, line = lax.optimization_barrier((plane, near, listed, place, line))
+    coef = exchange(near, ("x", "y_lo", "z")).reshape(rows, lanes)
     one, three, sibling = moved(plane, 1), moved(plane, -1), swap(listed)
-    coef, one, three, sibling = lax.optimization_barrier((coef, one, three, sibling))
+    coef, sibling = lax.optimization_barrier((coef, sibling))
     two = moved(one, 1)
 
     cols = synthesize(coef, line, tab)
@@ -442,8 +444,8 @@
 
     me = jnp.where(core == 0, lax.axis_index("x"), lax.axis_index("y_lo"))
     at = jnp.stack([core, me.astype(jnp.int32)])
-    own, weights = first_network(at, listed, cols, (plane, one, three, two))
-    sib = second_network(at, sibling, theirs, weights)
+    sib, weights = first_network(at, sibling, theirs, (plane, one, three, two))
+    own = second_network(at, listed, cols, weights)
     heat, pay = analyze(gauss_weight, own, swap(sib), place, tab)
     ours, theirs = from_latitudes(pay)
     return (heat[None], forward_legendre(legendre, ours, theirs, limit, core[None]))

time: 171 us -> 156 us (0.912)
  waiting for transfers between devices: 43.4 us -> 24 us
  starting transfers between devices: 58.9 us -> 66.1 us
  local copies, waits for them, and re-layouts: 7.24 us -> 5.4 us
    all_to_all x1, waiting for transfers between devices: 16.6 us -> 0.01 us  [exchange(): return lax.all_to_all(value, axes, 0, 0, tiled=True)]
    all_to_all x1, waiting for transfers between devices: 20.9 us -> 6.81 us  [gather_plane(): lax.all_to_all(copies, AXES, 0, 0, axis_index_groups=sheets(), tiled=True)]
    ppermute x0 -> x1, waiting for transfers between devices: none -> 9.61 us  [body(): far = lax.ppermute(far, 'y_hi', [(0, 1), (1, 0)])]
    ppermute x0 -> x1, starting transfers between devices: none -> 6.27 us  [body(): far = lax.ppermute(far, 'y_hi', [(0, 1), (1, 0)])]
    all_to_all x1, starting transfers between devices: 16.5 us -> 12.6 us  [exchange(): return lax.all_to_all(value, axes, 0, 0, tiled=True)]
    ppermute x6, starting transfers between devices: 15.3 us -> 19.2 us  [swap(): return lax.ppermute(value, 'core', [(0, 1), (1, 0)])]
    unnamed x19 -> x21, local copies, waits for them, and re-layouts: 4.47 us -> 3.4 us
  transfers between devices with their start and end apart: 11 -> 12, of which waited for: 6 -> 8; matrix products, arithmetic and copies ran while one was open for 4% -> 4% of each run, Pallas kernels for 11% -> 10%
where the time goes in v3:
time: 156 us
  starting transfers between devices  66.1 us (42%)
  Pallas kernels  29.3 us (19%)
  blocking collectives  25.9 us (17%)
  waiting for transfers between devices  24 us (15%)
  local copies, waits for them, and re-layouts  5.4 us (3%)
  other arithmetic  3.22 us (2%)
  between operations  1.56 us (1%)
    all_to_all x1, blocking collectives, exchange(): return lax.all_to_all(value, axes, 0, 0, tiled=True)  25.9 us
    ppermute x6, starting transfers between devices, swap(): return lax.ppermute(value, 'core', [(0, 1), (1, 0)])  19.2 us
    ppermute x3, starting transfers between devices, moved(): return lax.ppermute(value, AXES, pairs)  14.1 us
    all_to_all x1, starting transfers between devices, gather_plane(): lax.all_to_all(copies, AXES, 0, 0, axis_index_groups=sheets(), tiled=True)  14 us
    all_to_all x1, starting transfers between devices, exchange(): return lax.all_to_all(value, axes, 0, 0, tiled=True)  12.6 us
    ppermute x1, waiting for transfers between devices, body(): far = lax.ppermute(far, 'y_hi', [(0, 1), (1, 0)])  9.61 us
    pallas_call x1, Pallas kernels, synthesize(): pl.pallas_call(synth_kernel, out_shape=(jax.ShapeDtypeStruct((NBLK * 32,...  8.45 us
    pallas_call x1, Pallas kernels, first_network(): pl.pallas_call(functools.partial(first_network_kernel, counts), out_shape...  7.35 us
  transfers between devices with their start and end apart: 12, of which 8 were waited for; matrix products, arithmetic and copies ran while one was open for 4% of the time, Pallas kernels for 10%

profile of v3, /device:TPU:1, one launch (start us, length us, event | category | flops | bytes accessed | tf_op | source)
XLA Modules:
  0.0 155.6 jit_solution(3894347960418683896)
XLA Ops:
  0.6 2.2 %pack_weights.1 = bf16[32,176,128]{2,1,0:T(8,128)(2,1)} custom-call(s32[1]{0:T(128)} %bitcast.core_ref, bf16[1,64,512]{2,1,0:T(8,128)(2,1)} %w_in_ref.1, bf16[1,512]{1,0:T(2,128)(2,1)} %b_in_ref.1, bf16[1,16,512]{2,1,0:T(8,128)(2,1)} %w_out_ref.1), custom_call_target="tpu_custom_call" | custom-call | tf_op jit(solution)/shard_map/pack_weights/pallas_call | solution.py:74
  2.9 14.0 %all-to-all-start = ((bf16[32,176,128]{2,1,0:T(8,128)(2,1)}), bf16[32,176,128]{2,1,0:T(8,128)(2,1)}, u32[]{:S(2)}, u32[]{:S(2)}) async-start(bf16[32,176,128]{2,1,0:T(8,128)(2,1)} %pack_weights.1), calls=%async_computation | async-start | bytes 2883584 | tf_op jit(solution)/shard_map/all_to_all | solution.py:399
  20.0 3.6 %collective-permute-start = (bf16[256,1280]{1,0:T(8,128)(2,1)S(1)}, bf16[256,1280]{1,0:T(8,128)(2,1)S(1)}, u32[]{:S(2)}, u32[]{:S(2)}) collective-permute-start(bf16[256,1280]{1,0:T(8,128)(2,1)S(1)} %get-tuple-element.22), channel_id=1, source_target_pairs={{0,128},{128,0},{1,129},{129,1},{2,130},{130,2},{3,131},{131,3},{4... | collective-permute-start | bytes 1966088 | tf_op jit(solution)/shard_map/ppermute | solution.py:387
  26.3 6.3 %collective-permute-start.1 = (bf16[128,1280]{1,0:T(8,128)(2,1)}, bf16[128,1280]{1,0:T(8,128)(2,1)}, u32[]{:S(2)}, u32[]{:S(2)}) collective-permute-start(bf16[128,1280]{1,0:T(8,128)(2,1)} %add_convert_fusion.1), channel_id=1, source_target_pairs={{0,256},{256,0},{1,257},{257,1},{2,258},{258,2},{3,259},{259,3},{4... | collective-permute-start | bytes 983048 | tf_op jit(solution)/shard_map/ppermute | solution.py:429
  32.9 9.6 %collective-permute-done.1 = bf16[128,1280]{1,0:T(8,128)(2,1)} collective-permute-done((bf16[128,1280]{1,0:T(8,128)(2,1)}, bf16[128,1280]{1,0:T(8,128)(2,1)}, u32[]{:S(2)}, u32[]{:S(2)}) %collective-permute-start.1) | collective-permute-done | bytes 327712 | tf_op jit(solution)/shard_map/ppermute | solution.py:429
  42.5 2.1 %add_convert_fusion = bf16[128,1280]{1,0:T(8,128)(2,1)} fusion(bf16[128,1280]{1,0:T(8,128)(2,1)} %collective-permute-done.1, f32[256,1280]{1,0:T(8,128)} %copy-done.1, bf16[256,1280]{1,0:T(8,128)(2,1)} %copy-done.5), kind=kLoop, calls=%fused_computation | loop fusion | flops 819200 | bytes 1638400 | tf_op jit(solution)/shard_map/convert_element_type | solution.py:431
  46.4 6.8 %all-to-all-done.rest_0_ = bf16[32,176,128]{2,1,0:T(8,128)(2,1)} async-done(((bf16[32,176,128]{2,1,0:T(8,128)(2,1)}), bf16[32,176,128]{2,1,0:T(8,128)(2,1)}, u32[]{:S(2)}, u32[]{:S(2)}) %all-to-all-start) | async-done | bytes 1441824 | tf_op jit(solution)/shard_map/all_to_all | solution.py:399
  53.2 4.9 %collective-permute-start.5 = (bf16[32,176,128]{2,1,0:T(8,128)(2,1)}, bf16[32,176,128]{2,1,0:T(8,128)(2,1)}, u32[]{:S(2)}, u32[]{:S(2)}) collective-permute-start(bf16[32,176,128]{2,1,0:T(8,128)(2,1)} %all-to-all-done.rest_0_), channel_id=1, source_target_pairs={{0,32},{1,33},{2,34},{3,35},{4,36},{5,37},{6,38},{7,39},{8,40},{9,... | collective-permute-start | bytes 4325384 | tf_op jit(solution)/shard_map/ppermute | solution.py:377
  58.1 12.6 %all-to-all-start.1 = ((bf16[128,2,640]{2,1,0:T(2,128)(2,1)}), bf16[128,2,640]{2,1,0:T(2,128)(2,1)}, u32[]{:S(2)}, u32[]{:S(2)}) async-start(bf16[128,2,640]{2,1,0:T(2,128)(2,1)} %reshape.22), calls=%async_computation.1 | async-start | bytes 655360 | tf_op jit(solution)/shard_map/all_to_all | solution.py:395
  70.7 3.1 %collective-permute-start.6 = (bf16[32,176,128]{2,1,0:T(8,128)(2,1)}, bf16[32,176,128]{2,1,0:T(8,128)(2,1)}, u32[]{:S(2)}, u32[]{:S(2)}) collective-permute-start(bf16[32,176,128]{2,1,0:T(8,128)(2,1)} %all-to-all-done.rest_0_), channel_id=1, source_target_pairs={{0,96},{1,97},{2,98},{3,99},{4,100},{5,101},{6,102},{7,103},{8,104... | collective-permute-start | bytes 4325384 | tf_op jit(solution)/shard_map/ppermute | solution.py:377
  73.8 2.4 %collective-permute-done.5.rest_1_ = bf16[32,176,128]{2,1,0:T(8,128)(2,1)} collective-permute-done((bf16[32,176,128]{2,1,0:T(8,128)(2,1)}, bf16[32,176,128]{2,1,0:T(8,128)(2,1)}, u32[]{:S(2)}, u32[]{:S(2)}) %collective-permute-start.5) | collective-permute-done | bytes 1441824 | tf_op jit(solution)/shard_map/ppermute | solution.py:377
  76.3 6.1 %collective-permute-start.7 = (bf16[32,176,128]{2,1,0:T(8,128)(2,1)}, bf16[32,176,128]{2,1,0:T(8,128)(2,1)}, u32[]{:S(2)}, u32[]{:S(2)}) collective-permute-start(bf16[32,176,128]{2,1,0:T(8,128)(2,1)} %collective-permute-done.5.rest_1_), channel_id=1, source_target_pairs={{0,32},{1,33},{2,34},{3,35},{4,36},{5,37},{6,38},{7,39},{8,40},{9,... | collective-permute-start | bytes 4325384 | tf_op jit(solution)/shard_map/ppermute | solution.py:377
  82.4 1.9 %collective-permute-start.2 = (s32[2,88]{1,0:T(2,128)S(1)}, s32[2,88]{1,0:T(2,128)S(1)}, u32[]{:S(2)}, u32[]{:S(2)}) collective-permute-start(s32[2,88]{1,0:T(2,128)S(1)} %pad_add_fusion.list_ref), channel_id=1, source_target_pairs={{0,128},{128,0},{1,129},{129,1},{2,130},{130,2},{3,131},{131,3},{4... | collective-permute-start | bytes 2120 | tf_op jit(solution)/shard_map/ppermute | solution.py:387
  86.4 8.5 %synthesize.1 = (bf16[2816,128]{1,0:T(8,128)(2,1)}, bf16[2816,128]{1,0:T(8,128)(2,1)}) custom-call(bf16[128,1280]{1,0:T(8,128)(2,1)S(1)} %bitcast.21, s32[1,1280]{1,0:T(1,128)S(1)} %bitcast.24, f32[1008,128]{1,0:T(8,128)S(1)} %copy-done.3), custom_call_target="tpu_custom_call" | custom-call | flops 3000000000 | bytes 2500000 | tf_op jit(solution)/shard_map/synthesize/pallas_call | solution.py:171
  94.9 6.0 %collective-permute-start.3 = (bf16[2816,128]{1,0:T(8,128)(2,1)}, bf16[2816,128]{1,0:T(8,128)(2,1)}, u32[]{:S(2)}, u32[]{:S(2)}) collective-permute-start(bf16[2816,128]{1,0:T(8,128)(2,1)} %get-tuple-element.27.low_ref), channel_id=1, source_target_pairs={{0,128},{128,0},{1,129},{129,1},{2,130},{130,2},{3,131},{131,3},{4... | collective-permute-start | bytes 2162696 | tf_op jit(solution)/shard_map/ppermute | solution.py:387
  100.9 1.9 %collective-permute-start.4 = (bf16[2816,128]{1,0:T(8,128)(2,1)}, bf16[2816,128]{1,0:T(8,128)(2,1)}, u32[]{:S(2)}, u32[]{:S(2)}) collective-permute-start(bf16[2816,128]{1,0:T(8,128)(2,1)} %get-tuple-element.28.high_ref), channel_id=1, source_target_pairs={{0,128},{128,0},{1,129},{129,1},{2,130},{130,2},{3,131},{131,3},{4... | collective-permute-start | bytes 2162696 | tf_op jit(solution)/shard_map/ppermute | solution.py:387
  103.0 2.3 %collective-permute-done.4.high_ref = bf16[2816,128]{1,0:T(8,128)(2,1)} collective-permute-done((bf16[2816,128]{1,0:T(8,128)(2,1)}, bf16[2816,128]{1,0:T(8,128)(2,1)}, u32[]{:S(2)}, u32[]{:S(2)}) %collective-permute-start.4) | collective-permute-done | bytes 720928 | tf_op jit(solution)/shard_map/ppermute | solution.py:387
  105.3 7.3 %first_network.1 = (f32[8,11264]{1,0:T(8,128)S(1)}, bf16[128,176,128]{2,1,0:T(8,128)(2,1)S(1)}) custom-call(s32[2]{0:T(128)S(1)} %pad_add_fusion.1.at_ref, s32[2,88]{1,0:T(2,128)S(1)} %collective-permute-done.2.list_ref, bf16[2816,128]{1,0:T(8,128)(2,1)} %collective-permute-done.3.low_ref, bf16[2816,128]{1,0:T(8,128)(2,1)} %collective-permute-done.4.high_ref, ...), custom_call_target="tpu_custom_call" | custom-call | flops 2000000000 | bytes 13000000 | tf_op jit(solution)/shard_map/first_network/pallas_call | solution.py:230
  112.7 2.2 %collective-permute-start.8 = (f32[8,11264]{1,0:T(8,128)S(1)}, f32[8,11264]{1,0:T(8,128)S(1)}, u32[]{:S(2)}, u32[]{:S(2)}) collective-permute-start(f32[8,11264]{1,0:T(8,128)S(1)} %get-tuple-element.32), channel_id=1, source_target_pairs={{0,128},{128,0},{1,129},{129,1},{2,130},{130,2},{3,131},{131,3},{4... | collective-permute-start | bytes 1081352 | tf_op jit(solution)/shard_map/ppermute | solution.py:387
  115.6 4.7 %second_network.1.own_ref = f32[8,11264]{1,0:T(8,128)S(1)} custom-call(s32[2]{0:T(128)S(1)} %pad_add_fusion.1.at_ref, s32[2,88]{1,0:T(2,128)S(1)} %pad_add_fusion.list_ref, bf16[2816,128]{1,0:T(8,128)(2,1)} %get-tuple-element.27.low_ref, bf16[2816,128]{1,0:T(8,128)(2,1)} %get-tuple-element.28.high_ref, bf16[128,176,128]{2,1,0:T(8,128)(2,1)S(1)} %get-tuple-element.31.w_ref), custom_call_target="tpu_custom_call" | custom-call | flops 2000000000 | bytes 8000000 | tf_op jit(solution)/shard_map/second_network/pallas_call | solution.py:250
  120.3 2.6 %analyze.1 = (bf16[8,11264]{1,0:T(8,128)(2,1)}, bf16[256,256]{1,0:T(8,128)(2,1)S(1)}) custom-call(f32[1]{0:T(128)S(6)} %copy.20.gauss_ref, f32[8,11264]{1,0:T(8,128)S(1)} %second_network.1.own_ref, f32[8,11264]{1,0:T(8,128)S(1)} %collective-permute-done.8.got_ref, s32[10,128]{1,0:T(8,128)S(1)} %bitcast.23, f32[1008,128]{1,0:T(8,128)S(1)} %copy-done.4), custom_call_target="tpu_custom_call" | custom-call | flops 1000000000 | bytes 1500000 | tf_op jit(solution)/shard_map/analyze/pallas_call | solution.py:311
  122.9 25.9 %all_to_all.15 = bf16[256,2,128]{2,1,0:T(2,128)(2,1)S(1)} all-to-all(bf16[256,2,128]{2,1,0:T(2,128)(2,1)S(1)} %reshape.26), channel_id=1, replica_groups=mesh['y_hi'=2,'core'=2,'x'=4,'y_lo'=4,'z'=8] {'y_hi','x','y_lo','z'}, dimensions={0} | all-to-all | bytes 262144 | tf_op jit(solution)/shard_map/all_to_all | solution.py:395
  148.8 3.5 %collective-permute-start.9 = (bf16[256,256]{1,0:T(8,128)(2,1)S(1)}, bf16[256,256]{1,0:T(8,128)(2,1)S(1)}, u32[]{:S(2)}, u32[]{:S(2)}) collective-permute-start(bf16[256,256]{1,0:T(8,128)(2,1)S(1)} %bitcast.19), channel_id=1, source_target_pairs={{0,128},{128,0},{1,129},{129,1},{2,130},{130,2},{3,131},{131,3},{4... | collective-permute-start | bytes 393224 | tf_op jit(solution)/shard_map/ppermute | solution.py:387
  153.3 2.2 %forward_legendre.1 = bf16[10,16,320]{2,1,0:T(8,128)(2,1)} custom-call(s32[10]{0:T(128)S(1)} %subtract_subtract_fusion.limit_ref, s32[1]{0:T(128)} %bitcast.core_ref, bf16[10,320,512]{2,1,0:T(8,128)(2,1)S(1)} %copy-done, bf16[256,256]{1,0:T(8,128)(2,1)S(1)} %bitcast.20, bf16[256,256]{1,0:T(8,128)(2,1)S(1)} %collective-permute-done.9.theirs_ref), custom_call_target="tpu_custom_call" | custom-call | flops 52428800 | bytes 4000000 | tf_op jit(solution)/shard_map/forward_legendre/pallas_call | solution.py:350
  (40 shorter events, 11.2 us)
Async XLA Ops:
  0.6 16.4 %copy-start = (bf16[10,320,512]{2,1,0:T(8,128)(2,1)S(1)}, bf16[10,320,512]{2,1,0:T(8,128)(2,1)}, u32[]{:S(2)}) copy-start(bf16[10,320,512]{2,1,0:T(8,128)(2,1)} %table_ref.1) | copy-start | bytes 9830404
  2.9 14.1 %copy-start.6 = (s32[1280]{0:T(1024)S(1)}, s32[1280]{0:T(1024)}, u32[]{:S(2)}) copy-start(s32[1280]{0:T(1024)} %param.12) | copy-start | bytes 15364
  2.9 50.3 %all-to-all-start = ((bf16[32,176,128]{2,1,0:T(8,128)(2,1)}), bf16[32,176,128]{2,1,0:T(8,128)(2,1)}, u32[]{:S(2)}, u32[]{:S(2)}) async-start(bf16[32,176,128]{2,1,0:T(8,128)(2,1)} %pack_weights.1), calls=%async_computation | async-start | bytes 2883584 | tf_op jit(solution)/shard_map/all_to_all | solution.py:399
  17.0 1.1 copy-start.2
  20.0 5.3 %copy-start.1 = (f32[256,1280]{1,0:T(8,128)}, f32[256,1280]{1,0:T(8,128)S(1)}, u32[]{:S(2)}) copy-start(f32[256,1280]{1,0:T(8,128)S(1)} %get-tuple-element.21) | copy-start | bytes 3932164
  20.0 12.8 %copy-start.7 = (s32[1,88]{1,0:T(1,128)S(1)}, s32[1,88]{1,0:T(1,128)}, u32[]{:S(2)}) copy-start(s32[1,88]{1,0:T(1,128)} %param.14) | copy-start | bytes 1060
  20.0 12.8 %copy-start.8 = (s32[1,88,1]{1,2,0:T(1,128)S(1)}, s32[1,88,1]{1,2,0:T(1,128)}, u32[]{:S(2)}) copy-start(s32[1,88,1]{1,2,0:T(1,128)} %param.13) | copy-start | bytes 1060
  20.0 5.3 %collective-permute-start = (bf16[256,1280]{1,0:T(8,128)(2,1)S(1)}, bf16[256,1280]{1,0:T(8,128)(2,1)S(1)}, u32[]{:S(2)}, u32[]{:S(2)}) collective-permute-start(bf16[256,1280]{1,0:T(8,128)(2,1)S(1)} %get-tuple-element.22), channel_id=1, source_target_pairs={{0,128},{128,0},{1,129},{129,1},{2,130},{130,2},{3,131},{131,3},{4... | collective-permute-start | bytes 1966088 | tf_op jit(solution)/shard_map/ppermute | solution.py:387
  25.3 1.0 copy-start.5
  26.3 16.2 %collective-permute-start.1 = (bf16[128,1280]{1,0:T(8,128)(2,1)}, bf16[128,1280]{1,0:T(8,128)(2,1)}, u32[]{:S(2)}, u32[]{:S(2)}) collective-permute-start(bf16[128,1280]{1,0:T(8,128)(2,1)} %add_convert_fusion.1), channel_id=1, source_target_pairs={{0,256},{256,0},{1,257},{257,1},{2,258},{258,2},{3,259},{259,3},{4... | collective-permute-start | bytes 983048 | tf_op jit(solution)/shard_map/ppermute | solution.py:429
  53.2 23.1 %collective-permute-start.5 = (bf16[32,176,128]{2,1,0:T(8,128)(2,1)}, bf16[32,176,128]{2,1,0:T(8,128)(2,1)}, u32[]{:S(2)}, u32[]{:S(2)}) collective-permute-start(bf16[32,176,128]{2,1,0:T(8,128)(2,1)} %all-to-all-done.rest_0_), channel_id=1, source_target_pairs={{0,32},{1,33},{2,34},{3,35},{4,36},{5,37},{6,38},{7,39},{8,40},{9,... | collective-permute-start | bytes 4325384 | tf_op jit(solution)/shard_map/ppermute | solution.py:377
  58.1 26.2 %all-to-all-start.1 = ((bf16[128,2,640]{2,1,0:T(2,128)(2,1)}), bf16[128,2,640]{2,1,0:T(2,128)(2,1)}, u32[]{:S(2)}, u32[]{:S(2)}) async-start(bf16[128,2,640]{2,1,0:T(2,128)(2,1)} %reshape.22), calls=%async_computation.1 | async-start | bytes 655360 | tf_op jit(solution)/shard_map/all_to_all | solution.py:395
  70.7 34.7 %collective-permute-start.6 = (bf16[32,176,128]{2,1,0:T(8,128)(2,1)}, bf16[32,176,128]{2,1,0:T(8,128)(2,1)}, u32[]{:S(2)}, u32[]{:S(2)}) collective-permute-start(bf16[32,176,128]{2,1,0:T(8,128)(2,1)} %all-to-all-done.rest_0_), channel_id=1, source_target_pairs={{0,96},{1,97},{2,98},{3,99},{4,100},{5,101},{6,102},{7,103},{8,104... | collective-permute-start | bytes 4325384 | tf_op jit(solution)/shard_map/ppermute | solution.py:377
  76.3 29.1 %collective-permute-start.7 = (bf16[32,176,128]{2,1,0:T(8,128)(2,1)}, bf16[32,176,128]{2,1,0:T(8,128)(2,1)}, u32[]{:S(2)}, u32[]{:S(2)}) collective-permute-start(bf16[32,176,128]{2,1,0:T(8,128)(2,1)} %collective-permute-done.5.rest_1_), channel_id=1, source_target_pairs={{0,32},{1,33},{2,34},{3,35},{4,36},{5,37},{6,38},{7,39},{8,40},{9,... | collective-permute-start | bytes 4325384 | tf_op jit(solution)/shard_map/ppermute | solution.py:377
  82.4 3.0 %collective-permute-start.2 = (s32[2,88]{1,0:T(2,128)S(1)}, s32[2,88]{1,0:T(2,128)S(1)}, u32[]{:S(2)}, u32[]{:S(2)}) collective-permute-start(s32[2,88]{1,0:T(2,128)S(1)} %pad_add_fusion.list_ref), channel_id=1, source_target_pairs={{0,128},{128,0},{1,129},{129,1},{2,130},{130,2},{3,131},{131,3},{4... | collective-permute-start | bytes 2120 | tf_op jit(solution)/shard_map/ppermute | solution.py:387
  85.4 1.0 copy-start.3
  94.9 8.2 %collective-permute-start.3 = (bf16[2816,128]{1,0:T(8,128)(2,1)}, bf16[2816,128]{1,0:T(8,128)(2,1)}, u32[]{:S(2)}, u32[]{:S(2)}) collective-permute-start(bf16[2816,128]{1,0:T(8,128)(2,1)} %get-tuple-element.27.low_ref), channel_id=1, source_target_pairs={{0,128},{128,0},{1,129},{129,1},{2,130},{130,2},{3,131},{131,3},{4... | collective-permute-start | bytes 2162696 | tf_op jit(solution)/shard_map/ppermute | solution.py:387
  100.9 4.4 %collective-permute-start.4 = (bf16[2816,128]{1,0:T(8,128)(2,1)}, bf16[2816,128]{1,0:T(8,128)(2,1)}, u32[]{:S(2)}, u32[]{:S(2)}) collective-permute-start(bf16[2816,128]{1,0:T(8,128)(2,1)} %get-tuple-element.28.high_ref), channel_id=1, source_target_pairs={{0,128},{128,0},{1,129},{129,1},{2,130},{130,2},{3,131},{131,3},{4... | collective-permute-start | bytes 2162696 | tf_op jit(solution)/shard_map/ppermute | solution.py:387
  112.7 7.6 %collective-permute-start.8 = (f32[8,11264]{1,0:T(8,128)S(1)}, f32[8,11264]{1,0:T(8,128)S(1)}, u32[]{:S(2)}, u32[]{:S(2)}) collective-permute-start(f32[8,11264]{1,0:T(8,128)S(1)} %get-tuple-element.32), channel_id=1, source_target_pairs={{0,128},{128,0},{1,129},{129,1},{2,130},{130,2},{3,131},{131,3},{4... | collective-permute-start | bytes 1081352 | tf_op jit(solution)/shard_map/ppermute | solution.py:387
  115.6 4.7 %copy-start.4 = (f32[1008,128]{1,0:T(8,128)S(1)}, f32[1008,128]{1,0:T(8,128)}, u32[]{:S(2)}) copy-start(f32[1008,128]{1,0:T(8,128)} %constant.59.clone.held_ref) | copy-start | bytes 1548292
  148.8 4.5 %collective-permute-start.9 = (bf16[256,256]{1,0:T(8,128)(2,1)S(1)}, bf16[256,256]{1,0:T(8,128)(2,1)S(1)}, u32[]{:S(2)}, u32[]{:S(2)}) collective-permute-start(bf16[256,256]{1,0:T(8,128)(2,1)S(1)} %bitcast.19), channel_id=1, source_target_pairs={{0,128},{128,0},{1,129},{129,1},{2,130},{130,2},{3,131},{131,3},{4... | collective-permute-start | bytes 393224 | tf_op jit(solution)/shard_map/ppermute | solution.py:387

commit v4 on v3

--- a/solution.py
+++ b/solution.py
@@ -118,9 +118,7 @@
     )(limit, at, legendre, spectral)
 
 
-def synth_kernel(coef_ref, pos_ref, held_ref, low_ref, high_ref, grid_ref, out_ref, tab_ref, sem):
-    fetch = pltpu.make_async_copy(held_ref, tab_ref, sem)
-    fetch.start()
+def synth_kernel(coef_ref, pos_ref, tab_ref, cols_ref, grid_ref, out_ref):
     dests, lanes = coef_ref.shape
     slots = dests * lanes // BLK
     coef = jnp.concatenate([coef_ref[:, pl.ds(i, BLK)] for i in range(0, lanes, BLK)], axis=0)
@@ -135,7 +133,6 @@
         return carry
 
     lax.fori_loop(0, NHI, place, 0, unroll=5)
-    fetch.wait()
     first = tab_ref[pl.ds(FIRST, 2 * BLK), :][:, :32].astype(BF16)
     second = jnp.concatenate(
         [tab_ref[pl.ds(SECOND, NBLK), :], tab_ref[pl.ds(SECOND + NBLK, NBLK), :]], axis=1
@@ -161,42 +158,37 @@
         return carry
 
     lax.fori_loop(0, 32, pair, 0, unroll=8)
-    rows = low_ref.shape[0]
-    low_ref[...] = out_ref[pl.ds(0, rows), :].astype(BF16)
-    high_ref[...] = out_ref[pl.ds(rows, rows), :].astype(BF16)
+    cols_ref[...] = out_ref[...].astype(BF16)
 
 
 def synthesize(coef, pos, tab):
     vm = pl.BlockSpec(memory_space=pltpu.VMEM)
     return pl.pallas_call(
         synth_kernel,
-        out_shape=(jax.ShapeDtypeStruct((NBLK * 32, BLK), BF16),) * 2,
-        in_specs=[vm, vm, pl.BlockSpec(memory_space=pl.ANY)],
-        out_specs=(vm, vm),
+        out_shape=jax.ShapeDtypeStruct((NBLK * 64, BLK), BF16),
+        in_specs=[vm] * 3,
+        out_specs=vm,
         scratch_shapes=[
             pltpu.VMEM((16 * BLK, BLK), F32),
             pltpu.VMEM((NBLK * 64, BLK), F32),
-            pltpu.VMEM((ROWS, BLK), F32),
-            pltpu.SemaphoreType.DMA,
         ],
         compiler_params=pltpu.CompilerParams(vmem_limit_bytes=14 * 1024 * 1024),
-        cost_estimate=pl.CostEstimate(flops=3_000_000_000, bytes_accessed=2_500_000, transcendentals=0),
+        cost_estimate=pl.CostEstimate(flops=1_000_000_000, bytes_accessed=1_000_000, transcendentals=0),
         name="synthesize",
     )(coef, pos, tab)
 
 
-def regime_blocks(at_ref, list_ref, low_ref, high_ref, w_ref, out_ref):
+def regime_blocks(at_ref, list_ref, cols_ref, w_ref, out_ref):
     core, me = at_ref[0], at_ref[1]
 
     for b in range(NBLK):
-        cols_ref, row = (low_ref, b) if b < NBLK // 2 else (high_ref, b - NBLK // 2)
         regime = list_ref[0, b]
         x, y, z = regime // 32, regime // 8 % 4, regime % 8
         minor = jnp.where(core == 0, y, x)
         away = (jnp.where(core == 0, x, y) - me + 4) % 4
         part = jnp.where(away == 0, 0, jnp.where(away == 3, 1, jnp.where(away == 1, 2, 3)))
         e = part * 32 + minor * 8 + z
-        cols = cols_ref[pl.ds(row * 64, 64), :]
+        cols = cols_ref[pl.ds(b * 64, 64), :]
         w = lambda lo, n: w_ref[e, pl.ds(lo, n), :]
         w_in = jnp.concatenate([w(0, 64), w(64, 64)], axis=1)
         w_out = jnp.concatenate([w(128, 16), w(144, 16)], axis=1)
@@ -208,7 +200,7 @@
         out_ref[:, pl.ds(b * BLK, BLK)] = out[:8] + list_ref[1, b].astype(F32) * out[8:]
 
 
-def first_network_kernel(counts, at_ref, list_ref, low_ref, high_ref, *rest):
+def first_network_kernel(counts, at_ref, list_ref, cols_ref, *rest):
     parts = rest[: len(counts)]
     out_ref, w_ref, sems = rest[len(counts) :]
     copies = []
@@ -219,7 +211,7 @@
         start += count
     for copy in copies:
         copy.wait()
-    regime_blocks(at_ref, list_ref, low_ref, high_ref, w_ref, out_ref)
+    regime_blocks(at_ref, list_ref, cols_ref, w_ref, out_ref)
 
 
 def first_network(at, listed, cols, parts):
@@ -233,7 +225,7 @@
             jax.ShapeDtypeStruct((8, NLON), F32),
             jax.ShapeDtypeStruct((sum(counts), HALF_ROWS, BLK), BF16),
         ),
-        in_specs=[sm, sm, vm, vm] + [hbm] * len(parts),
+        in_specs=[sm, sm, vm] + [hbm] * len(parts),
         out_specs=(vm, vm),
         scratch_shapes=[pltpu.SemaphoreType.DMA((len(parts),))],
         compiler_params=pltpu.CompilerParams(vmem_limit_bytes=14 * 1024 * 1024),
@@ -241,7 +233,7 @@
             flops=2_000_000_000, bytes_accessed=13_000_000, transcendentals=2_900_000
         ),
         name="first_network",
-    )(at, listed, *cols, *parts)
+    )(at, listed, cols, *parts)
 
 
 def second_network(at, listed, cols, weights):
@@ -250,21 +242,19 @@
     return pl.pallas_call(
         regime_blocks,
         out_shape=jax.ShapeDtypeStruct((8, NLON), F32),
-        in_specs=[sm, sm, vm, vm, vm],
+        in_specs=[sm, sm, vm, vm],
         out_specs=vm,
         compiler_params=pltpu.CompilerParams(vmem_limit_bytes=10 * 1024 * 1024),
         cost_estimate=pl.CostEstimate(
             flops=2_000_000_000, bytes_accessed=8_000_000, transcendentals=2_900_000
         ),
         name="second_network",
-    )(at, listed, *cols, weights)
+    )(at, listed, cols, weights)
 
 
 def analysis_kernel(
-    gauss_ref, own_ref, got_ref, pos_ref, held_ref, heat_ref, pay_ref, hs_ref, r_ref, tab_ref, sem
+    gauss_ref, own_ref, got_ref, pos_ref, tab_ref, heat_ref, pay_ref, hs_ref, r_ref
 ):
-    fetch = pltpu.make_async_copy(held_ref, tab_ref, sem)
-    fetch.start()
     for b in range(NBLK):
         lanes = pl.ds(b * BLK, BLK)
         heat = (own_ref[:, lanes] + got_ref[:, lanes]).astype(BF16)
@@ -272,7 +262,6 @@
         hs_ref[pl.ds(b, 8, stride=BROWS), :] = heat.astype(F32)
     for lev in range(8):
         hs_ref[pl.ds(lev * BROWS + NBLK, BROWS - NBLK), :] = jnp.zeros((BROWS - NBLK, BLK), F32)
-    fetch.wait()
     inner = tab_ref[pl.ds(INNER, 2 * BLK), :][:, :BROWS].astype(BF16)
     last = jnp.concatenate([tab_ref[pl.ds(LAST, 32), :], tab_ref[pl.ds(LAST + 32, 32), :]], axis=1)
     last = last.astype(BF16)
@@ -314,13 +303,11 @@
             jax.ShapeDtypeStruct((8, NLON), BF16),
             jax.ShapeDtypeStruct((2 * pos_local.shape[1], 2 * BLK), BF16),
         ),
-        in_specs=[sm] + [vm] * 3 + [pl.BlockSpec(memory_space=pl.ANY)],
+        in_specs=[sm] + [vm] * 4,
         out_specs=(vm, vm),
         scratch_shapes=[
             pltpu.VMEM((8 * BROWS, BLK), F32),
             pltpu.VMEM((32 * 8, BLK), F32),
-            pltpu.VMEM((ROWS, BLK), F32),
-            pltpu.SemaphoreType.DMA,
         ],
         compiler_params=pltpu.CompilerParams(vmem_limit_bytes=8 * 1024 * 1024),
         cost_estimate=pl.CostEstimate(flops=1_000_000_000, bytes_accessed=1_500_000, transcendentals=0),
@@ -428,7 +415,8 @@
     far = (ours[:rows] + got[:rows].astype(F32)).astype(BF16)
     far = lax.ppermute(far, "y_hi", [(0, 1), (1, 0)])
     near = ours[rows:] + got[rows:].astype(F32) + far.astype(F32)
-    near = near.astype(BF16).reshape(rows, 2, lanes // 2)
+    near = near.astype(BF16)
+    near = jnp.stack([near[:, : lanes // 2], near[:, lanes // 2 :]], axis=1)
     listed = jnp.stack([regime[0, :, 0], daylight[0]])
     place = wavenumbers // NBLK * BLK + wavenumbers % NBLK
     place = place.reshape(-1, slots).T
@@ -440,12 +428,12 @@
     two = moved(one, 1)
 
     cols = synthesize(coef, line, tab)
-    theirs = tuple(swap(part) for part in cols)
+    theirs = swap(cols)
 
     me = jnp.where(core == 0, lax.axis_index("x"), lax.axis_index("y_lo"))
     at = jnp.stack([core, me.astype(jnp.int32)])
-    sib, weights = first_network(at, sibling, theirs, (plane, one, three, two))
-    own = second_network(at, listed, cols, weights)
+    own, weights = first_network(at, listed, cols, (plane, one, three, two))
+    sib = second_network(at, sibling, theirs, weights)
     heat, pay = analyze(gauss_weight, own, swap(sib), place, tab)
     ours, theirs = from_latitudes(pay)
     return (heat[None], forward_legendre(legendre, ours, theirs, limit, core[None]))

time: 156 us -> 154 us (0.987)
  starting transfers between devices: 66.1 us -> 62.5 us
    ppermute x3, starting transfers between devices: 14.1 us -> 8.31 us  [moved(): return lax.ppermute(value, AXES, pairs)]
    ppermute x6 -> x5, starting transfers between devices: 19.2 us -> 21.4 us  [swap(): return lax.ppermute(value, 'core', [(0, 1), (1, 0)])]
    optimization_barrier x0 -> x1, local copies, waits for them, and re-layouts: none -> 2.03 us  [body(): lax.optimization_barrier((plane, near, listed, place, line))]
    all_to_all x1, waiting for transfers between devices: 0.01 us -> 1.9 us  [exchange(): return lax.all_to_all(value, axes, 0, 0, tiled=True)]
    ppermute x3, waiting for transfers between devices: 2.45 us -> 0.62 us  [moved(): return lax.ppermute(value, AXES, pairs)]
    reshape x1 -> x0, local copies, waits for them, and re-layouts: 1.78 us -> none  [body(): near = near.astype(BF16).reshape(rows, 2, lanes // 2)]
    all_to_all x1, waiting for transfers between devices: 6.81 us -> 8.51 us  [gather_plane(): lax.all_to_all(copies, AXES, 0, 0, axis_index_groups=sheets(), tiled=True)]
    ppermute x6 -> x5, waiting for transfers between devices: 5.16 us -> 3.67 us  [swap(): return lax.ppermute(value, 'core', [(0, 1), (1, 0)])]
  transfers between devices with their start and end apart: 12 -> 11, of which waited for: 8 -> 7; matrix products, arithmetic and copies ran while one was open for 4% -> 4% of each run, Pallas kernels for 10% -> 11%
where the time goes in v4:
time: 154 us; the launch traced here: 153 us
  starting transfers between devices  62.5 us (41%)
  Pallas kernels  28.5 us (19%)
  blocking collectives  27.3 us (18%)
  waiting for transfers between devices  24.3 us (16%)
  local copies, waits for them, and re-layouts  5.67 us (4%)
  other arithmetic  3.24 us (2%)
  between operations  1.55 us (1%)
    all_to_all x1, blocking collectives, exchange(): return lax.all_to_all(value, axes, 0, 0, tiled=True)  27.3 us
    ppermute x5, starting transfers between devices, swap(): return lax.ppermute(value, 'core', [(0, 1), (1, 0)])  21.4 us
    all_to_all x1, starting transfers between devices, gather_plane(): lax.all_to_all(copies, AXES, 0, 0, axis_index_groups=sheets(), tiled=True)  14 us
    all_to_all x1, starting transfers between devices, exchange(): return lax.all_to_all(value, axes, 0, 0, tiled=True)  12.6 us
    ppermute x1, waiting for transfers between devices, body(): far = lax.ppermute(far, 'y_hi', [(0, 1), (1, 0)])  9.62 us
    all_to_all x1, waiting for transfers between devices, gather_plane(): lax.all_to_all(copies, AXES, 0, 0, axis_index_groups=sheets(), tiled=True)  8.51 us
    ppermute x3, starting transfers between devices, moved(): return lax.ppermute(value, AXES, pairs)  8.31 us
    pallas_call x1, Pallas kernels, synthesize(): pl.pallas_call(synth_kernel, out_shape=jax.ShapeDtypeStruct((NBLK * 64, B...  7.96 us
  transfers between devices with their start and end apart: 11, of which 7 were waited for; matrix products, arithmetic and copies ran while one was open for 4% of the time, Pallas kernels for 11%

profile of v4, /device:TPU:1, one launch (start us, length us, event | category | flops | bytes accessed | tf_op | source)
XLA Modules:
  0.0 153.0 jit_solution(10900393692185318804)
XLA Ops:
  0.6 2.2 %pack_weights.1 = bf16[32,176,128]{2,1,0:T(8,128)(2,1)} custom-call(s32[1]{0:T(128)} %bitcast.core_ref, bf16[1,64,512]{2,1,0:T(8,128)(2,1)} %w_in_ref.1, bf16[1,512]{1,0:T(2,128)(2,1)} %b_in_ref.1, bf16[1,16,512]{2,1,0:T(8,128)(2,1)} %w_out_ref.1), custom_call_target="tpu_custom_call" | custom-call | tf_op jit(solution)/shard_map/pack_weights/pallas_call | solution.py:74
  2.9 14.0 %all-to-all-start = ((bf16[32,176,128]{2,1,0:T(8,128)(2,1)}), bf16[32,176,128]{2,1,0:T(8,128)(2,1)}, u32[]{:S(2)}, u32[]{:S(2)}) async-start(bf16[32,176,128]{2,1,0:T(8,128)(2,1)} %pack_weights.1), calls=%async_computation | async-start | bytes 2883584 | tf_op jit(solution)/shard_map/all_to_all | solution.py:386
  18.2 1.8 %inverse_legendre.1 = (bf16[256,1280]{1,0:T(8,128)(2,1)S(1)}, f32[256,1280]{1,0:T(8,128)S(1)}) custom-call(s32[10]{0:T(128)S(1)} %subtract_subtract_fusion.limit_ref, s32[2]{0:T(128)S(1)} %pad_add_fusion.2.at_ref, bf16[10,320,512]{2,1,0:T(8,128)(2,1)S(1)} %copy-done, bf16[10,320,128]{2,1,0:T(8,128)(2,1)S(1)} %bitcast.22), custom_call_target="tpu_custom_call" | custom-call | flops 419430400 | bytes 6000000 | tf_op jit(solution)/shard_map/inverse_legendre/pallas_call | solution.py:108
  20.0 3.6 %collective-permute-start = (bf16[256,1280]{1,0:T(8,128)(2,1)S(1)}, bf16[256,1280]{1,0:T(8,128)(2,1)S(1)}, u32[]{:S(2)}, u32[]{:S(2)}) collective-permute-start(bf16[256,1280]{1,0:T(8,128)(2,1)S(1)} %get-tuple-element.20), channel_id=1, source_target_pairs={{0,128},{128,0},{1,129},{129,1},{2,130},{130,2},{3,131},{131,3},{4... | collective-permute-start | bytes 1966088 | tf_op jit(solution)/shard_map/ppermute | solution.py:374
  23.6 1.7 %collective-permute-done = bf16[256,1280]{1,0:T(8,128)(2,1)S(1)} collective-permute-done((bf16[256,1280]{1,0:T(8,128)(2,1)S(1)}, bf16[256,1280]{1,0:T(8,128)(2,1)S(1)}, u32[]{:S(2)}, u32[]{:S(2)}) %collective-permute-start) | collective-permute-done | bytes 655392 | tf_op jit(solution)/shard_map/ppermute | solution.py:374
  26.3 6.3 %collective-permute-start.1 = (bf16[128,1280]{1,0:T(8,128)(2,1)}, bf16[128,1280]{1,0:T(8,128)(2,1)}, u32[]{:S(2)}, u32[]{:S(2)}) collective-permute-start(bf16[128,1280]{1,0:T(8,128)(2,1)} %add_convert_fusion.1), channel_id=1, source_target_pairs={{0,256},{256,0},{1,257},{257,1},{2,258},{258,2},{3,259},{259,3},{4... | collective-permute-start | bytes 983048 | tf_op jit(solution)/shard_map/ppermute | solution.py:416
  32.9 9.6 %collective-permute-done.1 = bf16[128,1280]{1,0:T(8,128)(2,1)} collective-permute-done((bf16[128,1280]{1,0:T(8,128)(2,1)}, bf16[128,1280]{1,0:T(8,128)(2,1)}, u32[]{:S(2)}, u32[]{:S(2)}) %collective-permute-start.1) | collective-permute-done | bytes 327712 | tf_op jit(solution)/shard_map/ppermute | solution.py:416
  44.7 8.5 %all-to-all-done.rest_0_ = bf16[32,176,128]{2,1,0:T(8,128)(2,1)} async-done(((bf16[32,176,128]{2,1,0:T(8,128)(2,1)}), bf16[32,176,128]{2,1,0:T(8,128)(2,1)}, u32[]{:S(2)}, u32[]{:S(2)}) %all-to-all-start) | async-done | bytes 1441824 | tf_op jit(solution)/shard_map/all_to_all | solution.py:386
  53.2 3.2 %collective-permute-start.3 = (bf16[32,176,128]{2,1,0:T(8,128)(2,1)}, bf16[32,176,128]{2,1,0:T(8,128)(2,1)}, u32[]{:S(2)}, u32[]{:S(2)}) collective-permute-start(bf16[32,176,128]{2,1,0:T(8,128)(2,1)} %all-to-all-done.rest_0_), channel_id=1, source_target_pairs={{0,32},{1,33},{2,34},{3,35},{4,36},{5,37},{6,38},{7,39},{8,40},{9,... | collective-permute-start | bytes 4325384 | tf_op jit(solution)/shard_map/ppermute | solution.py:364
  56.4 2.0 %copy.16 = bf16[128,2,640]{2,1,0:T(2,128)(2,1)} copy(bf16[128,2,640]{2,0,1:T(8,128)(2,1)} %pad_maximum_fusion) | data formatting | bytes 655360 | tf_op jit(solution)/shard_map/optimization_barrier | solution.py:424
  58.4 12.6 %all-to-all-start.1 = ((bf16[128,2,640]{2,1,0:T(2,128)(2,1)}), bf16[128,2,640]{2,1,0:T(2,128)(2,1)}, u32[]{:S(2)}, u32[]{:S(2)}) async-start(bf16[128,2,640]{2,1,0:T(2,128)(2,1)} %copy.16), calls=%async_computation.1 | async-start | bytes 655360 | tf_op jit(solution)/shard_map/all_to_all | solution.py:382
  71.0 3.1 %collective-permute-start.4 = (bf16[32,176,128]{2,1,0:T(8,128)(2,1)}, bf16[32,176,128]{2,1,0:T(8,128)(2,1)}, u32[]{:S(2)}, u32[]{:S(2)}) collective-permute-start(bf16[32,176,128]{2,1,0:T(8,128)(2,1)} %all-to-all-done.rest_0_), channel_id=1, source_target_pairs={{0,96},{1,97},{2,98},{3,99},{4,100},{5,101},{6,102},{7,103},{8,104... | collective-permute-start | bytes 4325384 | tf_op jit(solution)/shard_map/ppermute | solution.py:364
  74.7 2.0 %collective-permute-start.5 = (bf16[32,176,128]{2,1,0:T(8,128)(2,1)}, bf16[32,176,128]{2,1,0:T(8,128)(2,1)}, u32[]{:S(2)}, u32[]{:S(2)}) collective-permute-start(bf16[32,176,128]{2,1,0:T(8,128)(2,1)} %collective-permute-done.3.rest_1_), channel_id=1, source_target_pairs={{0,32},{1,33},{2,34},{3,35},{4,36},{5,37},{6,38},{7,39},{8,40},{9,... | collective-permute-start | bytes 4325384 | tf_op jit(solution)/shard_map/ppermute | solution.py:364
  76.7 5.0 %collective-permute-start.2 = (s32[2,88]{1,0:T(2,128)S(1)}, s32[2,88]{1,0:T(2,128)S(1)}, u32[]{:S(2)}, u32[]{:S(2)}) collective-permute-start(s32[2,88]{1,0:T(2,128)S(1)} %pad_add_fusion.list_ref), channel_id=1, source_target_pairs={{0,128},{128,0},{1,129},{129,1},{2,130},{130,2},{3,131},{131,3},{4... | collective-permute-start | bytes 2120 | tf_op jit(solution)/shard_map/ppermute | solution.py:374
  81.7 1.9 %all-to-all-done.1 = bf16[128,2,640]{2,1,0:T(2,128)(2,1)} async-done(((bf16[128,2,640]{2,1,0:T(2,128)(2,1)}), bf16[128,2,640]{2,1,0:T(2,128)(2,1)}, u32[]{:S(2)}, u32[]{:S(2)}) %all-to-all-start.1) | async-done | bytes 327712 | tf_op jit(solution)/shard_map/all_to_all | solution.py:382
  85.7 8.0 %synthesize.1.cols_ref = bf16[5632,128]{1,0:T(8,128)(2,1)} custom-call(bf16[128,1280]{1,0:T(8,128)(2,1)S(1)} %bitcast.25, s32[1,1280]{1,0:T(1,128)S(1)} %bitcast.28, f32[1008,128]{1,0:T(8,128)S(1)} %copy-done.3), custom_call_target="tpu_custom_call" | custom-call | flops 1000000000 | bytes 1000000 | tf_op jit(solution)/shard_map/synthesize/pallas_call | solution.py:166
  93.6 7.3 %collective-permute-start.6 = (bf16[5632,128]{1,0:T(8,128)(2,1)}, bf16[5632,128]{1,0:T(8,128)(2,1)}, u32[]{:S(2)}, u32[]{:S(2)}) collective-permute-start(bf16[5632,128]{1,0:T(8,128)(2,1)} %synthesize.1.cols_ref), channel_id=1, source_target_pairs={{0,128},{128,0},{1,129},{129,1},{2,130},{130,2},{3,131},{131,3},{4... | collective-permute-start | bytes 4325384 | tf_op jit(solution)/shard_map/ppermute | solution.py:374
  101.0 7.4 %first_network.1 = (f32[8,11264]{1,0:T(8,128)S(1)}, bf16[128,176,128]{2,1,0:T(8,128)(2,1)S(1)}) custom-call(s32[2]{0:T(128)S(1)} %pad_add_fusion.1.at_ref, s32[2,88]{1,0:T(2,128)S(1)} %pad_add_fusion.list_ref, bf16[5632,128]{1,0:T(8,128)(2,1)} %synthesize.1.cols_ref, bf16[32,176,128]{2,1,0:T(8,128)(2,1)} %all-to-all-done.rest_0_, ...), custom_call_target="tpu_custom_call" | custom-call | flops 2000000000 | bytes 13000000 | tf_op jit(solution)/shard_map/first_network/pallas_call | solution.py:222
  108.4 4.7 %second_network.1 = f32[8,11264]{1,0:T(8,128)S(1)} custom-call(s32[2]{0:T(128)S(1)} %pad_add_fusion.1.at_ref, s32[2,88]{1,0:T(2,128)S(1)} %collective-permute-done.2.list_ref, bf16[5632,128]{1,0:T(8,128)(2,1)} %collective-permute-done.6.cols_ref, bf16[128,176,128]{2,1,0:T(8,128)(2,1)S(1)} %get-tuple-element.28.w_ref), custom_call_target="tpu_custom_call" | custom-call | flops 2000000000 | bytes 8000000 | tf_op jit(solution)/shard_map/second_network/pallas_call | solution.py:242
  113.1 1.9 %collective-permute-start.7 = (f32[8,11264]{1,0:T(8,128)S(1)}, f32[8,11264]{1,0:T(8,128)S(1)}, u32[]{:S(2)}, u32[]{:S(2)}) collective-permute-start(f32[8,11264]{1,0:T(8,128)S(1)} %second_network.1), channel_id=1, source_target_pairs={{0,128},{128,0},{1,129},{129,1},{2,130},{130,2},{3,131},{131,3},{4... | collective-permute-start | bytes 1081352 | tf_op jit(solution)/shard_map/ppermute | solution.py:374
  116.7 2.2 %analyze.1 = (bf16[8,11264]{1,0:T(8,128)(2,1)}, bf16[256,256]{1,0:T(8,128)(2,1)S(1)}) custom-call(f32[1]{0:T(128)S(6)} %copy.24.gauss_ref, f32[8,11264]{1,0:T(8,128)S(1)} %get-tuple-element.26.own_ref, f32[8,11264]{1,0:T(8,128)S(1)} %collective-permute-done.7.got_ref, s32[10,128]{1,0:T(8,128)S(1)} %bitcast.27, f32[1008,128]{1,0:T(8,128)S(1)} %copy-done.4), custom_call_target="tpu_custom_call" | custom-call | flops 1000000000 | bytes 1500000 | tf_op jit(solution)/shard_map/analyze/pallas_call | solution.py:300
  118.9 27.3 %all_to_all.15 = bf16[256,2,128]{2,1,0:T(2,128)(2,1)S(1)} all-to-all(bf16[256,2,128]{2,1,0:T(2,128)(2,1)S(1)} %reshape.22), channel_id=1, replica_groups=mesh['y_hi'=2,'core'=2,'x'=4,'y_lo'=4,'z'=8] {'y_hi','x','y_lo','z'}, dimensions={0} | all-to-all | bytes 262144 | tf_op jit(solution)/shard_map/all_to_all | solution.py:382
  146.2 3.6 %collective-permute-start.8 = (bf16[256,256]{1,0:T(8,128)(2,1)S(1)}, bf16[256,256]{1,0:T(8,128)(2,1)S(1)}, u32[]{:S(2)}, u32[]{:S(2)}) collective-permute-start(bf16[256,256]{1,0:T(8,128)(2,1)S(1)} %bitcast.23), channel_id=1, source_target_pairs={{0,128},{128,0},{1,129},{129,1},{2,130},{130,2},{3,131},{131,3},{4... | collective-permute-start | bytes 393224 | tf_op jit(solution)/shard_map/ppermute | solution.py:374
  150.8 2.2 %forward_legendre.1 = bf16[10,16,320]{2,1,0:T(8,128)(2,1)} custom-call(s32[10]{0:T(128)S(1)} %subtract_subtract_fusion.limit_ref, s32[1]{0:T(128)} %bitcast.core_ref, bf16[10,320,512]{2,1,0:T(8,128)(2,1)S(1)} %copy-done, bf16[256,256]{1,0:T(8,128)(2,1)S(1)} %bitcast.24, bf16[256,256]{1,0:T(8,128)(2,1)S(1)} %collective-permute-done.8.theirs_ref), custom_call_target="tpu_custom_call" | custom-call | flops 52428800 | bytes 4000000 | tf_op jit(solution)/shard_map/forward_legendre/pallas_call | solution.py:337
  (40 shorter events, 9.5 us)
Async XLA Ops:
  0.6 16.4 %copy-start = (bf16[10,320,512]{2,1,0:T(8,128)(2,1)S(1)}, bf16[10,320,512]{2,1,0:T(8,128)(2,1)}, u32[]{:S(2)}) copy-start(bf16[10,320,512]{2,1,0:T(8,128)(2,1)} %table_ref.1) | copy-start | bytes 9830404
  2.9 14.1 %copy-start.6 = (s32[1280]{0:T(1024)S(1)}, s32[1280]{0:T(1024)}, u32[]{:S(2)}) copy-start(s32[1280]{0:T(1024)} %param.12) | copy-start | bytes 15364
  2.9 50.3 %all-to-all-start = ((bf16[32,176,128]{2,1,0:T(8,128)(2,1)}), bf16[32,176,128]{2,1,0:T(8,128)(2,1)}, u32[]{:S(2)}, u32[]{:S(2)}) async-start(bf16[32,176,128]{2,1,0:T(8,128)(2,1)} %pack_weights.1), calls=%async_computation | async-start | bytes 2883584 | tf_op jit(solution)/shard_map/all_to_all | solution.py:386
  17.0 1.1 copy-start.2
  20.0 5.3 %copy-start.1 = (f32[256,1280]{1,0:T(8,128)}, f32[256,1280]{1,0:T(8,128)S(1)}, u32[]{:S(2)}) copy-start(f32[256,1280]{1,0:T(8,128)S(1)} %get-tuple-element.19) | copy-start | bytes 3932164
  20.0 12.8 %copy-start.7 = (s32[1,88]{1,0:T(1,128)S(1)}, s32[1,88]{1,0:T(1,128)}, u32[]{:S(2)}) copy-start(s32[1,88]{1,0:T(1,128)} %param.14) | copy-start | bytes 1060
  20.0 12.8 %copy-start.8 = (s32[1,88,1]{1,2,0:T(1,128)S(1)}, s32[1,88,1]{1,2,0:T(1,128)}, u32[]{:S(2)}) copy-start(s32[1,88,1]{1,2,0:T(1,128)} %param.13) | copy-start | bytes 1060
  20.0 5.3 %collective-permute-start = (bf16[256,1280]{1,0:T(8,128)(2,1)S(1)}, bf16[256,1280]{1,0:T(8,128)(2,1)S(1)}, u32[]{:S(2)}, u32[]{:S(2)}) collective-permute-start(bf16[256,1280]{1,0:T(8,128)(2,1)S(1)} %get-tuple-element.20), channel_id=1, source_target_pairs={{0,128},{128,0},{1,129},{129,1},{2,130},{130,2},{3,131},{131,3},{4... | collective-permute-start | bytes 1966088 | tf_op jit(solution)/shard_map/ppermute | solution.py:374
  25.3 1.0 copy-start.5
  26.3 16.2 %collective-permute-start.1 = (bf16[128,1280]{1,0:T(8,128)(2,1)}, bf16[128,1280]{1,0:T(8,128)(2,1)}, u32[]{:S(2)}, u32[]{:S(2)}) collective-permute-start(bf16[128,1280]{1,0:T(8,128)(2,1)} %add_convert_fusion.1), channel_id=1, source_target_pairs={{0,256},{256,0},{1,257},{257,1},{2,258},{258,2},{3,259},{259,3},{4... | collective-permute-start | bytes 983048 | tf_op jit(solution)/shard_map/ppermute | solution.py:416
  53.2 21.6 %collective-permute-start.3 = (bf16[32,176,128]{2,1,0:T(8,128)(2,1)}, bf16[32,176,128]{2,1,0:T(8,128)(2,1)}, u32[]{:S(2)}, u32[]{:S(2)}) collective-permute-start(bf16[32,176,128]{2,1,0:T(8,128)(2,1)} %all-to-all-done.rest_0_), channel_id=1, source_target_pairs={{0,32},{1,33},{2,34},{3,35},{4,36},{5,37},{6,38},{7,39},{8,40},{9,... | collective-permute-start | bytes 4325384 | tf_op jit(solution)/shard_map/ppermute | solution.py:364
  58.4 25.2 %all-to-all-start.1 = ((bf16[128,2,640]{2,1,0:T(2,128)(2,1)}), bf16[128,2,640]{2,1,0:T(2,128)(2,1)}, u32[]{:S(2)}, u32[]{:S(2)}) async-start(bf16[128,2,640]{2,1,0:T(2,128)(2,1)} %copy.16), calls=%async_computation.1 | async-start | bytes 655360 | tf_op jit(solution)/shard_map/all_to_all | solution.py:382
  71.0 30.0 %collective-permute-start.4 = (bf16[32,176,128]{2,1,0:T(8,128)(2,1)}, bf16[32,176,128]{2,1,0:T(8,128)(2,1)}, u32[]{:S(2)}, u32[]{:S(2)}) collective-permute-start(bf16[32,176,128]{2,1,0:T(8,128)(2,1)} %all-to-all-done.rest_0_), channel_id=1, source_target_pairs={{0,96},{1,97},{2,98},{3,99},{4,100},{5,101},{6,102},{7,103},{8,104... | collective-permute-start | bytes 4325384 | tf_op jit(solution)/shard_map/ppermute | solution.py:364
  74.7 26.2 %collective-permute-start.5 = (bf16[32,176,128]{2,1,0:T(8,128)(2,1)}, bf16[32,176,128]{2,1,0:T(8,128)(2,1)}, u32[]{:S(2)}, u32[]{:S(2)}) collective-permute-start(bf16[32,176,128]{2,1,0:T(8,128)(2,1)} %collective-permute-done.3.rest_1_), channel_id=1, source_target_pairs={{0,32},{1,33},{2,34},{3,35},{4,36},{5,37},{6,38},{7,39},{8,40},{9,... | collective-permute-start | bytes 4325384 | tf_op jit(solution)/shard_map/ppermute | solution.py:364
  76.7 7.9 %collective-permute-start.2 = (s32[2,88]{1,0:T(2,128)S(1)}, s32[2,88]{1,0:T(2,128)S(1)}, u32[]{:S(2)}, u32[]{:S(2)}) collective-permute-start(s32[2,88]{1,0:T(2,128)S(1)} %pad_add_fusion.list_ref), channel_id=1, source_target_pairs={{0,128},{128,0},{1,129},{129,1},{2,130},{130,2},{3,131},{131,3},{4... | collective-permute-start | bytes 2120 | tf_op jit(solution)/shard_map/ppermute | solution.py:374
  84.6 1.0 copy-start.3
  93.6 14.7 %collective-permute-start.6 = (bf16[5632,128]{1,0:T(8,128)(2,1)}, bf16[5632,128]{1,0:T(8,128)(2,1)}, u32[]{:S(2)}, u32[]{:S(2)}) collective-permute-start(bf16[5632,128]{1,0:T(8,128)(2,1)} %synthesize.1.cols_ref), channel_id=1, source_target_pairs={{0,128},{128,0},{1,129},{129,1},{2,130},{130,2},{3,131},{131,3},{4... | collective-permute-start | bytes 4325384 | tf_op jit(solution)/shard_map/ppermute | solution.py:374
  108.4 8.3 %copy-start.4 = (f32[1008,128]{1,0:T(8,128)S(1)}, f32[1008,128]{1,0:T(8,128)}, u32[]{:S(2)}) copy-start(f32[1008,128]{1,0:T(8,128)} %constant.59.clone.tab_ref) | copy-start | bytes 1548292
  113.1 3.6 %collective-permute-start.7 = (f32[8,11264]{1,0:T(8,128)S(1)}, f32[8,11264]{1,0:T(8,128)S(1)}, u32[]{:S(2)}, u32[]{:S(2)}) collective-permute-start(f32[8,11264]{1,0:T(8,128)S(1)} %second_network.1), channel_id=1, source_target_pairs={{0,128},{128,0},{1,129},{129,1},{2,130},{130,2},{3,131},{131,3},{4... | collective-permute-start | bytes 1081352 | tf_op jit(solution)/shard_map/ppermute | solution.py:374
  146.2 4.6 %collective-permute-start.8 = (bf16[256,256]{1,0:T(8,128)(2,1)S(1)}, bf16[256,256]{1,0:T(8,128)(2,1)S(1)}, u32[]{:S(2)}, u32[]{:S(2)}) collective-permute-start(bf16[256,256]{1,0:T(8,128)(2,1)S(1)} %bitcast.23), channel_id=1, source_target_pairs={{0,128},{128,0},{1,129},{129,1},{2,130},{130,2},{3,131},{131,3},{4... | collective-permute-start | bytes 393224 | tf_op jit(solution)/shard_map/ppermute | solution.py:374

commit v5 on v4

--- a/solution.py
+++ b/solution.py
@@ -158,7 +158,7 @@
         return carry
 
     lax.fori_loop(0, 32, pair, 0, unroll=8)
-    cols_ref[...] = out_ref[...].astype(BF16)
+    cols_ref[...] = out_ref[pl.ds(0, NBLK * 64), :].astype(BF16)
 
 
 def synthesize(coef, pos, tab):
@@ -169,8 +169,8 @@
         in_specs=[vm] * 3,
         out_specs=vm,
         scratch_shapes=[
-            pltpu.VMEM((16 * BLK, BLK), F32),
-            pltpu.VMEM((NBLK * 64, BLK), F32),
+            pltpu.VMEM((17 * BLK, BLK), F32),
+            pltpu.VMEM((NBLK * 64 + 64, BLK), F32),
         ],
         compiler_params=pltpu.CompilerParams(vmem_limit_bytes=14 * 1024 * 1024),
         cost_estimate=pl.CostEstimate(flops=1_000_000_000, bytes_accessed=1_000_000, transcendentals=0),
@@ -306,8 +306,8 @@
         in_specs=[sm] + [vm] * 4,
         out_specs=(vm, vm),
         scratch_shapes=[
-            pltpu.VMEM((8 * BROWS, BLK), F32),
-            pltpu.VMEM((32 * 8, BLK), F32),
+            pltpu.VMEM((9 * BROWS, BLK), F32),
+            pltpu.VMEM((33 * 8, BLK), F32),
         ],
         compiler_params=pltpu.CompilerParams(vmem_limit_bytes=8 * 1024 * 1024),
         cost_estimate=pl.CostEstimate(flops=1_000_000_000, bytes_accessed=1_500_000, transcendentals=0),
@@ -388,7 +388,7 @@
 
 def from_latitudes(pay):
     rows, lanes = pay.shape
-    pay = pay.reshape(rows, 2, lanes // 2)
+    pay = jnp.stack([pay[:, : lanes // 2], pay[:, lanes // 2 :]], axis=1)
     ours = exchange(pay, ("y_hi", "x", "y_lo", "z")).reshape(rows, lanes)
     return ours, swap(ours)
 

time: 154 us -> 154 us (level)
  no operation moved by 1% of the time
where the time goes in v5:
time: 154 us; the launch traced here: 153 us
  starting transfers between devices  62.5 us (41%)
  Pallas kernels  28.5 us (19%)
  blocking collectives  27.3 us (18%)
  waiting for transfers between devices  24.3 us (16%)
  local copies, waits for them, and re-layouts  5.79 us (4%)
  other arithmetic  3.26 us (2%)
  between operations  1.57 us (1%)
    all_to_all x1, blocking collectives, exchange(): return lax.all_to_all(value, axes, 0, 0, tiled=True)  27.3 us
    ppermute x5, starting transfers between devices, swap(): return lax.ppermute(value, 'core', [(0, 1), (1, 0)])  21.4 us
    all_to_all x1, starting transfers between devices, gather_plane(): lax.all_to_all(copies, AXES, 0, 0, axis_index_groups=sheets(), tiled=True)  14 us
    all_to_all x1, starting transfers between devices, exchange(): return lax.all_to_all(value, axes, 0, 0, tiled=True)  12.6 us
    ppermute x1, waiting for transfers between devices, body(): far = lax.ppermute(far, 'y_hi', [(0, 1), (1, 0)])  9.61 us
    all_to_all x1, waiting for transfers between devices, gather_plane(): lax.all_to_all(copies, AXES, 0, 0, axis_index_groups=sheets(), tiled=True)  8.52 us
    ppermute x3, starting transfers between devices, moved(): return lax.ppermute(value, AXES, pairs)  8.3 us
    pallas_call x1, Pallas kernels, synthesize(): pl.pallas_call(synth_kernel, out_shape=jax.ShapeDtypeStruct((NBLK * 64, B...  7.96 us
  transfers between devices with their start and end apart: 11, of which 7 were waited for; matrix products, arithmetic and copies ran while one was open for 4% of the time, Pallas kernels for 11%

profile of v5, /device:TPU:1, one launch (start us, length us, event | category | flops | bytes accessed | tf_op | source)
XLA Modules:
  0.0 153.2 jit_solution(5457198630216733164)
XLA Ops:
  0.6 2.2 %pack_weights.1 = bf16[32,176,128]{2,1,0:T(8,128)(2,1)} custom-call(s32[1]{0:T(128)} %bitcast.core_ref, bf16[1,64,512]{2,1,0:T(8,128)(2,1)} %w_in_ref.1, bf16[1,512]{1,0:T(2,128)(2,1)} %b_in_ref.1, bf16[1,16,512]{2,1,0:T(8,128)(2,1)} %w_out_ref.1), custom_call_target="tpu_custom_call" | custom-call | tf_op jit(solution)/shard_map/pack_weights/pallas_call | solution.py:74
  2.9 14.0 %all-to-all-start = ((bf16[32,176,128]{2,1,0:T(8,128)(2,1)}), bf16[32,176,128]{2,1,0:T(8,128)(2,1)}, u32[]{:S(2)}, u32[]{:S(2)}) async-start(bf16[32,176,128]{2,1,0:T(8,128)(2,1)} %pack_weights.1), calls=%async_computation | async-start | bytes 2883584 | tf_op jit(solution)/shard_map/all_to_all | solution.py:386
  18.2 1.8 %inverse_legendre.1 = (bf16[256,1280]{1,0:T(8,128)(2,1)S(1)}, f32[256,1280]{1,0:T(8,128)S(1)}) custom-call(s32[10]{0:T(128)S(1)} %subtract_subtract_fusion.limit_ref, s32[2]{0:T(128)S(1)} %pad_add_fusion.2.at_ref, bf16[10,320,512]{2,1,0:T(8,128)(2,1)S(1)} %copy-done, bf16[10,320,128]{2,1,0:T(8,128)(2,1)S(1)} %bitcast.26), custom_call_target="tpu_custom_call" | custom-call | flops 419430400 | bytes 6000000 | tf_op jit(solution)/shard_map/inverse_legendre/pallas_call | solution.py:108
  20.0 3.6 %collective-permute-start = (bf16[256,1280]{1,0:T(8,128)(2,1)S(1)}, bf16[256,1280]{1,0:T(8,128)(2,1)S(1)}, u32[]{:S(2)}, u32[]{:S(2)}) collective-permute-start(bf16[256,1280]{1,0:T(8,128)(2,1)S(1)} %get-tuple-element.20), channel_id=1, source_target_pairs={{0,128},{128,0},{1,129},{129,1},{2,130},{130,2},{3,131},{131,3},{4... | collective-permute-start | bytes 1966088 | tf_op jit(solution)/shard_map/ppermute | solution.py:374
  23.6 1.7 %collective-permute-done = bf16[256,1280]{1,0:T(8,128)(2,1)S(1)} collective-permute-done((bf16[256,1280]{1,0:T(8,128)(2,1)S(1)}, bf16[256,1280]{1,0:T(8,128)(2,1)S(1)}, u32[]{:S(2)}, u32[]{:S(2)}) %collective-permute-start) | collective-permute-done | bytes 655392 | tf_op jit(solution)/shard_map/ppermute | solution.py:374
  26.3 6.3 %collective-permute-start.1 = (bf16[128,1280]{1,0:T(8,128)(2,1)}, bf16[128,1280]{1,0:T(8,128)(2,1)}, u32[]{:S(2)}, u32[]{:S(2)}) collective-permute-start(bf16[128,1280]{1,0:T(8,128)(2,1)} %add_convert_fusion.1), channel_id=1, source_target_pairs={{0,256},{256,0},{1,257},{257,1},{2,258},{258,2},{3,259},{259,3},{4... | collective-permute-start | bytes 983048 | tf_op jit(solution)/shard_map/ppermute | solution.py:416
  32.9 9.6 %collective-permute-done.1 = bf16[128,1280]{1,0:T(8,128)(2,1)} collective-permute-done((bf16[128,1280]{1,0:T(8,128)(2,1)}, bf16[128,1280]{1,0:T(8,128)(2,1)}, u32[]{:S(2)}, u32[]{:S(2)}) %collective-permute-start.1) | collective-permute-done | bytes 327712 | tf_op jit(solution)/shard_map/ppermute | solution.py:416
  44.7 8.5 %all-to-all-done.rest_0_ = bf16[32,176,128]{2,1,0:T(8,128)(2,1)} async-done(((bf16[32,176,128]{2,1,0:T(8,128)(2,1)}), bf16[32,176,128]{2,1,0:T(8,128)(2,1)}, u32[]{:S(2)}, u32[]{:S(2)}) %all-to-all-start) | async-done | bytes 1441824 | tf_op jit(solution)/shard_map/all_to_all | solution.py:386
  53.2 3.2 %collective-permute-start.3 = (bf16[32,176,128]{2,1,0:T(8,128)(2,1)}, bf16[32,176,128]{2,1,0:T(8,128)(2,1)}, u32[]{:S(2)}, u32[]{:S(2)}) collective-permute-start(bf16[32,176,128]{2,1,0:T(8,128)(2,1)} %all-to-all-done.rest_0_), channel_id=1, source_target_pairs={{0,32},{1,33},{2,34},{3,35},{4,36},{5,37},{6,38},{7,39},{8,40},{9,... | collective-permute-start | bytes 4325384 | tf_op jit(solution)/shard_map/ppermute | solution.py:364
  56.4 2.0 %copy.18 = bf16[128,2,640]{2,1,0:T(2,128)(2,1)} copy(bf16[128,2,640]{2,0,1:T(8,128)(2,1)} %pad_maximum_fusion) | data formatting | bytes 655360 | tf_op jit(solution)/shard_map/optimization_barrier | solution.py:424
  58.4 12.6 %all-to-all-start.1 = ((bf16[128,2,640]{2,1,0:T(2,128)(2,1)}), bf16[128,2,640]{2,1,0:T(2,128)(2,1)}, u32[]{:S(2)}, u32[]{:S(2)}) async-start(bf16[128,2,640]{2,1,0:T(2,128)(2,1)} %copy.18), calls=%async_computation.1 | async-start | bytes 655360 | tf_op jit(solution)/shard_map/all_to_all | solution.py:382
  71.0 3.1 %collective-permute-start.4 = (bf16[32,176,128]{2,1,0:T(8,128)(2,1)}, bf16[32,176,128]{2,1,0:T(8,128)(2,1)}, u32[]{:S(2)}, u32[]{:S(2)}) collective-permute-start(bf16[32,176,128]{2,1,0:T(8,128)(2,1)} %all-to-all-done.rest_0_), channel_id=1, source_target_pairs={{0,96},{1,97},{2,98},{3,99},{4,100},{5,101},{6,102},{7,103},{8,104... | collective-permute-start | bytes 4325384 | tf_op jit(solution)/shard_map/ppermute | solution.py:364
  74.7 2.0 %collective-permute-start.5 = (bf16[32,176,128]{2,1,0:T(8,128)(2,1)}, bf16[32,176,128]{2,1,0:T(8,128)(2,1)}, u32[]{:S(2)}, u32[]{:S(2)}) collective-permute-start(bf16[32,176,128]{2,1,0:T(8,128)(2,1)} %collective-permute-done.3.rest_1_), channel_id=1, source_target_pairs={{0,32},{1,33},{2,34},{3,35},{4,36},{5,37},{6,38},{7,39},{8,40},{9,... | collective-permute-start | bytes 4325384 | tf_op jit(solution)/shard_map/ppermute | solution.py:364
  76.7 5.0 %collective-permute-start.2 = (s32[2,88]{1,0:T(2,128)S(1)}, s32[2,88]{1,0:T(2,128)S(1)}, u32[]{:S(2)}, u32[]{:S(2)}) collective-permute-start(s32[2,88]{1,0:T(2,128)S(1)} %pad_add_fusion.list_ref), channel_id=1, source_target_pairs={{0,128},{128,0},{1,129},{129,1},{2,130},{130,2},{3,131},{131,3},{4... | collective-permute-start | bytes 2120 | tf_op jit(solution)/shard_map/ppermute | solution.py:374
  81.7 1.9 %all-to-all-done.1 = bf16[128,2,640]{2,1,0:T(2,128)(2,1)} async-done(((bf16[128,2,640]{2,1,0:T(2,128)(2,1)}), bf16[128,2,640]{2,1,0:T(2,128)(2,1)}, u32[]{:S(2)}, u32[]{:S(2)}) %all-to-all-start.1) | async-done | bytes 327712 | tf_op jit(solution)/shard_map/all_to_all | solution.py:382
  85.7 8.0 %synthesize.1.cols_ref = bf16[5632,128]{1,0:T(8,128)(2,1)} custom-call(bf16[128,1280]{1,0:T(8,128)(2,1)S(1)} %bitcast.29, s32[1,1280]{1,0:T(1,128)S(1)} %bitcast.32, f32[1008,128]{1,0:T(8,128)S(1)} %copy-done.3), custom_call_target="tpu_custom_call" | custom-call | flops 1000000000 | bytes 1000000 | tf_op jit(solution)/shard_map/synthesize/pallas_call | solution.py:166
  93.6 7.2 %collective-permute-start.6 = (bf16[5632,128]{1,0:T(8,128)(2,1)}, bf16[5632,128]{1,0:T(8,128)(2,1)}, u32[]{:S(2)}, u32[]{:S(2)}) collective-permute-start(bf16[5632,128]{1,0:T(8,128)(2,1)} %synthesize.1.cols_ref), channel_id=1, source_target_pairs={{0,128},{128,0},{1,129},{129,1},{2,130},{130,2},{3,131},{131,3},{4... | collective-permute-start | bytes 4325384 | tf_op jit(solution)/shard_map/ppermute | solution.py:374
  101.0 7.4 %first_network.1 = (f32[8,11264]{1,0:T(8,128)S(1)}, bf16[128,176,128]{2,1,0:T(8,128)(2,1)S(1)}) custom-call(s32[2]{0:T(128)S(1)} %pad_add_fusion.1.at_ref, s32[2,88]{1,0:T(2,128)S(1)} %pad_add_fusion.list_ref, bf16[5632,128]{1,0:T(8,128)(2,1)} %synthesize.1.cols_ref, bf16[32,176,128]{2,1,0:T(8,128)(2,1)} %all-to-all-done.rest_0_, ...), custom_call_target="tpu_custom_call" | custom-call | flops 2000000000 | bytes 13000000 | tf_op jit(solution)/shard_map/first_network/pallas_call | solution.py:222
  108.4 4.7 %second_network.1 = f32[8,11264]{1,0:T(8,128)S(1)} custom-call(s32[2]{0:T(128)S(1)} %pad_add_fusion.1.at_ref, s32[2,88]{1,0:T(2,128)S(1)} %collective-permute-done.2.list_ref, bf16[5632,128]{1,0:T(8,128)(2,1)} %collective-permute-done.6.cols_ref, bf16[128,176,128]{2,1,0:T(8,128)(2,1)S(1)} %get-tuple-element.28.w_ref), custom_call_target="tpu_custom_call" | custom-call | flops 2000000000 | bytes 8000000 | tf_op jit(solution)/shard_map/second_network/pallas_call | solution.py:242
  113.1 1.9 %collective-permute-start.7 = (f32[8,11264]{1,0:T(8,128)S(1)}, f32[8,11264]{1,0:T(8,128)S(1)}, u32[]{:S(2)}, u32[]{:S(2)}) collective-permute-start(f32[8,11264]{1,0:T(8,128)S(1)} %second_network.1), channel_id=1, source_target_pairs={{0,128},{128,0},{1,129},{129,1},{2,130},{130,2},{3,131},{131,3},{4... | collective-permute-start | bytes 1081352 | tf_op jit(solution)/shard_map/ppermute | solution.py:374
  116.7 2.2 %analyze.1 = (bf16[8,11264]{1,0:T(8,128)(2,1)}, bf16[256,256]{1,0:T(8,128)(2,1)S(1)}) custom-call(f32[1]{0:T(128)S(6)} %copy.27.gauss_ref, f32[8,11264]{1,0:T(8,128)S(1)} %get-tuple-element.26.own_ref, f32[8,11264]{1,0:T(8,128)S(1)} %collective-permute-done.7.got_ref, s32[10,128]{1,0:T(8,128)S(1)} %bitcast.31, f32[1008,128]{1,0:T(8,128)S(1)} %copy-done.4), custom_call_target="tpu_custom_call" | custom-call | flops 1000000000 | bytes 1500000 | tf_op jit(solution)/shard_map/analyze/pallas_call | solution.py:300
  119.1 27.3 %all_to_all.15 = bf16[256,2,128]{2,1,0:T(2,128)(2,1)S(1)} all-to-all(bf16[256,2,128]{2,1,0:T(2,128)(2,1)S(1)} %copy.19), channel_id=1, replica_groups=mesh['y_hi'=2,'core'=2,'x'=4,'y_lo'=4,'z'=8] {'y_hi','x','y_lo','z'}, dimensions={0} | all-to-all | bytes 262144 | tf_op jit(solution)/shard_map/all_to_all | solution.py:382
  146.3 3.6 %collective-permute-start.8 = (bf16[256,256]{1,0:T(8,128)(2,1)S(1)}, bf16[256,256]{1,0:T(8,128)(2,1)S(1)}, u32[]{:S(2)}, u32[]{:S(2)}) collective-permute-start(bf16[256,256]{1,0:T(8,128)(2,1)S(1)} %bitcast.27), channel_id=1, source_target_pairs={{0,128},{128,0},{1,129},{129,1},{2,130},{130,2},{3,131},{131,3},{4... | collective-permute-start | bytes 393224 | tf_op jit(solution)/shard_map/ppermute | solution.py:374
  151.0 2.2 %forward_legendre.1 = bf16[10,16,320]{2,1,0:T(8,128)(2,1)} custom-call(s32[10]{0:T(128)S(1)} %subtract_subtract_fusion.limit_ref, s32[1]{0:T(128)} %bitcast.core_ref, bf16[10,320,512]{2,1,0:T(8,128)(2,1)S(1)} %copy-done, bf16[256,256]{1,0:T(8,128)(2,1)S(1)} %bitcast.28, bf16[256,256]{1,0:T(8,128)(2,1)S(1)} %collective-permute-done.8.theirs_ref), custom_call_target="tpu_custom_call" | custom-call | flops 52428800 | bytes 4000000 | tf_op jit(solution)/shard_map/forward_legendre/pallas_call | solution.py:337
  (42 shorter events, 9.6 us)
Async XLA Ops:
  0.6 16.4 %copy-start = (bf16[10,320,512]{2,1,0:T(8,128)(2,1)S(1)}, bf16[10,320,512]{2,1,0:T(8,128)(2,1)}, u32[]{:S(2)}) copy-start(bf16[10,320,512]{2,1,0:T(8,128)(2,1)} %table_ref.1) | copy-start | bytes 9830404
  2.9 14.1 %copy-start.6 = (s32[1280]{0:T(1024)S(1)}, s32[1280]{0:T(1024)}, u32[]{:S(2)}) copy-start(s32[1280]{0:T(1024)} %param.12) | copy-start | bytes 15364
  2.9 50.3 %all-to-all-start = ((bf16[32,176,128]{2,1,0:T(8,128)(2,1)}), bf16[32,176,128]{2,1,0:T(8,128)(2,1)}, u32[]{:S(2)}, u32[]{:S(2)}) async-start(bf16[32,176,128]{2,1,0:T(8,128)(2,1)} %pack_weights.1), calls=%async_computation | async-start | bytes 2883584 | tf_op jit(solution)/shard_map/all_to_all | solution.py:386
  17.0 1.1 copy-start.2
  20.0 5.3 %copy-start.1 = (f32[256,1280]{1,0:T(8,128)}, f32[256,1280]{1,0:T(8,128)S(1)}, u32[]{:S(2)}) copy-start(f32[256,1280]{1,0:T(8,128)S(1)} %get-tuple-element.19) | copy-start | bytes 3932164
  20.0 12.8 %copy-start.7 = (s32[1,88]{1,0:T(1,128)S(1)}, s32[1,88]{1,0:T(1,128)}, u32[]{:S(2)}) copy-start(s32[1,88]{1,0:T(1,128)} %param.14) | copy-start | bytes 1060
  20.0 12.8 %copy-start.8 = (s32[1,88,1]{1,2,0:T(1,128)S(1)}, s32[1,88,1]{1,2,0:T(1,128)}, u32[]{:S(2)}) copy-start(s32[1,88,1]{1,2,0:T(1,128)} %param.13) | copy-start | bytes 1060
  20.0 5.3 %collective-permute-start = (bf16[256,1280]{1,0:T(8,128)(2,1)S(1)}, bf16[256,1280]{1,0:T(8,128)(2,1)S(1)}, u32[]{:S(2)}, u32[]{:S(2)}) collective-permute-start(bf16[256,1280]{1,0:T(8,128)(2,1)S(1)} %get-tuple-element.20), channel_id=1, source_target_pairs={{0,128},{128,0},{1,129},{129,1},{2,130},{130,2},{3,131},{131,3},{4... | collective-permute-start | bytes 1966088 | tf_op jit(solution)/shard_map/ppermute | solution.py:374
  25.3 1.0 copy-start.5
  26.3 16.2 %collective-permute-start.1 = (bf16[128,1280]{1,0:T(8,128)(2,1)}, bf16[128,1280]{1,0:T(8,128)(2,1)}, u32[]{:S(2)}, u32[]{:S(2)}) collective-permute-start(bf16[128,1280]{1,0:T(8,128)(2,1)} %add_convert_fusion.1), channel_id=1, source_target_pairs={{0,256},{256,0},{1,257},{257,1},{2,258},{258,2},{3,259},{259,3},{4... | collective-permute-start | bytes 983048 | tf_op jit(solution)/shard_map/ppermute | solution.py:416
  53.2 21.6 %collective-permute-start.3 = (bf16[32,176,128]{2,1,0:T(8,128)(2,1)}, bf16[32,176,128]{2,1,0:T(8,128)(2,1)}, u32[]{:S(2)}, u32[]{:S(2)}) collective-permute-start(bf16[32,176,128]{2,1,0:T(8,128)(2,1)} %all-to-all-done.rest_0_), channel_id=1, source_target_pairs={{0,32},{1,33},{2,34},{3,35},{4,36},{5,37},{6,38},{7,39},{8,40},{9,... | collective-permute-start | bytes 4325384 | tf_op jit(solution)/shard_map/ppermute | solution.py:364
  58.4 25.2 %all-to-all-start.1 = ((bf16[128,2,640]{2,1,0:T(2,128)(2,1)}), bf16[128,2,640]{2,1,0:T(2,128)(2,1)}, u32[]{:S(2)}, u32[]{:S(2)}) async-start(bf16[128,2,640]{2,1,0:T(2,128)(2,1)} %copy.18), calls=%async_computation.1 | async-start | bytes 655360 | tf_op jit(solution)/shard_map/all_to_all | solution.py:382
  71.0 30.0 %collective-permute-start.4 = (bf16[32,176,128]{2,1,0:T(8,128)(2,1)}, bf16[32,176,128]{2,1,0:T(8,128)(2,1)}, u32[]{:S(2)}, u32[]{:S(2)}) collective-permute-start(bf16[32,176,128]{2,1,0:T(8,128)(2,1)} %all-to-all-done.rest_0_), channel_id=1, source_target_pairs={{0,96},{1,97},{2,98},{3,99},{4,100},{5,101},{6,102},{7,103},{8,104... | collective-permute-start | bytes 4325384 | tf_op jit(solution)/shard_map/ppermute | solution.py:364
  74.7 26.2 %collective-permute-start.5 = (bf16[32,176,128]{2,1,0:T(8,128)(2,1)}, bf16[32,176,128]{2,1,0:T(8,128)(2,1)}, u32[]{:S(2)}, u32[]{:S(2)}) collective-permute-start(bf16[32,176,128]{2,1,0:T(8,128)(2,1)} %collective-permute-done.3.rest_1_), channel_id=1, source_target_pairs={{0,32},{1,33},{2,34},{3,35},{4,36},{5,37},{6,38},{7,39},{8,40},{9,... | collective-permute-start | bytes 4325384 | tf_op jit(solution)/shard_map/ppermute | solution.py:364
  76.7 7.9 %collective-permute-start.2 = (s32[2,88]{1,0:T(2,128)S(1)}, s32[2,88]{1,0:T(2,128)S(1)}, u32[]{:S(2)}, u32[]{:S(2)}) collective-permute-start(s32[2,88]{1,0:T(2,128)S(1)} %pad_add_fusion.list_ref), channel_id=1, source_target_pairs={{0,128},{128,0},{1,129},{129,1},{2,130},{130,2},{3,131},{131,3},{4... | collective-permute-start | bytes 2120 | tf_op jit(solution)/shard_map/ppermute | solution.py:374
  84.6 1.0 copy-start.3
  93.6 14.7 %collective-permute-start.6 = (bf16[5632,128]{1,0:T(8,128)(2,1)}, bf16[5632,128]{1,0:T(8,128)(2,1)}, u32[]{:S(2)}, u32[]{:S(2)}) collective-permute-start(bf16[5632,128]{1,0:T(8,128)(2,1)} %synthesize.1.cols_ref), channel_id=1, source_target_pairs={{0,128},{128,0},{1,129},{129,1},{2,130},{130,2},{3,131},{131,3},{4... | collective-permute-start | bytes 4325384 | tf_op jit(solution)/shard_map/ppermute | solution.py:374
  108.4 8.3 %copy-start.4 = (f32[1008,128]{1,0:T(8,128)S(1)}, f32[1008,128]{1,0:T(8,128)}, u32[]{:S(2)}) copy-start(f32[1008,128]{1,0:T(8,128)} %constant.59.clone.tab_ref) | copy-start | bytes 1548292
  113.1 3.6 %collective-permute-start.7 = (f32[8,11264]{1,0:T(8,128)S(1)}, f32[8,11264]{1,0:T(8,128)S(1)}, u32[]{:S(2)}, u32[]{:S(2)}) collective-permute-start(f32[8,11264]{1,0:T(8,128)S(1)} %second_network.1), channel_id=1, source_target_pairs={{0,128},{128,0},{1,129},{129,1},{2,130},{130,2},{3,131},{131,3},{4... | collective-permute-start | bytes 1081352 | tf_op jit(solution)/shard_map/ppermute | solution.py:374
  146.3 4.6 %collective-permute-start.8 = (bf16[256,256]{1,0:T(8,128)(2,1)S(1)}, bf16[256,256]{1,0:T(8,128)(2,1)S(1)}, u32[]{:S(2)}, u32[]{:S(2)}) collective-permute-start(bf16[256,256]{1,0:T(8,128)(2,1)S(1)} %bitcast.27), channel_id=1, source_target_pairs={{0,128},{128,0},{1,129},{129,1},{2,130},{130,2},{3,131},{131,3},{4... | collective-permute-start | bytes 393224 | tf_op jit(solution)/shard_map/ppermute | solution.py:374
